TPU v7x, 256 devices: a whole 4x4x8 slice. The times are simulated.
256 devices in a mesh: dp: 4 (over x), vocab: 64 (over z, y, core).
Axes of the slice: x: 4, y: 4, z: 8, core: 2. Of those that a mesh axis runs over, the one named last changes fastest.
Arguments:
- hidden: bfloat16 [1024, 5120], P(('dp', 'vocab')), may hold values from -8 to 8
- teacher: bfloat16 [1024, 75968], P(('dp', 'vocab')), may hold values from -14 to 230
- head_weight: bfloat16 [5120, 75968], P('dp', 'vocab'), as said below
- loss_weight: float32 [1024], P(('dp', 'vocab')), may hold values from 1 to 10
Outputs:
- grad_hidden: bfloat16 [1024, 5120], P(('dp', 'vocab'))
- grad_head: bfloat16 [5120, 75968], P('dp', 'vocab')
Inputs may be any that keep to these rules, and one draw needn't show every extreme that they name: `head_weight`: entries lie within plus or minus 12 / sqrt(5120).
All inputs are finite; a program needn't handle non-finite values.
Results may differ from a plain program's by a relative error of at most 0.024.
Values may be sent and summed in bfloat16 or wider, within the bound.
No kernel may reach another device: no remote copies, remote signals or barrier semaphores. Data moves between devices by JAX's collectives and lax.ppermute only.
A program may use at most 128 MiB of HBM per device.

v0:
```python
import jax
import jax.numpy as jnp
from jax import lax
from jax.sharding import PartitionSpec as P

alpha_power = 0.5
beta_power = 0.25
joint_power = 0.75


def merged(value, axis, join):
    pieces = jax.tree.map(lambda part: lax.all_gather(part, axis), value)
    head = jax.tree.map(lambda part: part[0], pieces)
    tail = jax.tree.map(lambda part: part[1:], pieces)
    so_far, _ = lax.scan(lambda so_far, piece: (join(so_far, piece), None), head, tail)
    return so_far


def merge_four(first, second):
    top_student = jnp.maximum(first[0], second[0])
    top_teacher = jnp.maximum(first[2], second[2])
    student_sum = first[1] * jnp.exp(first[0] - top_student) + second[1] * jnp.exp(
        second[0] - top_student
    )
    teacher_sum = first[3] * jnp.exp(first[2] - top_teacher) + second[3] * jnp.exp(
        second[2] - top_teacher
    )
    return (top_student, student_sum, top_teacher, teacher_sum)


def body(hidden, teacher, head_weight, loss_weight):
    rows_all, weight_all = (
        lax.all_gather(hidden, "vocab", axis=0, tiled=True),
        lax.all_gather(loss_weight.astype(jnp.bfloat16), "vocab", axis=0, tiled=True).astype(
            loss_weight.dtype
        ),
    )
    teacher_slice = lax.all_to_all(teacher, "vocab", split_axis=1, concat_axis=0, tiled=True)
    whole_weight = lax.all_gather(head_weight, "dp", axis=0, tiled=True)
    logits = jnp.dot(rows_all, whole_weight, preferred_element_type=jnp.float32)
    teacher_float = teacher_slice.astype(jnp.float32)
    local_student = jnp.max(logits, axis=1)
    local_teacher = jnp.max(teacher_float, axis=1)
    shifted_student = logits - local_student[:, None]
    shifted_teacher = teacher_float - local_teacher[:, None]
    student_sum = jnp.sum(jnp.exp(shifted_student), axis=1)
    teacher_sum = jnp.sum(jnp.exp(shifted_teacher), axis=1)
    top_student, total_student, top_teacher, total_teacher = merged(
        (local_student, student_sum, local_teacher, teacher_sum), "vocab", merge_four
    )
    log_student = logits - (top_student + jnp.log(total_student))[:, None]
    log_teacher = teacher_float - (top_teacher + jnp.log(total_teacher))[:, None]
    mixed_part = jnp.exp(alpha_power * log_teacher + beta_power * log_student)
    joint_part = jnp.exp(joint_power * log_student)
    mixed_sum, joint_sum = lax.psum(
        (jnp.sum(mixed_part, axis=1), jnp.sum(joint_part, axis=1)), "vocab"
    )
    remainder = mixed_sum - joint_sum
    grad_logits = (
        -(weight_all / alpha_power)[:, None]
        * (mixed_part - joint_part - jnp.exp(log_student) * remainder[:, None])
    ).astype(jnp.bfloat16)
    contract_vocab = (((1,), (1,)), ((), ()))
    hidden_partial = lax.dot_general(
        grad_logits, whole_weight, contract_vocab, preferred_element_type=jnp.float32
    )
    grad_hidden = lax.psum_scatter(hidden_partial, "vocab", scatter_dimension=0, tiled=True).astype(
        jnp.bfloat16
    )
    contract_tokens = (((0,), (0,)), ((), ()))
    grad_head = lax.psum_scatter(
        lax.dot_general(
            rows_all, grad_logits, contract_tokens, preferred_element_type=jnp.float32
        ).astype(jnp.bfloat16),
        "dp",
        scatter_dimension=0,
        tiled=True,
    )
    return (grad_hidden, grad_head)


def solution(mesh):
    placed = (
        P(("dp", "vocab"), None),
        P(("dp", "vocab"), None),
        P("dp", "vocab"),
        P(("dp", "vocab")),
    )
    return jax.shard_map(
        body,
        mesh=mesh,
        in_specs=placed,
        out_specs=(P(("dp", "vocab"), None), P("dp", "vocab")),
        check_vma=False,
    )
```

profile of v0, /device:TPU:6, one launch (start us, length us, event | category | flops | bytes accessed | tf_op | source)
XLA Modules:
  0.0 795.6 jit_solution(5769309685772871507)
XLA Ops:
  7.2 0.0 all-gather.12.cloned.1.call-start
  7.2 0.7 all-gather.12.cloned.1.call-update
  7.9 0.0 copy-start.1
  7.9 0.0 all-gather.10.cloned.1.call-start
  8.0 0.7 all-gather.10.cloned.1.call-update
  8.7 0.3 copy-done.1
  9.0 1.0 all_to_all.12
  10.0 0.0 copy-start.5
  10.0 0.0 copy-start.4
  10.0 1.3 copy.9
  11.4 12.1 %all-to-all-start = ((bf16[4,64,1187]{2,0,1:T(4,128)(2,1)}), bf16[4,64,1187]{2,0,1:T(4,128)(2,1)S(1)}, u32[]{:S(2)}, u32[]{:S(2)}) async-start(bf16[4,64,1187]{2,0,1:T(4,128)(2,1)} %copy.9), calls=%async_computation | async-start | bytes 1310720 | tf_op jit(solution)/shard_map/all_to_all | solution.py:38
  23.5 0.0 reduce-scatter.2.cloned.1.call-start
  23.5 0.0 copy-done.5
  23.6 0.0 copy-done.4
  23.6 0.6 fusion.3
  24.8 0.2 dynamic-update-slice
  25.0 133.6 %all-reduce = bf16[256]{0:T(256)(128)(2,1)S(1)} all-reduce(bf16[256]{0:T(256)(128)(2,1)S(1)} %dynamic-update-slice), channel_id=1, replica_groups=mesh['dp'=4,'vocab'=64] {'vocab'}, use_global_device_ids=true, to_apply=%add | all-reduce | flops 256 | bytes 1024
  158.7 0.0 all-to-all-done
  158.7 0.3 bitcast_reduce_fusion
  159.0 0.1 reshape.60
  159.1 0.7 exponential_reduce_fusion
  159.8 0.1 reshape.62
  159.9 43.5 %all-gather.6 = f32[64,1,256]{2,1,0:T(1,128)S(1)} all-gather(f32[1,1,256]{2,1,0:T(1,128)S(1)} %reshape.62), channel_id=1, replica_groups=mesh['dp'=4,'vocab'=64] {'vocab'}, dimensions={0}, use_global_device_ids=true | all-gather | bytes 66560 | tf_op jit(solution)/shard_map/all_gather | solution.py:12
  203.4 43.8 %all-gather.5 = f32[64,1,256]{2,1,0:T(1,128)S(1)} all-gather(f32[1,1,256]{2,1,0:T(1,128)S(1)} %reshape.60), channel_id=1, replica_groups=mesh['dp'=4,'vocab'=64] {'vocab'}, dimensions={0}, use_global_device_ids=true | all-gather | bytes 66560 | tf_op jit(solution)/shard_map/all_gather | solution.py:12
  247.2 0.1 bitcast_convert_fusion
  247.3 0.5 reshape.41
  247.7 0.0 copy-done.3
  247.8 0.4 copy.10
  248.2 0.0 all-gather.12.cloned.1.call-done
  248.2 5.2 reshape.55
  253.4 7.3 fusion.4
  260.7 0.0 slice-start
  260.7 0.0 slice-start.1
  260.7 0.3 exponential_reduce_fusion.1
  261.0 40.8 %all-gather.4 = f32[64,1,256]{2,1,0:T(1,128)S(1)} all-gather(f32[1,1,256]{2,1,0:T(1,128)S(1)} %bitcast.60), channel_id=3, replica_groups=mesh['dp'=4,'vocab'=64] {'vocab'}, dimensions={0}, use_global_device_ids=true | all-gather | bytes 66560 | tf_op jit(solution)/shard_map/all_gather | solution.py:12
  301.8 43.4 %all-gather.3 = f32[64,1,256]{2,1,0:T(1,128)S(1)} all-gather(f32[1,1,256]{2,1,0:T(1,128)S(1)} %bitcast.59), channel_id=2, replica_groups=mesh['dp'=4,'vocab'=64] {'vocab'}, dimensions={0}, use_global_device_ids=true | all-gather | bytes 66560 | tf_op jit(solution)/shard_map/all_gather | solution.py:12
  345.2 0.0 slice-done
  345.2 0.0 slice-done.1
  345.2 5.9 while.16
  351.1 0.5 fusion.1
  351.6 126.8 %all-reduce.2 = (f32[256]{0:T(256)S(1)}, f32[256]{0:T(256)S(1)}) all-reduce(f32[256]{0:T(256)S(1)} %get-tuple-element.57, f32[256]{0:T(256)S(1)} %get-tuple-element.56), channel_id=1, replica_groups=mesh['dp'=4,'vocab'=64] {'vocab'}, use_global_device_ids=true, to_apply=%region_7.8 | all-reduce | flops 512 | bytes 4096 | tf_op jit(solution)/shard_map/psum | solution.py:55
  478.5 0.7 multiply_convert_fusion
  479.2 1.0 copy-done
  480.2 6.2 fusion
  486.4 0.0 reduce-scatter.2.cloned.1.call-update
  487.1 10.4 %fusion.5 = f32[256,5120]{1,0:T(8,128)} fusion(bf16[256,1187]{0,1:T(8,128)(2,1)S(1)} %multiply_convert_fusion, bf16[5120,1187]{0,1:T(8,128)(2,1)} %all-gather.10.cloned.1.call-done), kind=kOutput, calls=%fused_computation.27 | convolution fusion | flops 3111649280 | bytes 18005504 | tf_op jit(solution)/shard_map/dot_general | solution.py:64
  497.5 290.9 %all-reduce.4 = bf16[256,5120]{1,0:T(8,128)(2,1)S(1)} all-reduce(f32[256,5120]{1,0:T(8,128)} %fusion.5), channel_id=4, replica_groups=mesh['dp'=4,'vocab'=64] {'vocab'}, use_global_device_ids=true, to_apply=%region_10.11.clone | all-reduce | flops 1310720 | bytes 7864320
  788.4 0.6 dynamic-slice_convert_fusion
  (274 shorter events, 4.1 us)
Async XLA Ops:
  7.2 241.0 %all-gather.12.cloned.1.call-start = ((), (), s32[]{:S(2)}) async-start(), calls=%async_computation.4 | async-start | bytes 2662400 | tf_op jit(solution)/shard_map/all_gather | solution.py:33
  7.9 1.1 copy-start.1
  7.9 245.5 %all-gather.10.cloned.1.call-start = ((), (), s32[]{:S(2)}) async-start(), calls=%async_computation.2 | async-start | bytes 15257600 | tf_op jit(solution)/shard_map/all_gather | solution.py:39
  10.0 13.5 %copy-start.5 = (f32[4]{0:T(128)S(1)}, f32[4]{0:T(128)}, u32[]{:S(2)}) copy-start(f32[4]{0:T(128)} %param.9) | copy-start | bytes 52
  10.0 13.6 %copy-start.4 = (u32[256]{0:T(256)S(1)}, u32[256]{0:T(256)}, u32[]{:S(2)}) copy-start(u32[256]{0:T(256)} %constant.33) | copy-start | bytes 3076
  11.4 147.3 %all-to-all-start = ((bf16[4,64,1187]{2,0,1:T(4,128)(2,1)}), bf16[4,64,1187]{2,0,1:T(4,128)(2,1)S(1)}, u32[]{:S(2)}, u32[]{:S(2)}) async-start(bf16[4,64,1187]{2,0,1:T(4,128)(2,1)} %copy.9), calls=%async_computation | async-start | bytes 1310720 | tf_op jit(solution)/shard_map/all_to_all | solution.py:38
  23.5 765.6 %reduce-scatter.2.cloned.1.call-start = ((), (), s32[]{:S(2)}) async-start(), calls=%async_computation.3 | async-start | bytes 15257600 | tf_op jit(solution)/shard_map/reduce_scatter | solution.py:71
  203.4 43.9 %copy-start.2 = (f32[64,1,256]{2,1,0:T(1,128)}, f32[64,1,256]{2,1,0:T(1,128)S(1)}, u32[]{:S(2)}) copy-start(f32[64,1,256]{2,1,0:T(1,128)S(1)} %all-gather.6) | copy-start | bytes 196612
  247.1 0.6 copy-start.3
  260.7 84.5 %slice-start = ((f32[64,1,256]{2,1,0:T(1,128)}), f32[1,1,256]{2,1,0:T(1,128)S(1)}, s32[]{:S(2)}) async-start(f32[64,1,256]{2,1,0:T(1,128)} %copy-done.2), calls=%async_computation.5 | async-start | bytes 2048 | tf_op jit(solution)/shard_map/slice | solution.py:13
  260.7 84.5 %slice-start.1 = ((f32[64,1,256]{2,1,0:T(1,128)}), f32[1,1,256]{2,1,0:T(1,128)S(1)}, s32[]{:S(2)}) async-start(f32[64,1,256]{2,1,0:T(1,128)} %copy-done.3), calls=%async_computation.6 | async-start | bytes 2048 | tf_op jit(solution)/shard_map/slice | solution.py:13
  478.5 1.7 copy-start
Sparse Core Ops, SparseCore 0:
  10.7 80.7 all-gather.11
  93.3 114.3 all-gather.9
  486.6 110.8 reduce-scatter.1
where the time goes:
time: 796 us
  blocking collectives  723 us (91%)
  matrix products  23.9 us (3%)
  between operations  15.2 us (2%)
  local copies, waits for them, and re-layouts  13 us (2%)
  starting transfers between devices  12.2 us (2%)
    unnamed x2, blocking collectives  425 us
    all_gather x4, blocking collectives, merged(): pieces = jax.tree.map(lambda part: lax.all_gather(part, axis), value)  171 us
    psum x1, blocking collectives, body(): lax.psum((jnp.sum(mixed_part, axis=1), jnp.sum(joint_part, axis=1)), 'voc...  127 us
  transfers between devices with their start and end apart: 4, of which 0 were waited for; matrix products, arithmetic and copies ran while one was open for 3% of the time, Pallas kernels for 0%

commit v1 on v0

v1 whole, which is shorter than its diff:
```python
import jax
import jax.numpy as jnp
from jax import lax
from jax.sharding import Mesh, PartitionSpec as P

alpha_power = 0.5
beta_power = 0.25
joint_power = 0.75
smallest = 1e-37

NX, NZ, NY, NC = 4, 8, 4, 2
VOCAB = ("z", "y", "c")
OWN = 4
COLS = 1280
SLICE = 1187
SPAN = 256


def shift(count, by):
    return [(i, (i + by) % count) for i in range(count)]


def take(value, index, axis):
    return lax.dynamic_index_in_dim(value, index, axis, keepdims=False)


def rolled(value, by):
    count = value.shape[0]
    return lax.dynamic_slice_in_dim(jnp.concatenate([value, value], axis=0), by, count, axis=0)


def gather_hidden(hidden, x, y, c):
    pieces = hidden.reshape(OWN, NX, COLS).transpose(1, 0, 2)
    spread = jnp.broadcast_to(pieces[:, None], (NX, NZ, OWN, COLS)).reshape(NX * NZ, OWN, COLS)
    got = lax.all_to_all(spread, ("x", "z"), 0, 0, tiled=True)
    mine = rolled(got.reshape(NX, NZ * OWN, COLS), x)
    half = jnp.zeros((NX, NY, NZ * OWN, COLS), mine.dtype)
    half = lax.dynamic_update_slice(half, mine[:, None], (0, y, 0, 0))
    for by in range(1, NY):
        part = lax.ppermute(mine, "y", shift(NY, by))
        half = lax.dynamic_update_slice(half, part[:, None], (0, (y - by) % NY, 0, 0))
    other = lax.ppermute(half, "c", shift(NC, 1))
    whole = jnp.zeros((NX, NC) + half.shape[1:], half.dtype)
    whole = lax.dynamic_update_slice(whole, half[:, None], (0, c, 0, 0, 0))
    whole = lax.dynamic_update_slice(whole, other[:, None], (0, 1 - c, 0, 0, 0))
    return whole.reshape(NX, SPAN, COLS)


def split_three(value):
    high = value.astype(jnp.bfloat16)
    rest = value - high.astype(jnp.float32)
    middle = rest.astype(jnp.bfloat16)
    low = (rest - middle.astype(jnp.float32)).astype(jnp.bfloat16)
    return jnp.stack([high, middle, low], axis=-1)


def gather_teacher(teacher, loss_weight):
    parts = teacher.reshape(OWN, NZ * NY * NC, SLICE)
    weights = jnp.broadcast_to(split_three(loss_weight)[:, None], (OWN, NZ * NY * NC, 3))
    rows = jnp.concatenate([parts, weights], axis=2).transpose(1, 0, 2)
    got = lax.all_to_all(rows, VOCAB, 0, 0, tiled=True)
    got = got.reshape(NZ, NY, NC, OWN, SLICE + 3).transpose(4, 2, 1, 0, 3).reshape(SLICE + 3, SPAN)
    got = got.astype(jnp.float32)
    return got[:SLICE], got[SLICE] + got[SLICE + 1] + got[SLICE + 2]


def row_stats(student, teacher):
    top_s = jnp.max(student, axis=0)
    top_t = jnp.max(teacher, axis=0)
    s = student - top_s
    t = teacher - top_t

    def log_sum(value):
        return jnp.log(jnp.maximum(jnp.sum(jnp.exp(value), axis=0), smallest))

    return jnp.stack(
        [
            top_s + log_sum(s),
            top_t + log_sum(t),
            alpha_power * top_t + beta_power * top_s + log_sum(alpha_power * t + beta_power * s),
            joint_power * top_s + log_sum(joint_power * s),
        ]
    )


def body(hidden, teacher, head_weight, loss_weight):
    x, y, c = lax.axis_index("x"), lax.axis_index("y"), lax.axis_index("c")
    head = head_weight.T
    rows = gather_hidden(hidden, x, y, c)
    teacher_slice, weight = gather_teacher(teacher, loss_weight)

    def partial_logits(which):
        return lax.dot_general(
            head, rows[which], (((1,), (1,)), ((), ())), preferred_element_type=jnp.float32
        )

    sent = [
        lax.ppermute(partial_logits(r).astype(jnp.float16), "x", shift(NX, r)) for r in (2, 1, 3)
    ]
    logits = partial_logits(0)
    for part in sent:
        logits = logits + part.astype(jnp.float32)

    own = row_stats(logits, teacher_slice).reshape(8, 128)
    every = lax.all_to_all(
        jnp.broadcast_to(own[None], (NZ * NY * NC, 8, 128)), VOCAB, 0, 0, tiled=True
    ).reshape(NZ * NY * NC, 4, SPAN)
    top = jnp.max(every, axis=0)
    log_s, log_t, log_m, log_j = top + jnp.log(jnp.sum(jnp.exp(every - top), axis=0))
    remainder = jnp.exp(log_m - alpha_power * log_t - beta_power * log_s) - jnp.exp(
        log_j - joint_power * log_s
    )
    log_student = logits - log_s
    log_teacher = teacher_slice - log_t
    grad_logits = (
        -(weight / alpha_power)
        * (
            jnp.exp(alpha_power * log_teacher + beta_power * log_student)
            - jnp.exp(joint_power * log_student)
            - jnp.exp(log_student) * remainder
        )
    ).astype(jnp.bfloat16)

    groups = [grad_logits] + [
        lax.ppermute(grad_logits, "x", shift(NX, -r)) for r in range(1, NX)
    ]
    grads = jnp.concatenate(groups, axis=1)
    hidden_partial = lax.dot_general(
        grads, head, (((0,), (0,)), ((), ())), preferred_element_type=jnp.float32
    ).reshape(NX, NC, NY, NZ * OWN, COLS)
    away = lax.ppermute(take(hidden_partial, 1 - c, 1).astype(jnp.bfloat16), "c", shift(NC, 1))
    kept = take(hidden_partial, c, 1) + away.astype(jnp.float32)
    mine = take(kept, y, 1)
    for by in range(1, NY):
        part = take(kept, (y + by) % NY, 1).astype(jnp.bfloat16)
        mine = mine + lax.ppermute(part, "y", shift(NY, by)).astype(jnp.float32)
    mine = rolled(mine.astype(jnp.bfloat16), (NX - x) % NX)
    got = lax.all_to_all(mine.reshape(NX * NZ, OWN, COLS), ("x", "z"), 0, 0, tiled=True)
    total = jnp.sum(got.reshape(NX, NZ, OWN, COLS).astype(jnp.float32), axis=1)
    grad_hidden = total.transpose(1, 0, 2).reshape(OWN, NX * COLS).astype(jnp.bfloat16)
    grad_head = lax.dot_general(
        grads,
        rows.reshape(NX * SPAN, COLS),
        (((1,), (0,)), ((), ())),
        preferred_element_type=jnp.float32,
    ).astype(jnp.bfloat16)
    return grad_hidden, grad_head.T


def solution(mesh):
    fine = Mesh(mesh.devices.reshape(NX, NZ, NY, NC), ("x", "z", "y", "c"))
    every = ("x", "z", "y", "c")
    placed = (P(every, None), P(every, None), P("x", VOCAB), P(every))
    return jax.shard_map(
        body,
        mesh=fine,
        in_specs=placed,
        out_specs=(P(every, None), P("x", VOCAB)),
        check_vma=False,
    )
```

time: 796 us -> 258 us (0.32)
  blocking collectives: 723 us -> 0 us
  waiting for transfers between devices: 1.42 us -> 96.6 us
  local copies, waits for them, and re-layouts: 13 us -> 65.5 us
  starting transfers between devices: 12.2 us -> 49.8 us
  other arithmetic: 5.18 us -> 21.9 us
  between operations: 15.2 us -> 0.94 us
    unnamed x2 -> x0, blocking collectives: 425 us -> none
    all_gather x4 -> x0, blocking collectives: 171 us -> none  [merged(): pieces = jax.tree.map(lambda part: lax.all_gather(part, axis), value)]
    psum x1 -> x0, blocking collectives: 127 us -> none  [body(): lax.psum((jnp.sum(mixed_part, axis=1), jnp.sum(joint_part, axis=1)), 'voc...]
    ppermute x0 -> x14, waiting for transfers between devices: none -> 53.3 us  [the longest x3 28.1 us: body(): lax.ppermute(grad_logits, 'x', shift(NX, -r))]
    all_to_all x1 -> x4, waiting for transfers between devices: 0.01 us -> 43.3 us  [the longest x1 16.1 us: gather_teacher(): got = lax.all_to_all(rows, VOCAB, 0, 0, tiled=True)]
    slice x10 -> x4, local copies, waits for them, and re-layouts: 0.04 us -> 23.6 us  [the longest x3 20.7 us: gather_teacher(): return (got[:SLICE], got[SLICE] + got[SLICE + 1] + got[SLICE + 2])]
    all_to_all x1 -> x4, starting transfers between devices: 12.1 us -> 32.6 us  [the longest x1 11.6 us: gather_hidden(): got = lax.all_to_all(spread, ('x', 'z'), 0, 0, tiled=True)]
    ppermute x0 -> x14, starting transfers between devices: none -> 17.2 us  [the longest x3 5.83 us: gather_hidden(): part = lax.ppermute(mine, 'y', shift(NY, by))]
  transfers between devices with their start and end apart: 4 -> 18, of which waited for: 0 -> 11; matrix products, arithmetic and copies ran while one was open for 3% -> 27% of each run, Pallas kernels for 0% -> 0%
where the time goes in v1:
time: 258 us; the launch traced here: 254 us
  waiting for transfers between devices  96.6 us (37%)
  local copies, waits for them, and re-layouts  65.5 us (25%)
  starting transfers between devices  49.8 us (19%)
  other arithmetic  21.9 us (8%)
  matrix products  19.5 us (8%)
    ppermute x3, waiting for transfers between devices, body(): lax.ppermute(grad_logits, 'x', shift(NX, -r))  28.1 us
    slice x3, local copies, waits for them, and re-layouts, gather_teacher(): return (got[:SLICE], got[SLICE] + got[SLICE + 1] + got[SLICE + 2])  20.7 us
    all_to_all x1, waiting for transfers between devices, gather_teacher(): got = lax.all_to_all(rows, VOCAB, 0, 0, tiled=True)  16.1 us
    ppermute x3, waiting for transfers between devices, body(): mine = mine + lax.ppermute(part, 'y', shift(NY, by)).astype(jnp.float32)  14.6 us
    convert_element_type x1, local copies, waits for them, and re-layouts, gather_teacher(): got = got.astype(jnp.float32)  14.2 us
    all_to_all x1, waiting for transfers between devices, body(): lax.all_to_all(jnp.broadcast_to(own[None], (NZ * NY * NC, 8, 128)), VOCAB...  12 us
    all_to_all x1, waiting for transfers between devices, gather_hidden(): got = lax.all_to_all(spread, ('x', 'z'), 0, 0, tiled=True)  11.6 us
    all_to_all x1, starting transfers between devices, gather_hidden(): got = lax.all_to_all(spread, ('x', 'z'), 0, 0, tiled=True)  11.6 us
  transfers between devices with their start and end apart: 18, of which 11 were waited for; matrix products, arithmetic and copies ran while one was open for 27% of the time, Pallas kernels for 0%

profile of v1, /device:TPU:6, one launch (start us, length us, event | category | flops | bytes accessed | tf_op | source)
XLA Modules:
  0.0 254.2 jit_solution(13274785907632147357)
XLA Ops:
  2.4 11.6 %all-to-all-start.1 = ((bf16[32,4,1280]{2,1,0:T(4,128)(2,1)}), bf16[32,4,1280]{2,1,0:T(4,128)(2,1)S(1)}, u32[]{:S(2)}, u32[]{:S(2)}) async-start(bf16[32,4,1280]{2,1,0:T(4,128)(2,1)} %bitcast.115), calls=%async_computation.1 | async-start | bytes 655360 | tf_op jit(solution)/shard_map/all_to_all | solution.py:35
  14.1 11.6 %all-to-all-done.1 = bf16[32,4,1280]{2,1,0:T(4,128)(2,1)S(1)} async-done(((bf16[32,4,1280]{2,1,0:T(4,128)(2,1)}), bf16[32,4,1280]{2,1,0:T(4,128)(2,1)S(1)}, u32[]{:S(2)}, u32[]{:S(2)}) %all-to-all-start.1) | async-done | bytes 327712 | tf_op jit(solution)/shard_map/all_to_all | solution.py:35
  28.6 1.6 collective-permute-start
  30.3 3.0 %reshape.185 = bf16[4,64,1187]{2,1,0:T(8,128)(2,1)} reshape(bf16[4,75968]{1,0:T(4,128)(2,1)} %param.5) | data formatting | bytes 1215488 | tf_op jit(solution)/shard_map/reshape | solution.py:58
  33.3 2.4 copy.54
  35.7 2.9 %collective-permute-start.1 = (bf16[4,32,1280]{2,1,0:T(8,128)(2,1)S(1)}, bf16[4,32,1280]{2,1,0:T(8,128)(2,1)S(1)}, u32[]{:S(2)}, u32[]{:S(2)}) collective-permute-start(bf16[4,32,1280]{2,1,0:T(8,128)(2,1)S(1)} %get-tuple-element.7), channel_id=1, source_target_pairs={{0,4},{2,6},{4,0},{6,2},{1,5},{3,7},{5,1},{7,3},{8,12},{10,14},{12... | collective-permute-start | bytes 983048 | tf_op jit(solution)/shard_map/ppermute | solution.py:40
  38.6 1.3 collective-permute-start.2
  40.0 1.7 bitcast_dynamic-update-slice_fusion.3
  41.7 3.4 %collective-permute-done.1 = bf16[4,32,1280]{2,1,0:T(8,128)(2,1)S(1)} collective-permute-done((bf16[4,32,1280]{2,1,0:T(8,128)(2,1)S(1)}, bf16[4,32,1280]{2,1,0:T(8,128)(2,1)S(1)}, u32[]{:S(2)}, u32[]{:S(2)}) %collective-permute-start.1) | collective-permute-done | bytes 327712 | tf_op jit(solution)/shard_map/ppermute | solution.py:40
  45.9 3.8 %collective-permute-done.2 = bf16[4,32,1280]{2,1,0:T(8,128)(2,1)S(1)} collective-permute-done((bf16[4,32,1280]{2,1,0:T(8,128)(2,1)S(1)}, bf16[4,32,1280]{2,1,0:T(8,128)(2,1)S(1)}, u32[]{:S(2)}, u32[]{:S(2)}) %collective-permute-start.2) | collective-permute-done | bytes 327712 | tf_op jit(solution)/shard_map/ppermute | solution.py:40
  50.5 1.2 maximum_bitcast_fusion
  51.7 9.4 %all-to-all-start = ((bf16[64,4,1190]{2,1,0:T(4,128)(2,1)}), bf16[64,4,1190]{2,1,0:T(4,128)(2,1)}, u32[]{:S(2)}, u32[]{:S(2)}) async-start(bf16[64,4,1190]{2,1,0:T(4,128)(2,1)} %maximum_bitcast_fusion), calls=%async_computation | async-start | bytes 1310720 | tf_op jit(solution)/shard_map/all_to_all | solution.py:61
  61.1 1.8 broadcast_in_dim.49
  62.9 2.5 bitcast_dynamic-update-slice_fusion
  65.4 16.1 %all-to-all-done = bf16[64,4,1190]{2,1,0:T(4,128)(2,1)} async-done(((bf16[64,4,1190]{2,1,0:T(4,128)(2,1)}), bf16[64,4,1190]{2,1,0:T(4,128)(2,1)}, u32[]{:S(2)}, u32[]{:S(2)}) %all-to-all-start) | async-done | bytes 609312 | tf_op jit(solution)/shard_map/all_to_all | solution.py:61
  81.5 14.2 %copy.55 = f32[8,4,2,4,1190]{0,3,1,2,4:T(4,128)} copy(bf16[8,4,2,4,1190]{4,3,2,1,0:T(4,128)(2,1)} %bitcast.44) | data formatting | bytes 1827840 | tf_op jit(solution)/shard_map/convert_element_type | solution.py:63
  95.7 2.5 bitcast_dynamic-update-slice_fusion.1
  98.2 2.9 %fusion.21 = (bf16[1,2,4,32,1280]{4,3,2,1,0:T(8,128)(2,1)S(1)}, bf16[1,2,4,32,1280]{4,3,2,1,0:T(8,128)(2,1)S(1)}, bf16[1,2,4,32,1280]{4,3,2,1,0:T(8,128)(2,1)S(1)}, bf16[1,2,4,32,1280]{4,3,2,1,0:T(8,128)(2,1)}) fusion(bf16[4,2,4,32,1280]{4,3,2,1,0:T(8,128)(2,1)} %bitcast_dynamic-update-slice_fusion.1), kind=kLoop, calls=%fused_computation.69 | loop fusion | bytes 5242880 | tf_op jit(solution)/shard_map/slice | solution.py:94
  101.1 1.8 fusion.3
  102.9 1.8 fusion.5
  104.8 1.8 fusion.4
  106.6 1.4 collective-permute-start.5
  108.6 1.8 collective-permute-start.4
  110.4 10.9 %slice_reduce_fusion = (f32[2,4,8,4]{2,3,1,0:T(4,128)S(1)}, f32[1187,2,4,8,4]{3,4,2,1,0:T(4,128)}) fusion(f32[1190,2,4,8,4]{3,4,2,1,0:T(4,128)S(1)} %bitcast.112), kind=kLoop, calls=%fused_computation.68 | loop fusion | flops 303616 | bytes 2432000 | tf_op jit(solution)/shard_map/reduce_max | solution.py:69
  121.7 15.3 %copy.57 = f32[1187,2,4,8,4]{0,4,3,2,1:T(4,128)} copy(f32[1187,2,4,8,4]{3,4,2,1,0:T(4,128)} %get-tuple-element.9) | data formatting | bytes 2430976 | tf_op jit(solution)/shard_map/slice | solution.py:64
  137.0 2.7 %slice.42 = f32[1187,256]{0,1:T(8,128)} reshape(f32[1187,2,4,8,4]{0,4,3,2,1:T(4,128)} %copy.57) | data formatting | bytes 2430976 | tf_op jit(solution)/shard_map/slice | solution.py:64
  139.6 2.7 %copy.66 = f32[1187,256]{1,0:T(8,128)} copy(f32[1187,256]{0,1:T(8,128)} %slice.42) | data formatting | bytes 2430976 | tf_op jit(solution)/shard_map/slice | solution.py:64
  142.4 2.9 %fusion.23 = (f32[256]{0:T(256)S(1)}, f32[1187,256]{1,0:T(8,128)S(1)}) fusion(f16[1187,256]{1,0:T(8,128)(2,1)} %collective-permute-done.6, f16[1187,256]{1,0:T(8,128)(2,1)} %collective-permute-done.5, f16[1187,256]{1,0:T(8,128)(2,1)} %collective-permute-done.4, bf16[256,1280]{1,0:T(8,128)(2,1)} %bitcast.116, bf16[1280,1187]{0,1:T(8,128)(2,1)S(1)} %copy-done), kind=kOutput, calls=%fused_computation.71 | convolution fusion | flops 780039168 | bytes 6733824 | tf_op jit(solution)/shard_map/dot_general | solution.py:93
  147.1 5.8 %all-to-all-start.2 = ((f32[64,8,128]{2,1,0:T(8,128)}), f32[64,8,128]{2,1,0:T(8,128)S(1)}, u32[]{:S(2)}, u32[]{:S(2)}) async-start(f32[64,8,128]{2,1,0:T(8,128)} %broadcast_in_dim.59), calls=%async_computation.2 | async-start | bytes 524288 | tf_op jit(solution)/shard_map/all_to_all | solution.py:105
  153.9 12.0 %all-to-all-done.2 = f32[64,8,128]{2,1,0:T(8,128)S(1)} async-done(((f32[64,8,128]{2,1,0:T(8,128)}), f32[64,8,128]{2,1,0:T(8,128)S(1)}, u32[]{:S(2)}, u32[]{:S(2)}) %all-to-all-start.2) | async-done | bytes 262176 | tf_op jit(solution)/shard_map/all_to_all | solution.py:105
  166.1 2.3 multiply_convert_fusion
  168.4 1.6 collective-permute-start.9
  170.0 2.2 collective-permute-start.8
  172.2 12.9 %collective-permute-done.9 = bf16[1187,256]{1,0:T(8,128)(2,1)S(1)} collective-permute-done((bf16[1187,256]{1,0:T(8,128)(2,1)S(1)}, bf16[1187,256]{1,0:T(8,128)(2,1)S(1)}, u32[]{:S(2)}, u32[]{:S(2)}) %collective-permute-start.9) | collective-permute-done | bytes 607776 | tf_op jit(solution)/shard_map/ppermute | solution.py:125
  185.1 3.1 %collective-permute-done.8 = bf16[1187,256]{1,0:T(8,128)(2,1)S(1)} collective-permute-done((bf16[1187,256]{1,0:T(8,128)(2,1)S(1)}, bf16[1187,256]{1,0:T(8,128)(2,1)S(1)}, u32[]{:S(2)}, u32[]{:S(2)}) %collective-permute-start.8) | collective-permute-done | bytes 607776 | tf_op jit(solution)/shard_map/ppermute | solution.py:125
  188.2 12.0 %collective-permute-done.7 = bf16[1187,256]{1,0:T(8,128)(2,1)S(1)} collective-permute-done((bf16[1187,256]{1,0:T(8,128)(2,1)S(1)}, bf16[1187,256]{1,0:T(8,128)(2,1)S(1)}, u32[]{:S(2)}, u32[]{:S(2)}) %collective-permute-start.7) | collective-permute-done | bytes 607776 | tf_op jit(solution)/shard_map/ppermute | solution.py:125
  200.3 3.7 %fusion.10 = f32[1024,1280]{1,0:T(8,128)S(1)} fusion(bf16[1280,1187]{0,1:T(8,128)(2,1)S(1)} %copy-done, bf16[1187,256]{1,0:T(8,128)(2,1)S(1)} %collective-permute-done.9, bf16[1187,256]{1,0:T(8,128)(2,1)S(1)} %collective-permute-done.8, bf16[1187,256]{1,0:T(8,128)(2,1)S(1)} %collective-permute-done.7, bf16[1187,256]{1,0:T(8,128)(2,1)S(1)} %multiply_convert_fusion), kind=kOutput, calls=%fused_computation.34 | convolution fusion | flops 3121373184 | bytes 10712576 | tf_op jit(solution)/shard_map/dot_general | solution.py:128
  204.0 2.3 copy-done.5
  206.3 1.2 fusion.6
  207.6 3.4 %collective-permute-done.10 = bf16[4,4,32,1280]{3,2,1,0:T(8,128)(2,1)} collective-permute-done((bf16[4,4,32,1280]{3,2,1,0:T(8,128)(2,1)}, bf16[4,4,32,1280]{3,2,1,0:T(8,128)(2,1)}, u32[]{:S(2)}, u32[]{:S(2)}) %collective-permute-start.10) | collective-permute-done | bytes 1310752 | tf_op jit(solution)/shard_map/ppermute | solution.py:131
  210.9 2.4 bitcast_add_fusion
  213.4 1.5 copy-done.3
  216.5 2.5 collective-permute-start.13
  219.6 14.6 %collective-permute-done.11 = bf16[4,32,1280]{2,1,0:T(8,128)(2,1)} collective-permute-done((bf16[4,32,1280]{2,1,0:T(8,128)(2,1)}, bf16[4,32,1280]{2,1,0:T(8,128)(2,1)}, u32[]{:S(2)}, u32[]{:S(2)}) %collective-permute-start.11) | collective-permute-done | bytes 327712 | tf_op jit(solution)/shard_map/ppermute | solution.py:136
  234.1 1.5 fusion.9
  236.6 5.8 %all-to-all-start.3 = ((bf16[32,4,1280]{2,1,0:T(4,128)(2,1)}), bf16[32,4,1280]{2,1,0:T(4,128)(2,1)S(1)}, u32[]{:S(2)}, u32[]{:S(2)}) async-start(bf16[32,4,1280]{2,1,0:T(4,128)(2,1)} %reshape.190), calls=%async_computation.3 | async-start | bytes 655360 | tf_op jit(solution)/shard_map/all_to_all | solution.py:138
  242.4 7.4 %convolution_convert_fusion = bf16[1280,1187]{0,1:T(8,128)(2,1)} fusion(bf16[1024,1280]{1,0:T(8,128)(2,1)} %bitcast.43, bf16[1187,256]{1,0:T(8,128)(2,1)} %copy-done.10, bf16[1187,256]{1,0:T(8,128)(2,1)} %copy-done.11, bf16[1187,256]{1,0:T(8,128)(2,1)} %copy-done.12, bf16[1187,256]{1,0:T(8,128)(2,1)} %copy-done.8), kind=kOutput, calls=%fused_computation | convolution fusion | flops 3122892544 | bytes 8091136 | tf_op jit(solution)/shard_map/dot_general | solution.py:141
  249.8 3.6 %all-to-all-done.3 = bf16[32,4,1280]{2,1,0:T(4,128)(2,1)S(1)} async-done(((bf16[32,4,1280]{2,1,0:T(4,128)(2,1)}), bf16[32,4,1280]{2,1,0:T(4,128)(2,1)S(1)}, u32[]{:S(2)}, u32[]{:S(2)}) %all-to-all-start.3) | async-done | bytes 327712 | tf_op jit(solution)/shard_map/all_to_all | solution.py:138
  (70 shorter events, 14.1 us)
Async XLA Ops:
  0.6 100.5 %copy-start = (bf16[1280,1187]{0,1:T(8,128)(2,1)S(1)}, bf16[1280,1187]{0,1:T(8,128)(2,1)}, u32[]{:S(2)}) copy-start(bf16[1280,1187]{0,1:T(8,128)(2,1)} %param.6) | copy-start | bytes 9116164
  2.4 23.3 %all-to-all-start.1 = ((bf16[32,4,1280]{2,1,0:T(4,128)(2,1)}), bf16[32,4,1280]{2,1,0:T(4,128)(2,1)S(1)}, u32[]{:S(2)}, u32[]{:S(2)}) async-start(bf16[32,4,1280]{2,1,0:T(4,128)(2,1)} %bitcast.115), calls=%async_computation.1 | async-start | bytes 655360 | tf_op jit(solution)/shard_map/all_to_all | solution.py:35
  26.5 1.2 copy-start.7
  26.5 3.6 %copy-start.9 = (f32[4]{0:T(128)S(1)}, f32[4]{0:T(128)}, u32[]{:S(2)}) copy-start(f32[4]{0:T(128)} %param.7) | copy-start | bytes 52
  28.6 11.4 %collective-permute-start = (bf16[4,32,1280]{2,1,0:T(8,128)(2,1)S(1)}, bf16[4,32,1280]{2,1,0:T(8,128)(2,1)}, u32[]{:S(2)}, u32[]{:S(2)}) collective-permute-start(bf16[4,32,1280]{2,1,0:T(8,128)(2,1)S(1)} %get-tuple-element.7), channel_id=1, source_target_pairs={{0,2},{2,4},{4,6},{6,0},{1,3},{3,5},{5,7},{7,1},{8,10},{10,12},{12... | collective-permute-start | bytes 983048 | tf_op jit(solution)/shard_map/ppermute | solution.py:40
  35.7 14.8 %copy-start.6 = (bf16[4,64,1187]{2,0,1:T(4,128)(2,1)S(1)}, bf16[4,64,1187]{2,0,1:T(4,128)(2,1)}, u32[]{:S(2)}) copy-start(bf16[4,64,1187]{2,0,1:T(4,128)(2,1)} %copy.54) | copy-start | bytes 1823236
  35.7 9.4 %collective-permute-start.1 = (bf16[4,32,1280]{2,1,0:T(8,128)(2,1)S(1)}, bf16[4,32,1280]{2,1,0:T(8,128)(2,1)S(1)}, u32[]{:S(2)}, u32[]{:S(2)}) collective-permute-start(bf16[4,32,1280]{2,1,0:T(8,128)(2,1)S(1)} %get-tuple-element.7), channel_id=1, source_target_pairs={{0,4},{2,6},{4,0},{6,2},{1,5},{3,7},{5,1},{7,3},{8,12},{10,14},{12... | collective-permute-start | bytes 983048 | tf_op jit(solution)/shard_map/ppermute | solution.py:40
  38.6 11.1 %collective-permute-start.2 = (bf16[4,32,1280]{2,1,0:T(8,128)(2,1)S(1)}, bf16[4,32,1280]{2,1,0:T(8,128)(2,1)S(1)}, u32[]{:S(2)}, u32[]{:S(2)}) collective-permute-start(bf16[4,32,1280]{2,1,0:T(8,128)(2,1)S(1)} %get-tuple-element.7), channel_id=1, source_target_pairs={{0,6},{2,0},{4,2},{6,4},{1,7},{3,1},{5,3},{7,5},{8,14},{10,8},{12,... | collective-permute-start | bytes 983048 | tf_op jit(solution)/shard_map/ppermute | solution.py:40
  50.4 45.3 %collective-permute-start.3 = (bf16[4,4,32,1280]{3,2,1,0:T(8,128)(2,1)}, bf16[4,4,32,1280]{3,2,1,0:T(8,128)(2,1)}, u32[]{:S(2)}, u32[]{:S(2)}) collective-permute-start(bf16[4,4,32,1280]{3,2,1,0:T(8,128)(2,1)} %bitcast_dynamic-update-slice_fusion.4), channel_id=1, source_target_pairs={{0,1},{1,0},{2,3},{3,2},{4,5},{5,4},{6,7},{7,6},{8,9},{9,8},{10,11... | collective-permute-start | bytes 3932168 | tf_op jit(solution)/shard_map/ppermute | solution.py:42
  51.7 29.8 %all-to-all-start = ((bf16[64,4,1190]{2,1,0:T(4,128)(2,1)}), bf16[64,4,1190]{2,1,0:T(4,128)(2,1)}, u32[]{:S(2)}, u32[]{:S(2)}) async-start(bf16[64,4,1190]{2,1,0:T(4,128)(2,1)} %maximum_bitcast_fusion), calls=%async_computation | async-start | bytes 1310720 | tf_op jit(solution)/shard_map/all_to_all | solution.py:61
  98.2 12.2 %copy-start.1 = (f32[8,4,2,4,1190]{0,3,1,2,4:T(4,128)S(1)}, f32[8,4,2,4,1190]{0,3,1,2,4:T(4,128)}, u32[]{:S(2)}) copy-start(f32[8,4,2,4,1190]{0,3,1,2,4:T(4,128)} %copy.55) | copy-start | bytes 3655684
  106.6 35.8 %collective-permute-start.5 = (f16[1187,256]{1,0:T(8,128)(2,1)}, f16[1187,256]{1,0:T(8,128)(2,1)}, u32[]{:S(2)}, u32[]{:S(2)}) collective-permute-start(f16[1187,256]{1,0:T(8,128)(2,1)} %fusion.4), channel_id=1, source_target_pairs={{0,64},{64,128},{128,192},{192,0},{1,65},{65,129},{129,193},{193,1... | collective-permute-start | bytes 1823240 | tf_op jit(solution)/shard_map/ppermute | solution.py:98
  108.0 34.4 %collective-permute-start.6 = (f16[1187,256]{1,0:T(8,128)(2,1)}, f16[1187,256]{1,0:T(8,128)(2,1)}, u32[]{:S(2)}, u32[]{:S(2)}) collective-permute-start(f16[1187,256]{1,0:T(8,128)(2,1)} %fusion.5), channel_id=1, source_target_pairs={{0,192},{64,0},{128,64},{192,128},{1,193},{65,1},{129,65},{193,129... | collective-permute-start | bytes 1823240 | tf_op jit(solution)/shard_map/ppermute | solution.py:98
  108.6 33.8 %collective-permute-start.4 = (f16[1187,256]{1,0:T(8,128)(2,1)}, f16[1187,256]{1,0:T(8,128)(2,1)}, u32[]{:S(2)}, u32[]{:S(2)}) collective-permute-start(f16[1187,256]{1,0:T(8,128)(2,1)} %fusion.3), channel_id=1, source_target_pairs={{0,128},{64,192},{128,0},{192,64},{1,129},{65,193},{129,1},{193,65... | collective-permute-start | bytes 1823240 | tf_op jit(solution)/shard_map/ppermute | solution.py:98
  142.4 2.9 %copy-start.2 = (f32[1187,256]{1,0:T(8,128)S(1)}, f32[1187,256]{1,0:T(8,128)}, u32[]{:S(2)}) copy-start(f32[1187,256]{1,0:T(8,128)} %copy.66) | copy-start | bytes 3646468
  145.3 1.0 copy-start.4
  147.1 18.7 %all-to-all-start.2 = ((f32[64,8,128]{2,1,0:T(8,128)}), f32[64,8,128]{2,1,0:T(8,128)S(1)}, u32[]{:S(2)}, u32[]{:S(2)}) async-start(f32[64,8,128]{2,1,0:T(8,128)} %broadcast_in_dim.59), calls=%async_computation.2 | async-start | bytes 524288 | tf_op jit(solution)/shard_map/all_to_all | solution.py:105
  168.4 35.6 %copy-start.8 = (bf16[1187,256]{1,0:T(8,128)(2,1)}, bf16[1187,256]{1,0:T(8,128)(2,1)S(1)}, u32[]{:S(2)}) copy-start(bf16[1187,256]{1,0:T(8,128)(2,1)S(1)} %multiply_convert_fusion) | copy-start | bytes 1823236
  168.4 16.7 %collective-permute-start.9 = (bf16[1187,256]{1,0:T(8,128)(2,1)S(1)}, bf16[1187,256]{1,0:T(8,128)(2,1)S(1)}, u32[]{:S(2)}, u32[]{:S(2)}) collective-permute-start(bf16[1187,256]{1,0:T(8,128)(2,1)S(1)} %multiply_convert_fusion), channel_id=1, source_target_pairs={{0,64},{64,128},{128,192},{192,0},{1,65},{65,129},{129,193},{193,1... | collective-permute-start | bytes 1823240 | tf_op jit(solution)/shard_map/ppermute | solution.py:125
  170.0 18.2 %collective-permute-start.8 = (bf16[1187,256]{1,0:T(8,128)(2,1)S(1)}, bf16[1187,256]{1,0:T(8,128)(2,1)S(1)}, u32[]{:S(2)}, u32[]{:S(2)}) collective-permute-start(bf16[1187,256]{1,0:T(8,128)(2,1)S(1)} %multiply_convert_fusion), channel_id=1, source_target_pairs={{0,128},{64,192},{128,0},{192,64},{1,129},{65,193},{129,1},{193,65... | collective-permute-start | bytes 1823240 | tf_op jit(solution)/shard_map/ppermute | solution.py:125
  172.2 28.1 %collective-permute-start.7 = (bf16[1187,256]{1,0:T(8,128)(2,1)S(1)}, bf16[1187,256]{1,0:T(8,128)(2,1)S(1)}, u32[]{:S(2)}, u32[]{:S(2)}) collective-permute-start(bf16[1187,256]{1,0:T(8,128)(2,1)S(1)} %multiply_convert_fusion), channel_id=1, source_target_pairs={{0,192},{64,0},{128,64},{192,128},{1,193},{65,1},{129,65},{193,129... | collective-permute-start | bytes 1823240 | tf_op jit(solution)/shard_map/ppermute | solution.py:125
  185.1 18.9 %copy-start.10 = (bf16[1187,256]{1,0:T(8,128)(2,1)}, bf16[1187,256]{1,0:T(8,128)(2,1)S(1)}, u32[]{:S(2)}) copy-start(bf16[1187,256]{1,0:T(8,128)(2,1)S(1)} %collective-permute-done.9) | copy-start | bytes 1823236
  188.2 15.8 %copy-start.11 = (bf16[1187,256]{1,0:T(8,128)(2,1)}, bf16[1187,256]{1,0:T(8,128)(2,1)S(1)}, u32[]{:S(2)}) copy-start(bf16[1187,256]{1,0:T(8,128)(2,1)S(1)} %collective-permute-done.8) | copy-start | bytes 1823236
  200.2 3.8 %copy-start.12 = (bf16[1187,256]{1,0:T(8,128)(2,1)}, bf16[1187,256]{1,0:T(8,128)(2,1)S(1)}, u32[]{:S(2)}) copy-start(bf16[1187,256]{1,0:T(8,128)(2,1)S(1)} %collective-permute-done.7) | copy-start | bytes 1823236
  204.0 2.3 copy-start.5
  207.6 3.4 %collective-permute-start.10 = (bf16[4,4,32,1280]{3,2,1,0:T(8,128)(2,1)}, bf16[4,4,32,1280]{3,2,1,0:T(8,128)(2,1)}, u32[]{:S(2)}, u32[]{:S(2)}) collective-permute-start(bf16[4,4,32,1280]{3,2,1,0:T(8,128)(2,1)} %fusion.6), channel_id=1, source_target_pairs={{0,1},{1,0},{2,3},{3,2},{4,5},{5,4},{6,7},{7,6},{8,9},{9,8},{10,11... | collective-permute-start | bytes 3932168 | tf_op jit(solution)/shard_map/ppermute | solution.py:131
  213.4 1.5 copy-start.3
  215.8 18.3 %collective-permute-start.11 = (bf16[4,32,1280]{2,1,0:T(8,128)(2,1)}, bf16[4,32,1280]{2,1,0:T(8,128)(2,1)}, u32[]{:S(2)}, u32[]{:S(2)}) collective-permute-start(bf16[4,32,1280]{2,1,0:T(8,128)(2,1)} %get-tuple-element.10), channel_id=1, source_target_pairs={{0,2},{2,4},{4,6},{6,0},{1,3},{3,5},{5,7},{7,1},{8,10},{10,12},{12... | collective-permute-start | bytes 983048 | tf_op jit(solution)/shard_map/ppermute | solution.py:136
  216.5 17.6 %collective-permute-start.13 = (bf16[4,32,1280]{2,1,0:T(8,128)(2,1)}, bf16[4,32,1280]{2,1,0:T(8,128)(2,1)}, u32[]{:S(2)}, u32[]{:S(2)}) collective-permute-start(bf16[4,32,1280]{2,1,0:T(8,128)(2,1)} %get-tuple-element.11), channel_id=1, source_target_pairs={{0,6},{2,0},{4,2},{6,4},{1,7},{3,1},{5,3},{7,5},{8,14},{10,8},{12,... | collective-permute-start | bytes 983048 | tf_op jit(solution)/shard_map/ppermute | solution.py:136
  219.1 15.1 %collective-permute-start.12 = (bf16[4,32,1280]{2,1,0:T(8,128)(2,1)S(1)}, bf16[4,32,1280]{2,1,0:T(8,128)(2,1)}, u32[]{:S(2)}, u32[]{:S(2)}) collective-permute-start(bf16[4,32,1280]{2,1,0:T(8,128)(2,1)S(1)} %get-tuple-element.12), channel_id=1, source_target_pairs={{0,4},{2,6},{4,0},{6,2},{1,5},{3,7},{5,1},{7,3},{8,12},{10,14},{12... | collective-permute-start | bytes 983048 | tf_op jit(solution)/shard_map/ppermute | solution.py:136
  236.6 16.8 %all-to-all-start.3 = ((bf16[32,4,1280]{2,1,0:T(4,128)(2,1)}), bf16[32,4,1280]{2,1,0:T(4,128)(2,1)S(1)}, u32[]{:S(2)}, u32[]{:S(2)}) async-start(bf16[32,4,1280]{2,1,0:T(4,128)(2,1)} %reshape.190), calls=%async_computation.3 | async-start | bytes 655360 | tf_op jit(solution)/shard_map/all_to_all | solution.py:138

commit v2 on v1

v2 whole, which is shorter than its diff:
```python
import jax
import jax.numpy as jnp
from jax import lax
from jax.sharding import Mesh, PartitionSpec as P

alpha_power = 0.5
beta_power = 0.25
joint_power = 0.75
smallest = 1e-37

NX, NZ, NY, NC = 4, 8, 4, 2
VOCAB = ("z", "y", "c")
OWN = 4
COLS = 1280
SLICE = 1187
SPAN = 256


def shift(count, by):
    return [(i, (i + by) % count) for i in range(count)]


def rolled(value, by):
    count = value.shape[0]
    return lax.dynamic_slice_in_dim(jnp.concatenate([value, value], axis=0), by, count, axis=0)


def gather_hidden(hidden, x):
    pieces = hidden.reshape(OWN, NX, COLS).transpose(1, 0, 2)
    spread = jnp.broadcast_to(pieces[:, None], (NX, NZ, OWN, COLS)).reshape(NX * NZ, OWN, COLS)
    got = lax.all_to_all(spread, ("x", "z"), 0, 0, tiled=True)
    mine = rolled(got.reshape(NX, NZ * OWN, COLS), x)
    near = [mine] + [lax.ppermute(mine, "y", shift(NY, by)) for by in range(1, NY)]
    far = [lax.ppermute(block, "c", shift(NC, 1)) for block in near]
    return jnp.concatenate(near + far, axis=1)


def order(y, c):
    place = jnp.arange(SPAN)
    core, back, z, own = place // 128, place // 32 % NY, place // OWN % NZ, place % OWN
    true = ((z * NY + (y - back) % NY) * NC + (c + core) % NC) * OWN + own
    return place[:, None] == true[None, :]


def split_three(value):
    high = value.astype(jnp.bfloat16)
    rest = value - high.astype(jnp.float32)
    middle = rest.astype(jnp.bfloat16)
    low = (rest - middle.astype(jnp.float32)).astype(jnp.bfloat16)
    return jnp.stack([high, middle, low], axis=-1)


def teacher_rows(teacher, loss_weight):
    parts = teacher.reshape(OWN, NZ * NY * NC, SLICE)
    weights = jnp.broadcast_to(split_three(loss_weight)[:, None], (OWN, NZ * NY * NC, 3))
    return jnp.concatenate([parts, weights], axis=2).transpose(1, 0, 2)


def gather_teacher(rows, chosen):
    got = lax.all_to_all(rows, VOCAB, 0, 0, tiled=True).reshape(SPAN, SLICE + 3)
    got = lax.dot_general(
        got,
        chosen.astype(jnp.bfloat16),
        (((0,), (0,)), ((), ())),
        preferred_element_type=jnp.float32,
    )
    return got[:SLICE], got[SLICE] + got[SLICE + 1] + got[SLICE + 2]


def row_stats(student, teacher):
    top_s = jnp.max(student, axis=0)
    top_t = jnp.max(teacher, axis=0)
    s = student - top_s
    t = teacher - top_t

    def log_sum(value):
        return jnp.log(jnp.maximum(jnp.sum(jnp.exp(value), axis=0), smallest))

    return jnp.stack(
        [
            top_s + log_sum(s),
            top_t + log_sum(t),
            alpha_power * top_t + beta_power * top_s + log_sum(alpha_power * t + beta_power * s),
            joint_power * top_s + log_sum(joint_power * s),
        ]
    )


def moved(value, chosen, axis):
    return lax.dot_general(
        value,
        chosen.astype(jnp.float32),
        (((1,), (axis,)), ((), ())),
        precision=lax.Precision.HIGHEST,
        preferred_element_type=jnp.float32,
    )


def body(hidden, teacher, head_weight, loss_weight):
    x, y, c = lax.axis_index("x"), lax.axis_index("y"), lax.axis_index("c")
    head = head_weight.T
    chosen = order(y, c)
    rows = gather_hidden(hidden, x)
    taught = teacher_rows(teacher, loss_weight)

    def partial_logits(which):
        return lax.dot_general(
            head, rows[which], (((1,), (1,)), ((), ())), preferred_element_type=jnp.float32
        )

    halves = [partial_logits(r).astype(jnp.float16) for r in (2, 1, 3)]
    halves[0], taught = lax.optimization_barrier((halves[0], taught))
    sent = [lax.ppermute(half, "x", shift(NX, r)) for half, r in zip(halves, (2, 1, 3))]
    teacher_slice, weight = gather_teacher(taught, chosen)
    logits = partial_logits(0)
    for part in sent:
        logits = logits + part.astype(jnp.float32)

    own = moved(row_stats(logits, teacher_slice), chosen, 1).reshape(8, 128)
    every = lax.all_to_all(
        jnp.broadcast_to(own[None], (NZ * NY * NC, 8, 128)), VOCAB, 0, 0, tiled=True
    ).reshape(NZ * NY * NC, 4, SPAN)
    top = jnp.max(every, axis=0)
    merged = top + jnp.log(jnp.sum(jnp.exp(every - top), axis=0))
    log_s, log_t, log_m, log_j = moved(merged, chosen, 0)
    remainder = jnp.exp(log_m - alpha_power * log_t - beta_power * log_s) - jnp.exp(
        log_j - joint_power * log_s
    )
    log_student = logits - log_s
    log_teacher = teacher_slice - log_t
    grad_logits = (
        -(weight / alpha_power)
        * (
            jnp.exp(alpha_power * log_teacher + beta_power * log_student)
            - jnp.exp(joint_power * log_student)
            - jnp.exp(log_student) * remainder
        )
    ).astype(jnp.bfloat16)

    groups = [grad_logits] + [
        lax.ppermute(grad_logits, "x", shift(NX, -r)) for r in range(1, NX)
    ]

    def shared(which):
        part = jnp.stack(
            [
                lax.dot_general(
                    groups[r], head, (((0,), (0,)), ((), ())), preferred_element_type=jnp.float32
                )
                for r in which
            ]
        ).reshape(len(which), NC, NY, NZ * OWN, COLS)
        away = lax.ppermute(part[:, 1].astype(jnp.bfloat16), "c", shift(NC, 1))
        both = part[:, 0] + away.astype(jnp.float32)
        mine = both[:, 0]
        for by in range(1, NY):
            away = lax.ppermute(both[:, by].astype(jnp.bfloat16), "y", shift(NY, -by))
            mine = mine + away.astype(jnp.float32)
        return mine.astype(jnp.bfloat16)

    early, late = shared((0, 1)), shared((2, 3))
    mine = rolled(jnp.concatenate([early, late], axis=0), (NX - x) % NX)
    got = lax.all_to_all(mine.reshape(NX * NZ, OWN, COLS), ("x", "z"), 0, 0, tiled=True)
    total = jnp.sum(got.reshape(NX, NZ, OWN, COLS).astype(jnp.float32), axis=1)
    grad_hidden = total.transpose(1, 0, 2).reshape(OWN, NX * COLS).astype(jnp.bfloat16)
    grad_head = lax.dot_general(
        jnp.concatenate(groups, axis=1),
        rows.reshape(NX * SPAN, COLS),
        (((1,), (0,)), ((), ())),
        preferred_element_type=jnp.float32,
    ).astype(jnp.bfloat16)
    return grad_hidden, grad_head.T


def solution(mesh):
    fine = Mesh(mesh.devices.reshape(NX, NZ, NY, NC), ("x", "z", "y", "c"))
    every = ("x", "z", "y", "c")
    placed = (P(every, None), P(every, None), P("x", VOCAB), P(every))
    return jax.shard_map(
        body,
        mesh=fine,
        in_specs=placed,
        out_specs=(P(every, None), P("x", VOCAB)),
        check_vma=False,
    )
```

time: 258 us -> 205 us (0.79)
  local copies, waits for them, and re-layouts: 65.5 us -> 13.8 us
  other arithmetic: 21.9 us -> 9.72 us
  matrix products: 19.5 us -> 26.1 us
  starting transfers between devices: 49.8 us -> 56.1 us
    slice x4 -> x0, local copies, waits for them, and re-layouts: 23.6 us -> none  [the longest x3 20.7 us: gather_teacher(): return (got[:SLICE], got[SLICE] + got[SLICE + 1] + got[SLICE + 2])]
    ppermute x11 -> x18, waiting for transfers between devices: 25.2 us -> 44.3 us  [the longest x3 26.7 us: body(): lax.ppermute(half, 'x', shift(NX, r))]
    convert_element_type x3 -> x2, local copies, waits for them, and re-layouts: 16.4 us -> 0.07 us  [shared(): away = lax.ppermute(both[:, by].astype(jnp.bfloat16), 'y', shift(NY, -by))]
    all_to_all x1, waiting for transfers between devices: 16.1 us -> 0.01 us  [gather_teacher(): got = lax.all_to_all(rows, VOCAB, 0, 0, tiled=True).reshape(SPAN, SLICE + 3)]
    reduce_max x1, other arithmetic: 10.9 us -> 0.17 us  [row_stats(): top_t = jnp.max(teacher, axis=0)]
    dynamic_update_slice x5 -> x0, local copies, waits for them, and re-layouts: 8.18 us -> none  [the longest x3 3.21 us: gather_hidden(): lax.dynamic_update_slice(half, part[:, None], (0, (y - by) % NY, 0, 0))]
    all_to_all x1, starting transfers between devices: 5.76 us -> 10.4 us  [body(): lax.all_to_all(jnp.broadcast_to(own[None], (NZ * NY * NC, 8, 128)), VOCAB...]
    dot_general x2 -> x8, matrix products: 11.1 us -> 15.6 us  [the longest x1 7.37 us: body(): lax.dot_general(jnp.concatenate(groups, axis=1), rows.reshape(NX * SPAN,...]
  transfers between devices with their start and end apart: 18 -> 25, of which waited for: 11 -> 16; matrix products, arithmetic and copies ran while one was open for 27% -> 15% of each run, Pallas kernels for 0% -> 0%
where the time goes in v2:
time: 205 us; the launch traced here: 202 us
  waiting for transfers between devices  95.3 us (46%)
  starting transfers between devices  56.1 us (27%)
  matrix products  26.1 us (13%)
  local copies, waits for them, and re-layouts  13.8 us (7%)
  other arithmetic  9.72 us (5%)
    ppermute x3, waiting for transfers between devices, body(): lax.ppermute(half, 'x', shift(NX, r))  26.7 us
    ppermute x3, waiting for transfers between devices, body(): lax.ppermute(grad_logits, 'x', shift(NX, -r))  24.5 us
    all_to_all x1, waiting for transfers between devices, body(): lax.all_to_all(jnp.broadcast_to(own[None], (NZ * NY * NC, 8, 128)), VOCAB...  12.1 us
    all_to_all x1, starting transfers between devices, gather_hidden(): got = lax.all_to_all(spread, ('x', 'z'), 0, 0, tiled=True)  11.7 us
    all_to_all x1, waiting for transfers between devices, gather_hidden(): got = lax.all_to_all(spread, ('x', 'z'), 0, 0, tiled=True)  11 us
    dot_general x4, matrix products, partial_logits(): lax.dot_general(head, rows[which], (((1,), (1,)), ((), ())), preferred_el...  10.4 us
    all_to_all x1, starting transfers between devices, body(): lax.all_to_all(jnp.broadcast_to(own[None], (NZ * NY * NC, 8, 128)), VOCAB...  10.4 us
    ppermute x6, waiting for transfers between devices, shared(): away = lax.ppermute(both[:, by].astype(jnp.bfloat16), 'y', shift(NY, -by))  10.3 us
  transfers between devices with their start and end apart: 25, of which 16 were waited for; matrix products, arithmetic and copies ran while one was open for 15% of the time, Pallas kernels for 0%

profile of v2, /device:TPU:6, one launch (start us, length us, event | category | flops | bytes accessed | tf_op | source)
XLA Modules:
  0.0 202.0 jit_solution(7286321283923489416)
XLA Ops:
  0.6 1.0 reshape.256
  2.4 11.7 %all-to-all-start = ((bf16[32,4,1280]{2,1,0:T(4,128)(2,1)}), bf16[32,4,1280]{2,1,0:T(4,128)(2,1)}, u32[]{:S(2)}, u32[]{:S(2)}) async-start(bf16[32,4,1280]{2,1,0:T(4,128)(2,1)} %bitcast.1), calls=%async_computation | async-start | bytes 655360 | tf_op jit(solution)/shard_map/all_to_all | solution.py:31
  14.8 11.0 %all-to-all-done = bf16[32,4,1280]{2,1,0:T(4,128)(2,1)} async-done(((bf16[32,4,1280]{2,1,0:T(4,128)(2,1)}), bf16[32,4,1280]{2,1,0:T(4,128)(2,1)}, u32[]{:S(2)}, u32[]{:S(2)}) %all-to-all-start) | async-done | bytes 327712 | tf_op jit(solution)/shard_map/all_to_all | solution.py:31
  25.8 1.1 reshape.258
  26.9 1.0 constant_dynamic-update-slice_fusion.7
  27.9 3.0 %collective-permute-start.2 = (bf16[4,32,1280]{2,1,0:T(8,128)(2,1)}, bf16[4,32,1280]{2,1,0:T(8,128)(2,1)S(1)}, u32[]{:S(2)}, u32[]{:S(2)}) collective-permute-start(bf16[4,32,1280]{2,1,0:T(8,128)(2,1)} %get-tuple-element.15), channel_id=1, source_target_pairs={{0,6},{2,0},{4,2},{6,4},{1,7},{3,1},{5,3},{7,5},{8,14},{10,8},{12,... | collective-permute-start | bytes 983048 | tf_op jit(solution)/shard_map/ppermute | solution.py:33
  31.5 1.0 collective-permute-start
  32.6 3.0 %reshape.259 = bf16[4,64,1187]{2,1,0:T(8,128)(2,1)} reshape(bf16[4,75968]{1,0:T(4,128)(2,1)} %param.5) | data formatting | bytes 1215488 | tf_op jit(solution)/shard_map/reshape | solution.py:54
  35.6 1.7 copy.34
  37.3 1.2 maximum_bitcast_fusion
  38.5 3.9 %collective-permute-done.2 = bf16[4,32,1280]{2,1,0:T(8,128)(2,1)S(1)} collective-permute-done((bf16[4,32,1280]{2,1,0:T(8,128)(2,1)}, bf16[4,32,1280]{2,1,0:T(8,128)(2,1)S(1)}, u32[]{:S(2)}, u32[]{:S(2)}) %collective-permute-start.2) | collective-permute-done | bytes 327712 | tf_op jit(solution)/shard_map/ppermute | solution.py:33
  42.9 3.2 %collective-permute-done = bf16[4,32,1280]{2,1,0:T(8,128)(2,1)} collective-permute-done((bf16[4,32,1280]{2,1,0:T(8,128)(2,1)}, bf16[4,32,1280]{2,1,0:T(8,128)(2,1)}, u32[]{:S(2)}, u32[]{:S(2)}) %collective-permute-start) | collective-permute-done | bytes 327712 | tf_op jit(solution)/shard_map/ppermute | solution.py:33
  46.1 1.0 constant_dynamic-update-slice_fusion.6
  47.1 1.0 constant_dynamic-update-slice_fusion.5
  48.3 1.8 fusion.5
  50.2 1.9 fusion.3
  52.0 6.9 %all-to-all-start.1 = ((bf16[64,4,1190]{2,1,0:T(4,128)(2,1)}), bf16[64,4,1190]{2,1,0:T(4,128)(2,1)}, u32[]{:S(2)}, u32[]{:S(2)}) async-start(bf16[64,4,1190]{2,1,0:T(4,128)(2,1)} %maximum_bitcast_fusion), calls=%async_computation.1 | async-start | bytes 1310720 | tf_op jit(solution)/shard_map/all_to_all | solution.py:60
  58.9 2.9 %fusion.4 = f16[1187,256]{1,0:T(8,128)(2,1)} fusion(bf16[1280,1187]{0,1:T(8,128)(2,1)S(1)} %copy-done, bf16[4,256,1280]{2,1,0:T(8,128)(2,1)} %copy-done.4), kind=kOutput, calls=%fused_computation.13 | convolution fusion | flops 778216192 | bytes 4301824 | tf_op jit(solution)/shard_map/dot_general | solution.py:107
  61.9 1.8 collective-permute-start.7
  63.7 1.6 collective-permute-start.8
  65.8 14.6 %collective-permute-done.7 = f16[1187,256]{1,0:T(8,128)(2,1)} collective-permute-done((f16[1187,256]{1,0:T(8,128)(2,1)}, f16[1187,256]{1,0:T(8,128)(2,1)}, u32[]{:S(2)}, u32[]{:S(2)}) %collective-permute-start.7) | collective-permute-done | bytes 607776 | tf_op jit(solution)/shard_map/ppermute | solution.py:113
  80.4 10.8 %collective-permute-done.8 = f16[1187,256]{1,0:T(8,128)(2,1)} collective-permute-done((f16[1187,256]{1,0:T(8,128)(2,1)}, f16[1187,256]{1,0:T(8,128)(2,1)}, u32[]{:S(2)}, u32[]{:S(2)}) %collective-permute-start.8) | collective-permute-done | bytes 607776 | tf_op jit(solution)/shard_map/ppermute | solution.py:113
  91.2 1.2 collective-permute-done.9
  92.5 3.8 %fusion.76 = (f32[256]{0:T(256)S(1)}, f32[1187,256]{1,0:T(8,128)}) fusion(f16[1187,256]{1,0:T(8,128)(2,1)} %collective-permute-done.9, f16[1187,256]{1,0:T(8,128)(2,1)} %collective-permute-done.8, f16[1187,256]{1,0:T(8,128)(2,1)} %collective-permute-done.7, bf16[1280,1187]{0,1:T(8,128)(2,1)S(1)} %copy-done, bf16[4,256,1280]{2,1,0:T(8,128)(2,1)} %copy-done.4), kind=kOutput, calls=%fused_computation.157 | convolution fusion | flops 780039168 | bytes 6741504 | tf_op jit(solution)/shard_map/dot_general | solution.py:107
  96.2 2.2 %reshape.260 = bf16[256,1190]{1,0:T(8,128)(2,1)} reshape(bf16[64,4,1190]{2,1,0:T(4,128)(2,1)} %all-to-all-done.1) | data formatting | bytes 1218560 | tf_op jit(solution)/shard_map/reshape | solution.py:60
  98.5 1.6 fusion.37
  102.0 10.4 %all-to-all-start.2 = ((f32[64,8,128]{2,1,0:T(8,128)}), f32[64,8,128]{2,1,0:T(8,128)S(1)}, u32[]{:S(2)}, u32[]{:S(2)}) async-start(f32[64,8,128]{2,1,0:T(8,128)} %broadcast_in_dim.11), calls=%async_computation.2 | async-start | bytes 524288 | tf_op jit(solution)/shard_map/all_to_all | solution.py:120
  113.2 12.1 %all-to-all-done.2 = f32[64,8,128]{2,1,0:T(8,128)S(1)} async-done(((f32[64,8,128]{2,1,0:T(8,128)}), f32[64,8,128]{2,1,0:T(8,128)S(1)}, u32[]{:S(2)}, u32[]{:S(2)}) %all-to-all-start.2) | async-done | bytes 262176 | tf_op jit(solution)/shard_map/all_to_all | solution.py:120
  125.8 3.2 %multiply_convert_fusion = bf16[1187,256]{1,0:T(8,128)(2,1)} fusion(f32[1187,256]{1,0:T(8,128)} %get-tuple-element.33, f32[1190,256]{1,0:T(8,128)} %copy-done.1, f32[256]{0:T(256)S(1)} %bitcast.141, f32[256]{0:T(256)S(1)} %bitcast.142, f32[256]{0:T(256)S(1)} %bitcast.140, f32[256]{0:T(256)S(1)} %bitcast.143), kind=kLoop, calls=%fused_computation.32 | loop fusion | flops 3342592 | bytes 3042816 | tf_op jit(solution)/shard_map/convert_element_type | solution.py:138
  129.4 2.8 %collective-permute-start.16 = (bf16[1187,256]{1,0:T(8,128)(2,1)}, bf16[1187,256]{1,0:T(8,128)(2,1)S(1)}, u32[]{:S(2)}, u32[]{:S(2)}) collective-permute-start(bf16[1187,256]{1,0:T(8,128)(2,1)} %multiply_convert_fusion), channel_id=1, source_target_pairs={{0,64},{64,128},{128,192},{192,0},{1,65},{65,129},{129,193},{193,1... | collective-permute-start | bytes 1823240 | tf_op jit(solution)/shard_map/ppermute | solution.py:141
  132.8 2.2 %fusion.77 = f32[256,1280]{1,0:T(8,128)S(1)} fusion(bf16[1187,256]{1,0:T(8,128)(2,1)} %multiply_convert_fusion, bf16[1280,1187]{0,1:T(8,128)(2,1)S(1)} %copy-done), kind=kOutput, calls=%fused_computation.158 | convolution fusion | flops 777912320 | bytes 4957184 | tf_op jit(solution)/shard_map/dot_general | solution.py:147
  135.0 24.5 %collective-permute-done.10 = bf16[1187,256]{1,0:T(8,128)(2,1)} collective-permute-done((bf16[1187,256]{1,0:T(8,128)(2,1)}, bf16[1187,256]{1,0:T(8,128)(2,1)}, u32[]{:S(2)}, u32[]{:S(2)}) %collective-permute-start.10) | collective-permute-done | bytes 607776 | tf_op jit(solution)/shard_map/ppermute | solution.py:141
  159.5 2.1 %fusion.78 = f32[256,1280]{1,0:T(8,128)S(1)} fusion(bf16[1187,256]{1,0:T(8,128)(2,1)} %collective-permute-done.10, bf16[1280,1187]{0,1:T(8,128)(2,1)S(1)} %copy-done), kind=kOutput, calls=%fused_computation.159 | convolution fusion | flops 777912320 | bytes 4957184 | tf_op jit(solution)/shard_map/dot_general | solution.py:147
  162.0 1.1 fusion.79
  163.1 1.1 fusion.80
  165.7 1.5 collective-permute-start.14
  167.2 1.7 collective-permute-start.13
  169.1 1.7 collective-permute-start.18
  171.2 1.0 collective-permute-done.12
  172.2 1.7 collective-permute-start.19
  174.0 1.5 collective-permute-done.14
  175.4 2.1 %collective-permute-done.13 = bf16[2,32,1280]{2,1,0:T(8,128)(2,1)S(1)} collective-permute-done((bf16[2,32,1280]{2,1,0:T(8,128)(2,1)S(1)}, bf16[2,32,1280]{2,1,0:T(8,128)(2,1)S(1)}, u32[]{:S(2)}, u32[]{:S(2)}) %collective-permute-start.13) | collective-permute-done | bytes 163872 | tf_op jit(solution)/shard_map/ppermute | solution.py:157
  177.6 1.7 collective-permute-done.18
  179.3 1.8 collective-permute-done.20
  181.1 2.2 %collective-permute-done.19 = bf16[2,32,1280]{2,1,0:T(8,128)(2,1)S(1)} collective-permute-done((bf16[2,32,1280]{2,1,0:T(8,128)(2,1)S(1)}, bf16[2,32,1280]{2,1,0:T(8,128)(2,1)S(1)}, u32[]{:S(2)}, u32[]{:S(2)}) %collective-permute-start.19) | collective-permute-done | bytes 163872 | tf_op jit(solution)/shard_map/ppermute | solution.py:157
  184.5 6.1 %all-to-all-start.3 = ((bf16[32,4,1280]{2,1,0:T(4,128)(2,1)}), bf16[32,4,1280]{2,1,0:T(4,128)(2,1)S(1)}, u32[]{:S(2)}, u32[]{:S(2)}) async-start(bf16[32,4,1280]{2,1,0:T(4,128)(2,1)} %reshape.261), calls=%async_computation.3 | async-start | bytes 655360 | tf_op jit(solution)/shard_map/all_to_all | solution.py:163
  190.6 7.4 %convolution_convert_fusion = bf16[1280,1187]{0,1:T(8,128)(2,1)} fusion(bf16[1024,1280]{1,0:T(8,128)(2,1)} %bitcast.138, bf16[1187,256]{1,0:T(8,128)(2,1)} %copy-done.5, bf16[1187,256]{1,0:T(8,128)(2,1)} %copy-done.6, bf16[1187,256]{1,0:T(8,128)(2,1)} %collective-permute-done.10, bf16[1187,256]{1,0:T(8,128)(2,1)} %multiply_convert_fusion), kind=kOutput, calls=%fused_computation | convolution fusion | flops 3122892544 | bytes 8091136 | tf_op jit(solution)/shard_map/dot_general | solution.py:166
  197.9 3.3 %all-to-all-done.3 = bf16[32,4,1280]{2,1,0:T(4,128)(2,1)S(1)} async-done(((bf16[32,4,1280]{2,1,0:T(4,128)(2,1)}), bf16[32,4,1280]{2,1,0:T(4,128)(2,1)S(1)}, u32[]{:S(2)}, u32[]{:S(2)}) %all-to-all-start.3) | async-done | bytes 327712 | tf_op jit(solution)/shard_map/all_to_all | solution.py:163
  (72 shorter events, 12.2 us)
Async XLA Ops:
  0.6 47.7 %copy-start = (bf16[1280,1187]{0,1:T(8,128)(2,1)S(1)}, bf16[1280,1187]{0,1:T(8,128)(2,1)}, u32[]{:S(2)}) copy-start(bf16[1280,1187]{0,1:T(8,128)(2,1)} %param.6) | copy-start | bytes 9116164
  2.4 23.4 %all-to-all-start = ((bf16[32,4,1280]{2,1,0:T(4,128)(2,1)}), bf16[32,4,1280]{2,1,0:T(4,128)(2,1)}, u32[]{:S(2)}, u32[]{:S(2)}) async-start(bf16[32,4,1280]{2,1,0:T(4,128)(2,1)} %bitcast.1), calls=%async_computation | async-start | bytes 655360 | tf_op jit(solution)/shard_map/all_to_all | solution.py:31
  27.9 14.6 %collective-permute-start.2 = (bf16[4,32,1280]{2,1,0:T(8,128)(2,1)}, bf16[4,32,1280]{2,1,0:T(8,128)(2,1)S(1)}, u32[]{:S(2)}, u32[]{:S(2)}) collective-permute-start(bf16[4,32,1280]{2,1,0:T(8,128)(2,1)} %get-tuple-element.15), channel_id=1, source_target_pairs={{0,6},{2,0},{4,2},{6,4},{1,7},{3,1},{5,3},{7,5},{8,14},{10,8},{12,... | collective-permute-start | bytes 983048 | tf_op jit(solution)/shard_map/ppermute | solution.py:33
  30.9 11.8 %collective-permute-start.1 = (bf16[4,32,1280]{2,1,0:T(8,128)(2,1)}, bf16[4,32,1280]{2,1,0:T(8,128)(2,1)}, u32[]{:S(2)}, u32[]{:S(2)}) collective-permute-start(bf16[4,32,1280]{2,1,0:T(8,128)(2,1)} %get-tuple-element.15), channel_id=1, source_target_pairs={{0,4},{2,6},{4,0},{6,2},{1,5},{3,7},{5,1},{7,3},{8,12},{10,14},{12... | collective-permute-start | bytes 983048 | tf_op jit(solution)/shard_map/ppermute | solution.py:33
  31.5 14.6 %collective-permute-start = (bf16[4,32,1280]{2,1,0:T(8,128)(2,1)}, bf16[4,32,1280]{2,1,0:T(8,128)(2,1)}, u32[]{:S(2)}, u32[]{:S(2)}) collective-permute-start(bf16[4,32,1280]{2,1,0:T(8,128)(2,1)} %get-tuple-element.15), channel_id=1, source_target_pairs={{0,2},{2,4},{4,6},{6,0},{1,3},{3,5},{5,7},{7,1},{8,10},{10,12},{12... | collective-permute-start | bytes 983048 | tf_op jit(solution)/shard_map/ppermute | solution.py:33
  35.6 10.5 %copy-start.3 = (bf16[4,256,1280]{2,1,0:T(8,128)(2,1)S(1)}, bf16[4,256,1280]{2,1,0:T(8,128)(2,1)}, u32[]{:S(2)}) copy-start(bf16[4,256,1280]{2,1,0:T(8,128)(2,1)} %get-tuple-element.14) | copy-start | bytes 7864324
  38.5 9.6 %collective-permute-start.3 = (bf16[4,32,1280]{2,1,0:T(8,128)(2,1)}, bf16[4,32,1280]{2,1,0:T(8,128)(2,1)S(1)}, u32[]{:S(2)}, u32[]{:S(2)}) collective-permute-start(bf16[4,32,1280]{2,1,0:T(8,128)(2,1)} %get-tuple-element.15), channel_id=1, source_target_pairs={{0,1},{1,0},{2,3},{3,2},{4,5},{5,4},{6,7},{7,6},{8,9},{9,8},{10,11... | collective-permute-start | bytes 983048 | tf_op jit(solution)/shard_map/ppermute | solution.py:34
  42.4 5.9 %collective-permute-start.6 = (bf16[4,32,1280]{2,1,0:T(8,128)(2,1)S(1)}, bf16[4,32,1280]{2,1,0:T(8,128)(2,1)S(1)}, u32[]{:S(2)}, u32[]{:S(2)}) collective-permute-start(bf16[4,32,1280]{2,1,0:T(8,128)(2,1)S(1)} %collective-permute-done.2), channel_id=1, source_target_pairs={{0,1},{1,0},{2,3},{3,2},{4,5},{5,4},{6,7},{7,6},{8,9},{9,8},{10,11... | collective-permute-start | bytes 983048 | tf_op jit(solution)/shard_map/ppermute | solution.py:34
  42.7 5.5 %collective-permute-start.5 = (bf16[4,32,1280]{2,1,0:T(8,128)(2,1)}, bf16[4,32,1280]{2,1,0:T(8,128)(2,1)S(1)}, u32[]{:S(2)}, u32[]{:S(2)}) collective-permute-start(bf16[4,32,1280]{2,1,0:T(8,128)(2,1)} %collective-permute-done.1), channel_id=1, source_target_pairs={{0,1},{1,0},{2,3},{3,2},{4,5},{5,4},{6,7},{7,6},{8,9},{9,8},{10,11... | collective-permute-start | bytes 983048 | tf_op jit(solution)/shard_map/ppermute | solution.py:34
  46.1 2.1 %collective-permute-start.4 = (bf16[4,32,1280]{2,1,0:T(8,128)(2,1)}, bf16[4,32,1280]{2,1,0:T(8,128)(2,1)S(1)}, u32[]{:S(2)}, u32[]{:S(2)}) collective-permute-start(bf16[4,32,1280]{2,1,0:T(8,128)(2,1)} %collective-permute-done), channel_id=1, source_target_pairs={{0,1},{1,0},{2,3},{3,2},{4,5},{5,4},{6,7},{7,6},{8,9},{9,8},{10,11... | collective-permute-start | bytes 983048 | tf_op jit(solution)/shard_map/ppermute | solution.py:34
  48.3 1.8 copy-start.4
  52.0 44.2 %all-to-all-start.1 = ((bf16[64,4,1190]{2,1,0:T(4,128)(2,1)}), bf16[64,4,1190]{2,1,0:T(4,128)(2,1)}, u32[]{:S(2)}, u32[]{:S(2)}) async-start(bf16[64,4,1190]{2,1,0:T(4,128)(2,1)} %maximum_bitcast_fusion), calls=%async_computation.1 | async-start | bytes 1310720 | tf_op jit(solution)/shard_map/all_to_all | solution.py:60
  61.9 18.5 %collective-permute-start.7 = (f16[1187,256]{1,0:T(8,128)(2,1)}, f16[1187,256]{1,0:T(8,128)(2,1)}, u32[]{:S(2)}, u32[]{:S(2)}) collective-permute-start(f16[1187,256]{1,0:T(8,128)(2,1)} %fusion.3), channel_id=1, source_target_pairs={{0,128},{64,192},{128,0},{192,64},{1,129},{65,193},{129,1},{193,65... | collective-permute-start | bytes 1823240 | tf_op jit(solution)/shard_map/ppermute | solution.py:113
  63.7 27.5 %collective-permute-start.8 = (f16[1187,256]{1,0:T(8,128)(2,1)}, f16[1187,256]{1,0:T(8,128)(2,1)}, u32[]{:S(2)}, u32[]{:S(2)}) collective-permute-start(f16[1187,256]{1,0:T(8,128)(2,1)} %fusion.4), channel_id=1, source_target_pairs={{0,64},{64,128},{128,192},{192,0},{1,65},{65,129},{129,193},{193,1... | collective-permute-start | bytes 1823240 | tf_op jit(solution)/shard_map/ppermute | solution.py:113
  65.3 27.2 %collective-permute-start.9 = (f16[1187,256]{1,0:T(8,128)(2,1)}, f16[1187,256]{1,0:T(8,128)(2,1)}, u32[]{:S(2)}, u32[]{:S(2)}) collective-permute-start(f16[1187,256]{1,0:T(8,128)(2,1)} %fusion.5), channel_id=1, source_target_pairs={{0,192},{64,0},{128,64},{192,128},{1,193},{65,1},{129,65},{193,129... | collective-permute-start | bytes 1823240 | tf_op jit(solution)/shard_map/ppermute | solution.py:113
  98.4 1.7 copy-start.2
  100.0 1.0 copy-start.1
  102.0 23.4 %all-to-all-start.2 = ((f32[64,8,128]{2,1,0:T(8,128)}), f32[64,8,128]{2,1,0:T(8,128)S(1)}, u32[]{:S(2)}, u32[]{:S(2)}) async-start(f32[64,8,128]{2,1,0:T(8,128)} %broadcast_in_dim.11), calls=%async_computation.2 | async-start | bytes 524288 | tf_op jit(solution)/shard_map/all_to_all | solution.py:120
  129.0 30.5 %collective-permute-start.10 = (bf16[1187,256]{1,0:T(8,128)(2,1)}, bf16[1187,256]{1,0:T(8,128)(2,1)}, u32[]{:S(2)}, u32[]{:S(2)}) collective-permute-start(bf16[1187,256]{1,0:T(8,128)(2,1)} %multiply_convert_fusion), channel_id=1, source_target_pairs={{0,192},{64,0},{128,64},{192,128},{1,193},{65,1},{129,65},{193,129... | collective-permute-start | bytes 1823240 | tf_op jit(solution)/shard_map/ppermute | solution.py:141
  129.4 33.7 %collective-permute-start.16 = (bf16[1187,256]{1,0:T(8,128)(2,1)}, bf16[1187,256]{1,0:T(8,128)(2,1)S(1)}, u32[]{:S(2)}, u32[]{:S(2)}) collective-permute-start(bf16[1187,256]{1,0:T(8,128)(2,1)} %multiply_convert_fusion), channel_id=1, source_target_pairs={{0,64},{64,128},{128,192},{192,0},{1,65},{65,129},{129,193},{193,1... | collective-permute-start | bytes 1823240 | tf_op jit(solution)/shard_map/ppermute | solution.py:141
  132.2 29.8 %collective-permute-start.15 = (bf16[1187,256]{1,0:T(8,128)(2,1)}, bf16[1187,256]{1,0:T(8,128)(2,1)S(1)}, u32[]{:S(2)}, u32[]{:S(2)}) collective-permute-start(bf16[1187,256]{1,0:T(8,128)(2,1)} %multiply_convert_fusion), channel_id=1, source_target_pairs={{0,128},{64,192},{128,0},{192,64},{1,129},{65,193},{129,1},{193,65... | collective-permute-start | bytes 1823240 | tf_op jit(solution)/shard_map/ppermute | solution.py:141
  161.7 3.2 %collective-permute-start.11 = (bf16[2,4,32,1280]{3,2,1,0:T(8,128)(2,1)S(1)}, bf16[2,4,32,1280]{3,2,1,0:T(8,128)(2,1)S(1)}, u32[]{:S(2)}, u32[]{:S(2)}) collective-permute-start(bf16[2,4,32,1280]{3,2,1,0:T(8,128)(2,1)S(1)} %fusion.21), channel_id=1, source_target_pairs={{0,1},{1,0},{2,3},{3,2},{4,5},{5,4},{6,7},{7,6},{8,9},{9,8},{10,11... | collective-permute-start | bytes 1966088 | tf_op jit(solution)/shard_map/ppermute | solution.py:153
  162.0 1.1 copy-start.6
  163.1 1.1 copy-start.5
  164.3 4.6 %collective-permute-start.17 = (bf16[2,4,32,1280]{3,2,0,1:T(8,128)(2,1)S(1)}, bf16[2,4,32,1280]{3,2,0,1:T(8,128)(2,1)S(1)}, u32[]{:S(2)}, u32[]{:S(2)}) collective-permute-start(bf16[2,4,32,1280]{3,2,0,1:T(8,128)(2,1)S(1)} %fusion.22), channel_id=1, source_target_pairs={{0,1},{1,0},{2,3},{3,2},{4,5},{5,4},{6,7},{7,6},{8,9},{9,8},{10,11... | collective-permute-start | bytes 1966088 | tf_op jit(solution)/shard_map/ppermute | solution.py:153
  165.1 7.1 %collective-permute-start.12 = (bf16[2,32,1280]{2,1,0:T(8,128)(2,1)S(1)}, bf16[2,32,1280]{2,1,0:T(8,128)(2,1)S(1)}, u32[]{:S(2)}, u32[]{:S(2)}) collective-permute-start(bf16[2,32,1280]{2,1,0:T(8,128)(2,1)S(1)} %get-tuple-element.19), channel_id=1, source_target_pairs={{0,6},{2,0},{4,2},{6,4},{1,7},{3,1},{5,3},{7,5},{8,14},{10,8},{12,... | collective-permute-start | bytes 491528 | tf_op jit(solution)/shard_map/ppermute | solution.py:157
  165.7 9.7 %collective-permute-start.14 = (bf16[2,32,1280]{2,1,0:T(8,128)(2,1)S(1)}, bf16[2,32,1280]{2,1,0:T(8,128)(2,1)S(1)}, u32[]{:S(2)}, u32[]{:S(2)}) collective-permute-start(bf16[2,32,1280]{2,1,0:T(8,128)(2,1)S(1)} %get-tuple-element.20), channel_id=1, source_target_pairs={{0,2},{2,4},{4,6},{6,0},{1,3},{3,5},{5,7},{7,1},{8,10},{10,12},{12... | collective-permute-start | bytes 491528 | tf_op jit(solution)/shard_map/ppermute | solution.py:157
  167.2 10.3 %collective-permute-start.13 = (bf16[2,32,1280]{2,1,0:T(8,128)(2,1)S(1)}, bf16[2,32,1280]{2,1,0:T(8,128)(2,1)S(1)}, u32[]{:S(2)}, u32[]{:S(2)}) collective-permute-start(bf16[2,32,1280]{2,1,0:T(8,128)(2,1)S(1)} %get-tuple-element.21), channel_id=1, source_target_pairs={{0,4},{2,6},{4,0},{6,2},{1,5},{3,7},{5,1},{7,3},{8,12},{10,14},{12... | collective-permute-start | bytes 491528 | tf_op jit(solution)/shard_map/ppermute | solution.py:157
  169.1 10.2 %collective-permute-start.18 = (bf16[2,32,1280]{2,1,0:T(8,128)(2,1)S(1)}, bf16[2,32,1280]{2,1,0:T(8,128)(2,1)S(1)}, u32[]{:S(2)}, u32[]{:S(2)}) collective-permute-start(bf16[2,32,1280]{2,1,0:T(8,128)(2,1)S(1)} %get-tuple-element.16), channel_id=1, source_target_pairs={{0,6},{2,0},{4,2},{6,4},{1,7},{3,1},{5,3},{7,5},{8,14},{10,8},{12,... | collective-permute-start | bytes 491528 | tf_op jit(solution)/shard_map/ppermute | solution.py:157
  170.9 10.2 %collective-permute-start.20 = (bf16[2,32,1280]{2,1,0:T(8,128)(2,1)S(1)}, bf16[2,32,1280]{2,1,0:T(8,128)(2,1)S(1)}, u32[]{:S(2)}, u32[]{:S(2)}) collective-permute-start(bf16[2,32,1280]{2,1,0:T(8,128)(2,1)S(1)} %get-tuple-element.17), channel_id=1, source_target_pairs={{0,2},{2,4},{4,6},{6,0},{1,3},{3,5},{5,7},{7,1},{8,10},{10,12},{12... | collective-permute-start | bytes 491528 | tf_op jit(solution)/shard_map/ppermute | solution.py:157
  172.2 11.1 %collective-permute-start.19 = (bf16[2,32,1280]{2,1,0:T(8,128)(2,1)S(1)}, bf16[2,32,1280]{2,1,0:T(8,128)(2,1)S(1)}, u32[]{:S(2)}, u32[]{:S(2)}) collective-permute-start(bf16[2,32,1280]{2,1,0:T(8,128)(2,1)S(1)} %get-tuple-element.18), channel_id=1, source_target_pairs={{0,4},{2,6},{4,0},{6,2},{1,5},{3,7},{5,1},{7,3},{8,12},{10,14},{12... | collective-permute-start | bytes 491528 | tf_op jit(solution)/shard_map/ppermute | solution.py:157
  184.5 16.8 %all-to-all-start.3 = ((bf16[32,4,1280]{2,1,0:T(4,128)(2,1)}), bf16[32,4,1280]{2,1,0:T(4,128)(2,1)S(1)}, u32[]{:S(2)}, u32[]{:S(2)}) async-start(bf16[32,4,1280]{2,1,0:T(4,128)(2,1)} %reshape.261), calls=%async_computation.3 | async-start | bytes 655360 | tf_op jit(solution)/shard_map/all_to_all | solution.py:163

commit v3 on v2

v3 whole, which is shorter than its diff:
```python
import jax
import jax.numpy as jnp
from jax import lax
from jax.experimental import pallas as pl
from jax.experimental.pallas import tpu as pltpu
from jax.sharding import Mesh, PartitionSpec as P

alpha_power = 0.5
beta_power = 0.25
joint_power = 0.75
smallest = 1e-37
far_below = -1e30

NX, NZ, NY, NC = 4, 8, 4, 2
VOCAB = ("z", "y", "c")
OWN = 4
COLS = 1280
SLICE = 1187
PADDED = 1200
TILE = 240
CHUNK = 80
SPAN = 256
HALF = 128


def shift(count, by):
    return [(i, (i + by) % count) for i in range(count)]


def rolled(value, by):
    count = value.shape[0]
    return lax.dynamic_slice_in_dim(jnp.concatenate([value, value], axis=0), by, count, axis=0)


def gather_hidden(hidden, x, taught):
    pieces = hidden.reshape(OWN, NX, COLS).transpose(1, 0, 2)
    spread = jnp.broadcast_to(pieces[:, None], (NX, NZ, OWN, COLS)).reshape(NX * NZ, OWN, COLS)
    got = lax.all_to_all(spread, ("x", "z"), 0, 0, tiled=True)
    mine = rolled(got.reshape(NX, NZ * OWN, COLS), x)
    mine, taught = lax.optimization_barrier((mine, taught))
    near = [mine] + [lax.ppermute(mine, "y", shift(NY, by)) for by in range(1, NY)]
    far = [lax.ppermute(block, "c", shift(NC, 1)) for block in near]
    return near + far, taught


def order(y, c):
    place = jnp.arange(SPAN)
    core, back, z, own = place // 128, place // 32 % NY, place // OWN % NZ, place % OWN
    true = ((z * NY + (y - back) % NY) * NC + (c + core) % NC) * OWN + own
    return place[:, None] == true[None, :]


def split_three(value):
    high = value.astype(jnp.bfloat16)
    rest = value - high.astype(jnp.float32)
    middle = rest.astype(jnp.bfloat16)
    low = (rest - middle.astype(jnp.float32)).astype(jnp.bfloat16)
    return jnp.stack([high, middle, low], axis=-1)


def teacher_rows(teacher, loss_weight):
    parts = teacher.reshape(OWN, NZ * NY * NC, SLICE)
    weights = jnp.pad(split_three(loss_weight), ((0, 0), (0, PADDED - SLICE - 3)))
    weights = jnp.broadcast_to(weights[:, None], (OWN, NZ * NY * NC, PADDED - SLICE))
    return jnp.concatenate([parts, weights], axis=2).transpose(1, 0, 2)


def gather_teacher(rows, chosen):
    got = lax.all_to_all(rows, VOCAB, 0, 0, tiled=True).reshape(SPAN, PADDED)
    return lax.dot_general(
        got,
        chosen.astype(jnp.bfloat16),
        (((0,), (0,)), ((), ())),
        preferred_element_type=jnp.float32,
    )


def code(value):
    square = value * value
    fourth = square * square
    return (fourth * fourth * value).astype(jnp.bfloat16)


def decode(coded):
    value = coded.astype(jnp.float32)
    size = jnp.abs(value)
    root = jnp.where(size > 1e-36, jnp.exp(jnp.log(jnp.maximum(size, 1e-36)) * (1.0 / 9.0)), 0.0)
    return jnp.where(value < 0.0, -root, root)


def times(left, right):
    return lax.dot_general(
        left, right, (((1,), (1,)), ((), ())), preferred_element_type=jnp.float32
    )


def call(kernel, grid, ins, outs, scratch, flops, moved, *args):
    return pl.pallas_call(
        kernel,
        grid=grid,
        in_specs=ins,
        out_specs=[spec for spec, _ in outs],
        out_shape=[jax.ShapeDtypeStruct(shape, dtype) for _, (shape, dtype) in outs],
        scratch_shapes=scratch,
        cost_estimate=pl.CostEstimate(flops=flops, bytes_accessed=moved, transcendentals=0),
        compiler_params=pltpu.CompilerParams(vmem_limit_bytes=40 * 2**20),
    )(*args)


def whole(*shape):
    return pl.BlockSpec(shape, lambda *_: (0,) * len(shape))


def tiled(width):
    return pl.BlockSpec((TILE, width), lambda i: (i, 0))


BLOCK = (NX, NZ * OWN, COLS)
PIECE = ((PADDED, HALF), jnp.bfloat16)
KEPT = ((PADDED, HALF), jnp.float32)


def relayed_partials(head, blocks):
    def kernel(head_ref, *refs):
        refs, (near_ref, far_ref, rows_ref) = refs[:8], refs[8:]

        @pl.when(pl.program_id(0) == 0)
        def _():
            for at, ref in enumerate(refs):
                rows_ref[32 * at : 32 * at + 32] = ref[0]

        got = times(head_ref[...], rows_ref[...])
        near_ref[...] = code(got[:, :HALF])
        far_ref[...] = code(got[:, HALF:])

    return call(
        kernel,
        (PADDED // TILE,),
        [tiled(COLS)] + [pl.BlockSpec((1, NZ * OWN, COLS), lambda i: (2, 0, 0))] * 8,
        [(tiled(HALF), PIECE), (tiled(HALF), PIECE)],
        [pltpu.VMEM((SPAN, COLS), jnp.bfloat16)],
        2 * PADDED * SPAN * COLS,
        4 * 10**6,
        head,
        *blocks,
    )


def other_partials(head, blocks):
    def kernel(head_ref, *refs):
        refs, (rows_ref, near3_ref, far1_ref, near1_ref, far3_ref, own_ref) = refs[:8], refs[8:]

        @pl.when(pl.program_id(0) == 0)
        def _():
            for at, ref in enumerate(refs):
                rows_ref[:, 32 * at : 32 * at + 32] = ref[...]

        left = head_ref[...]
        got = times(left, rows_ref[3])
        near3_ref[...] = code(got[:, :HALF])
        far3_ref[...] = got[:, HALF:]
        got = times(left, rows_ref[1])
        near1_ref[...] = got[:, :HALF]
        far1_ref[...] = code(got[:, HALF:])
        own_ref[...] = times(left, rows_ref[0])

    return call(
        kernel,
        (PADDED // TILE,),
        [tiled(COLS)] + [whole(*BLOCK)] * 8,
        [(whole(NX, SPAN, COLS), ((NX, SPAN, COLS), jnp.bfloat16))]
        + [(tiled(HALF), PIECE)] * 2
        + [(tiled(HALF), KEPT)] * 2
        + [(tiled(SPAN), ((PADDED, SPAN), jnp.float32))],
        [],
        6 * PADDED * SPAN * COLS,
        12 * 10**6,
        head,
        *blocks,
    )


def added(kept, arrived):
    def kernel(*refs):
        for ours, theirs, out in zip(refs[:2], refs[2:4], refs[4:]):
            out[...] = code(ours[...] + decode(theirs[...]))

    return call(
        kernel,
        (PADDED // TILE,),
        [tiled(HALF)] * 4,
        [(tiled(HALF), PIECE)] * 2,
        [],
        40 * PADDED * SPAN,
        2 * 10**6,
        *kept,
        *arrived,
    )


def chunks(step, start):
    return lax.fori_loop(
        0, PADDED // CHUNK, lambda i, carry: step(pl.ds(pl.multiple_of(i * CHUNK, CHUNK), CHUNK), i, carry), start
    )


def valid(i):
    return lax.broadcasted_iota(jnp.int32, (CHUNK, SPAN), 0) + i * CHUNK < SLICE


def folded(value, join):
    return join(value.reshape(CHUNK // 8, 8, SPAN), axis=0)


def exact(left, right, dims):
    return lax.dot_general(
        left, right, (dims, ((), ())), precision=lax.Precision.HIGHEST, preferred_element_type=jnp.float32
    )


def statistics(own, parts, teacher, chosen):
    def kernel(own_ref, a0, a1, b0, b1, teacher_ref, chosen_ref, logits_ref, sums_ref):
        def first(rows, i, tops):
            arrived = jnp.concatenate(
                [decode(a0[rows, :]) + decode(a1[rows, :]), decode(b0[rows, :]) + decode(b1[rows, :])],
                axis=1,
            )
            student = jnp.where(valid(i), own_ref[rows, :] + arrived, far_below)
            taught = jnp.where(valid(i), teacher_ref[rows, :], far_below)
            logits_ref[rows, :] = student
            return (
                jnp.maximum(tops[0], folded(student, jnp.max)),
                jnp.maximum(tops[1], folded(taught, jnp.max)),
            )

        lowest = jnp.full((8, SPAN), far_below, jnp.float32)
        top_s, top_t = chunks(first, (lowest, lowest))
        top_s = jnp.max(top_s, axis=0, keepdims=True)
        top_t = jnp.max(top_t, axis=0, keepdims=True)

        def second(rows, i, sums):
            s = logits_ref[rows, :] - top_s
            t = jnp.where(valid(i), teacher_ref[rows, :] - top_t, far_below)
            terms = (s, t, alpha_power * t + beta_power * s, joint_power * s)
            return tuple(so_far + folded(jnp.exp(term), jnp.sum) for so_far, term in zip(sums, terms))

        sums = chunks(second, (jnp.zeros((8, SPAN), jnp.float32),) * 4)
        tops = (top_s, top_t, alpha_power * top_t + beta_power * top_s, joint_power * top_s)
        rows = [
            top + jnp.log(jnp.maximum(jnp.sum(total, axis=0, keepdims=True), smallest))
            for top, total in zip(tops, sums)
        ]
        rows = exact(jnp.concatenate(rows + rows, axis=0), chosen_ref[...], ((1,), (1,)))
        packed = jnp.concatenate([rows[:4, :HALF], rows[:4, HALF:]], axis=0)
        sums_ref[...] = jnp.broadcast_to(packed[None], sums_ref.shape)

    logits = ((PADDED, SPAN), jnp.float32)
    sums = ((NZ * NY * NC, 8, HALF), jnp.float32)
    return call(
        kernel,
        (1,),
        [whole(PADDED, SPAN)] + [whole(PADDED, HALF)] * 4 + [whole(PADDED, SPAN), whole(SPAN, SPAN)],
        [(whole(*logits[0]), logits), (whole(*sums[0]), sums)],
        [],
        100 * PADDED * SPAN,
        5 * 10**6,
        own,
        *parts,
        teacher,
        chosen,
    )


def gradients(every, logits, teacher, chosen):
    def kernel(every_ref, logits_ref, teacher_ref, chosen_ref, near_ref, far_ref):
        sums = every_ref[...]
        top = jnp.max(sums, axis=0)
        merged = top + jnp.log(jnp.sum(jnp.exp(sums - top[None]), axis=0))
        merged = jnp.concatenate([merged[:4], merged[4:]], axis=1)
        merged = exact(jnp.concatenate([merged, merged], axis=0), chosen_ref[...], ((1,), (0,)))
        log_s, log_t, log_m, log_j = (merged[k : k + 1] for k in range(4))
        remainder = jnp.exp(log_m - alpha_power * log_t - beta_power * log_s) - jnp.exp(
            log_j - joint_power * log_s
        )
        tail = teacher_ref[SLICE - 3 : SLICE + 5, :]
        weight = -(tail[3:4] + tail[4:5] + tail[5:6]) / alpha_power

        def step(rows, i, carry):
            s = logits_ref[rows, :] - log_s
            t = jnp.where(valid(i), teacher_ref[rows, :] - log_t, far_below)
            got = (
                jnp.exp(alpha_power * t + beta_power * s)
                - jnp.exp(joint_power * s)
                - jnp.exp(s) * remainder
            )
            got = (weight * got).astype(jnp.bfloat16)
            near_ref[rows, :] = got[:, :HALF]
            far_ref[rows, :] = got[:, HALF:]
            return carry

        chunks(step, 0)

    return call(
        kernel,
        (1,),
        [whole(NZ * NY * NC, 8, HALF)] + [whole(PADDED, SPAN)] * 2 + [whole(SPAN, SPAN)],
        [(whole(PADDED, HALF), PIECE)] * 2,
        [],
        60 * PADDED * SPAN,
        4 * 10**6,
        every,
        logits,
        teacher,
        chosen,
    )


def head_gradient(pieces, rows):
    def kernel(*refs):
        left = jnp.concatenate([ref[...] for ref in refs[:8]], axis=1)
        refs[9][...] = jnp.dot(left, refs[8][...], preferred_element_type=jnp.float32).astype(
            jnp.bfloat16
        )

    return call(
        kernel,
        (PADDED // TILE,),
        [tiled(HALF)] * 8 + [whole(NX * SPAN, COLS)],
        [(tiled(COLS), ((SLICE, COLS), jnp.bfloat16))],
        [],
        2 * PADDED * COLS * NX * SPAN,
        9 * 10**6,
        *pieces,
        rows,
    )[0]


def body(hidden, teacher, head_weight, loss_weight):
    x, y, c = lax.axis_index("x"), lax.axis_index("y"), lax.axis_index("c")
    head = jnp.pad(head_weight.T, ((0, PADDED - SLICE), (0, 0)))
    chosen = order(y, c).astype(jnp.float32)
    blocks, taught = gather_hidden(hidden, x, teacher_rows(teacher, loss_weight))

    def sent(value, by):
        return lax.ppermute(value, "x", shift(NX, by))

    relay = relayed_partials(head, blocks)
    relay = [sent(relay[0], 1), sent(relay[1], -1)]
    rows, near3, far1, near1, far3, own = other_partials(head, blocks)
    direct = [sent(near3, -1), sent(far1, 1)]
    summed = added((near1, far3), relay)
    summed = [sent(summed[0], 1), sent(summed[1], -1)]
    taught = gather_teacher(taught, chosen)
    logits, sums = statistics(own, (direct[0], summed[0], direct[1], summed[1]), taught, chosen)
    every = lax.all_to_all(sums, VOCAB, 0, 0, tiled=True)
    near, far = gradients(every, logits, taught, chosen)

    def passed(value, by):
        return lax.ppermute(value, "x", shift(NX, by))

    near = [near, passed(near, -1), None, passed(near, 1)]
    far = [far, passed(far, -1), None, passed(far, 1)]
    near[2], far[2] = passed(near[1], -1), passed(far[3], 1)

    def rows_of(parts, which):
        return jnp.stack(
            [
                lax.dot_general(
                    parts[r], head, (((0,), (0,)), ((), ())), preferred_element_type=jnp.float32
                )
                for r in which
            ]
        ).reshape(len(which), NY, NZ * OWN, COLS)

    def across(which):
        away = lax.ppermute(rows_of(far, which).astype(jnp.bfloat16), "c", shift(NC, 1))
        both = rows_of(near, which) + away.astype(jnp.float32)
        return both[:, 0], [both[:, by].astype(jnp.bfloat16) for by in range(1, NY)]

    def along(others):
        return [lax.ppermute(part, "y", shift(NY, -by)) for by, part in enumerate(others, 1)]

    def shared(mine, others):
        return (mine + sum(part.astype(jnp.float32) for part in others)).astype(jnp.bfloat16)

    mine, others = across((0, 1, 3))
    others = along(others)
    others[0], near[2], far[2] = lax.optimization_barrier((others[0], near[2], far[2]))
    late, far_others = across((2,))
    early, late = shared(mine, others), shared(late, along(far_others))
    early = jnp.concatenate([early[:2], late, early[2:]], axis=0)
    mine = rolled(early, (NX - x) % NX)
    got = lax.all_to_all(mine.reshape(NX * NZ, OWN, COLS), ("x", "z"), 0, 0, tiled=True)
    total = jnp.sum(got.reshape(NX, NZ, OWN, COLS).astype(jnp.float32), axis=1)
    grad_hidden = total.transpose(1, 0, 2).reshape(OWN, NX * COLS).astype(jnp.bfloat16)
    pieces = [part for pair in zip(near, far) for part in pair]
    grad_head = head_gradient(pieces, rows.reshape(NX * SPAN, COLS))
    return grad_hidden, grad_head.T


def solution(mesh):
    fine = Mesh(mesh.devices.reshape(NX, NZ, NY, NC), ("x", "z", "y", "c"))
    every = ("x", "z", "y", "c")
    placed = (P(every, None), P(every, None), P("x", VOCAB), P(every))
    return jax.shard_map(
        body,
        mesh=fine,
        in_specs=placed,
        out_specs=(P(every, None), P("x", VOCAB)),
        check_vma=False,
    )
```

time: 205 us -> 179 us (0.87)
  waiting for transfers between devices: 95.3 us -> 50.8 us
  blocking collectives: 0 us -> 24.4 us
  Pallas kernels: 0 us -> 19.4 us
  matrix products: 26.1 us -> 8.41 us
  other arithmetic: 9.72 us -> 5.92 us
  starting transfers between devices: 56.1 us -> 52.4 us
    ppermute x14 -> x20, waiting for transfers between devices: 61.5 us -> 35.3 us  [the longest x6 15.8 us: passed(): return lax.ppermute(value, 'x', shift(NX, by))]
    all_to_all x0 -> x1, blocking collectives: none -> 24.4 us  [body(): every = lax.all_to_all(sums, VOCAB, 0, 0, tiled=True)]
    pallas_call x0 -> x6, Pallas kernels: none -> 19.4 us  [call(): pl.pallas_call(kernel, grid=grid, in_specs=ins, out_specs=[spec for spec,...]
    dot_general x11 -> x8, matrix products: 24.5 us -> 6.96 us  [rows_of(): lax.dot_general(parts[r], head, (((0,), (0,)), ((), ())), preferred_eleme...]
    all_to_all x2 -> x1, waiting for transfers between devices: 12.1 us -> 0.01 us  [gather_teacher(): got = lax.all_to_all(rows, VOCAB, 0, 0, tiled=True).reshape(SPAN, PADDED)]
    all_to_all x2 -> x1, starting transfers between devices: 17.3 us -> 5.47 us  [gather_teacher(): got = lax.all_to_all(rows, VOCAB, 0, 0, tiled=True).reshape(SPAN, PADDED)]
    ppermute x14 -> x20, starting transfers between devices: 16.2 us -> 21.8 us  [the longest x6 7.78 us: passed(): return lax.ppermute(value, 'x', shift(NX, by))]
    all_to_all x1, waiting for transfers between devices: 11 us -> 6.93 us  [gather_hidden(): got = lax.all_to_all(spread, ('x', 'z'), 0, 0, tiled=True)]
  transfers between devices with their start and end apart: 25 -> 30, of which waited for: 16 -> 16; matrix products, arithmetic and copies ran while one was open for 15% -> 12% of each run, Pallas kernels for 0% -> 9%
where the time goes in v3:
time: 179 us; the launch traced here: 177 us
  starting transfers between devices  52.4 us (29%)
  waiting for transfers between devices  50.8 us (28%)
  blocking collectives  24.4 us (14%)
  Pallas kernels  19.4 us (11%)
  local copies, waits for them, and re-layouts  14.7 us (8%)
  matrix products  8.41 us (5%)
  other arithmetic  5.92 us (3%)
    all_to_all x1, blocking collectives, body(): every = lax.all_to_all(sums, VOCAB, 0, 0, tiled=True)  24.4 us
    pallas_call x6, Pallas kernels, call(): pl.pallas_call(kernel, grid=grid, in_specs=ins, out_specs=[spec for spec,...  19.4 us
    ppermute x6, waiting for transfers between devices, passed(): return lax.ppermute(value, 'x', shift(NX, by))  15.8 us
    all_to_all x1, starting transfers between devices, gather_hidden(): got = lax.all_to_all(spread, ('x', 'z'), 0, 0, tiled=True)  11.6 us
    ppermute x6, waiting for transfers between devices, along(): lax.ppermute(part, 'y', shift(NY, -by))  11 us
    ppermute x6, waiting for transfers between devices, sent(): return lax.ppermute(value, 'x', shift(NX, by))  8.45 us
    ppermute x6, starting transfers between devices, passed(): return lax.ppermute(value, 'x', shift(NX, by))  7.78 us
    ppermute x6, starting transfers between devices, sent(): return lax.ppermute(value, 'x', shift(NX, by))  7.43 us
  transfers between devices with their start and end apart: 30, of which 16 were waited for; matrix products, arithmetic and copies ran while one was open for 12% of the time, Pallas kernels for 9%

profile of v3, /device:TPU:6, one launch (start us, length us, event | category | flops | bytes accessed | tf_op | source)
XLA Modules:
  0.0 177.1 jit_solution(16175953964008852383)
XLA Ops:
  2.3 11.6 %all-to-all-start = ((bf16[32,4,1280]{2,1,0:T(4,128)(2,1)}), bf16[32,4,1280]{2,1,0:T(4,128)(2,1)S(1)}, u32[]{:S(2)}, u32[]{:S(2)}) async-start(bf16[32,4,1280]{2,1,0:T(4,128)(2,1)} %bitcast.2), calls=%async_computation | async-start | bytes 655360 | tf_op jit(solution)/shard_map/all_to_all | solution.py:38
  14.7 2.1 %reshape.195 = bf16[4,64,1187]{2,1,0:T(8,128)(2,1)S(1)} reshape(bf16[4,75968]{1,0:T(4,128)(2,1)} %param.5) | data formatting | bytes 1215488 | tf_op jit(solution)/shard_map/reshape | solution.py:62
  17.4 1.2 maximum_bitcast_fusion
  18.6 6.9 %all-to-all-done = bf16[32,4,1280]{2,1,0:T(4,128)(2,1)S(1)} async-done(((bf16[32,4,1280]{2,1,0:T(4,128)(2,1)}), bf16[32,4,1280]{2,1,0:T(4,128)(2,1)S(1)}, u32[]{:S(2)}, u32[]{:S(2)}) %all-to-all-start) | async-done | bytes 327712 | tf_op jit(solution)/shard_map/all_to_all | solution.py:38
  25.8 1.7 collective-permute-start
  27.4 2.9 %collective-permute-start.1 = (bf16[4,32,1280]{2,1,0:T(8,128)(2,1)S(1)}, bf16[4,32,1280]{2,1,0:T(8,128)(2,1)}, u32[]{:S(2)}, u32[]{:S(2)}) collective-permute-start(bf16[4,32,1280]{2,1,0:T(8,128)(2,1)S(1)} %fusion.2.refs_0_), channel_id=1, source_target_pairs={{0,4},{2,6},{4,0},{6,2},{1,5},{3,7},{5,1},{7,3},{8,12},{10,14},{12... | collective-permute-start | bytes 983048 | tf_op jit(solution)/shard_map/ppermute | solution.py:41
  30.3 1.3 collective-permute-start.2
  31.7 5.5 %all-to-all-start.1 = ((bf16[64,4,1200]{2,1,0:T(4,128)(2,1)}), bf16[64,4,1200]{2,1,0:T(4,128)(2,1)}, u32[]{:S(2)}, u32[]{:S(2)}) async-start(bf16[64,4,1200]{2,1,0:T(4,128)(2,1)} %maximum_bitcast_fusion), calls=%async_computation.1 | async-start | bytes 1310720 | tf_op jit(solution)/shard_map/all_to_all | solution.py:69
  37.8 5.0 %collective-permute-done.1.refs_2_ = bf16[4,32,1280]{2,1,0:T(8,128)(2,1)} collective-permute-done((bf16[4,32,1280]{2,1,0:T(8,128)(2,1)S(1)}, bf16[4,32,1280]{2,1,0:T(8,128)(2,1)}, u32[]{:S(2)}, u32[]{:S(2)}) %collective-permute-start.1) | collective-permute-done | bytes 327712 | tf_op jit(solution)/shard_map/ppermute | solution.py:41
  43.3 2.1 %pad.8.head_ref = bf16[1200,1280]{1,0:T(8,128)(2,1)S(1)} pad(bf16[1187,1280]{1,0:T(8,128)(2,1)} %bitcast.67, bf16[]{:T(256)} %constant.95.clone.1), padding=0_13x0_0 | pad | bytes 6110722 | tf_op jit(solution)/shard_map/jit(_pad)/pad | solution.py:340
  45.4 3.2 %shard_map.60 = (bf16[1200,128]{1,0:T(8,128)(2,1)S(1)}, bf16[1200,128]{1,0:T(8,128)(2,1)S(1)}) custom-call(bf16[1200,1280]{1,0:T(8,128)(2,1)S(1)} %pad.8.head_ref, bf16[4,32,1280]{2,1,0:T(8,128)(2,1)S(1)} %fusion.2.refs_0_, bf16[4,32,1280]{2,1,0:T(8,128)(2,1)} %collective-permute-done.refs_1_, bf16[4,32,1280]{2,1,0:T(8,128)(2,1)} %collective-permute-done.1.refs_2_, ...), custom_call_target="tpu_custom_call" | custom-call | flops 786432000 | bytes 4000000 | tf_op jit(solution)/shard_map/pallas_call | solution.py:98
  48.6 0.9 collective-permute-start.8
  49.5 1.2 collective-permute-start.9
  50.8 6.1 %shard_map.59 = (bf16[4,256,1280]{2,1,0:T(8,128)(2,1)S(1)}, bf16[1200,128]{1,0:T(8,128)(2,1)}, bf16[1200,128]{1,0:T(8,128)(2,1)}, f32[1200,128]{1,0:T(8,128)S(1)...) custom-call(bf16[1200,1280]{1,0:T(8,128)(2,1)S(1)} %pad.8.head_ref, bf16[4,32,1280]{2,1,0:T(8,128)(2,1)S(1)} %fusion.2.refs_0_, ...), custom_call_target="tpu_custom_call" | custom-call | flops 2359296000 | bytes 12000000 | tf_op jit(solution)/shard_map/pallas_call | solution.py:98
  56.9 1.0 copy-done
  57.9 1.5 copy-done.2
  59.4 2.0 %collective-permute-start.11 = (bf16[1200,128]{1,0:T(8,128)(2,1)}, bf16[1200,128]{1,0:T(8,128)(2,1)S(1)}, u32[]{:S(2)}, u32[]{:S(2)}) collective-permute-start(bf16[1200,128]{1,0:T(8,128)(2,1)} %get-tuple-element.29), channel_id=1, source_target_pairs={{0,64},{64,128},{128,192},{192,0},{1,65},{65,129},{129,193},{193,1... | collective-permute-start | bytes 921608 | tf_op jit(solution)/shard_map/ppermute | solution.py:345
  61.5 0.9 shard_map.61
  62.3 3.3 %collective-permute-start.10 = (bf16[1200,128]{1,0:T(8,128)(2,1)S(1)}, bf16[1200,128]{1,0:T(8,128)(2,1)S(1)}, u32[]{:S(2)}, u32[]{:S(2)}) collective-permute-start(bf16[1200,128]{1,0:T(8,128)(2,1)S(1)} %get-tuple-element.28), channel_id=1, source_target_pairs={{0,64},{64,128},{128,192},{192,0},{1,65},{65,129},{129,193},{193,1... | collective-permute-start | bytes 921608 | tf_op jit(solution)/shard_map/ppermute | solution.py:345
  65.7 2.2 %reshape.196 = bf16[256,1200]{1,0:T(8,128)(2,1)} reshape(bf16[64,4,1200]{2,1,0:T(4,128)(2,1)} %all-to-all-done.1) | data formatting | bytes 1228800 | tf_op jit(solution)/shard_map/reshape | solution.py:69
  67.9 1.5 fusion.6.teacher_ref
  69.8 3.2 %collective-permute-done.7.a0 = bf16[1200,128]{1,0:T(8,128)(2,1)S(1)} collective-permute-done((bf16[1200,128]{1,0:T(8,128)(2,1)}, bf16[1200,128]{1,0:T(8,128)(2,1)S(1)}, u32[]{:S(2)}, u32[]{:S(2)}) %collective-permute-start.7) | collective-permute-done | bytes 307232 | tf_op jit(solution)/shard_map/ppermute | solution.py:345
  73.1 1.8 collective-permute-done.10.a1
  74.8 2.9 %collective-permute-done.12.b1 = bf16[1200,128]{1,0:T(8,128)(2,1)S(1)} collective-permute-done((bf16[1200,128]{1,0:T(8,128)(2,1)S(1)}, bf16[1200,128]{1,0:T(8,128)(2,1)S(1)}, u32[]{:S(2)}, u32[]{:S(2)}) %collective-permute-start.12) | collective-permute-done | bytes 307232 | tf_op jit(solution)/shard_map/ppermute | solution.py:345
  77.8 3.0 %shard_map.62 = (f32[1200,256]{1,0:T(8,128)S(1)}, f32[64,8,128]{2,1,0:T(8,128)S(1)}) custom-call(f32[1200,256]{1,0:T(8,128)S(1)} %copy-done.1, bf16[1200,128]{1,0:T(8,128)(2,1)S(1)} %collective-permute-done.7.a0, bf16[1200,128]{1,0:T(8,128)(2,1)S(1)} %collective-permute-done.10.a1, bf16[1200,128]{1,0:T(8,128)(2,1)S(1)} %collective-permute-done.11.b0, ...), custom_call_target="tpu_custom_call" | custom-call | flops 30720000 | bytes 5000000 | tf_op jit(solution)/shard_map/pallas_call | solution.py:98
  80.8 24.4 %all_to_all.20.every_ref = f32[64,8,128]{2,1,0:T(8,128)S(1)} all-to-all(f32[64,8,128]{2,1,0:T(8,128)S(1)} %get-tuple-element.32), channel_id=1, replica_groups=mesh['x'=4,'z'=8,'y'=4,'c'=2] {'z','y','c'}, dimensions={0} | all-to-all | bytes 524288 | tf_op jit(solution)/shard_map/all_to_all | solution.py:355
  105.1 1.2 shard_map.63
  106.5 3.2 %collective-permute-start.16 = (bf16[1200,128]{1,0:T(8,128)(2,1)S(1)}, bf16[1200,128]{1,0:T(8,128)(2,1)S(1)}, u32[]{:S(2)}, u32[]{:S(2)}) collective-permute-start(bf16[1200,128]{1,0:T(8,128)(2,1)S(1)} %get-tuple-element.35.refs_1_), channel_id=1, source_target_pairs={{0,64},{64,128},{128,192},{192,0},{1,65},{65,129},{129,193},{193,1... | collective-permute-start | bytes 921608 | tf_op jit(solution)/shard_map/ppermute | solution.py:359
  110.3 6.8 %collective-permute-done.15.refs_3_ = bf16[1200,128]{1,0:T(8,128)(2,1)S(1)} collective-permute-done((bf16[1200,128]{1,0:T(8,128)(2,1)S(1)}, bf16[1200,128]{1,0:T(8,128)(2,1)S(1)}, u32[]{:S(2)}, u32[]{:S(2)}) %collective-permute-start.15) | collective-permute-done | bytes 307232 | tf_op jit(solution)/shard_map/ppermute | solution.py:359
  118.7 3.2 %collective-permute-start.14 = (bf16[1200,128]{1,0:T(8,128)(2,1)S(1)}, bf16[1200,128]{1,0:T(8,128)(2,1)S(1)}, u32[]{:S(2)}, u32[]{:S(2)}) collective-permute-start(bf16[1200,128]{1,0:T(8,128)(2,1)S(1)} %get-tuple-element.34.refs_0_), channel_id=1, source_target_pairs={{0,64},{64,128},{128,192},{192,0},{1,65},{65,129},{129,193},{193,1... | collective-permute-start | bytes 921608 | tf_op jit(solution)/shard_map/ppermute | solution.py:359
  122.6 1.2 collective-permute-start.20
  123.7 5.8 %collective-permute-done.13.refs_2_ = bf16[1200,128]{1,0:T(8,128)(2,1)S(1)} collective-permute-done((bf16[1200,128]{1,0:T(8,128)(2,1)S(1)}, bf16[1200,128]{1,0:T(8,128)(2,1)S(1)}, u32[]{:S(2)}, u32[]{:S(2)}) %collective-permute-start.13) | collective-permute-done | bytes 307232 | tf_op jit(solution)/shard_map/ppermute | solution.py:359
  130.8 1.6 fusion.38
  133.7 2.2 %collective-permute-start.21 = (bf16[3,32,1280]{2,1,0:T(8,128)(2,1)S(1)}, bf16[3,32,1280]{2,1,0:T(8,128)(2,1)S(1)}, u32[]{:S(2)}, u32[]{:S(2)}) collective-permute-start(bf16[3,32,1280]{2,1,0:T(8,128)(2,1)S(1)} %get-tuple-element.48), channel_id=1, source_target_pairs={{0,4},{2,6},{4,0},{6,2},{1,5},{3,7},{5,1},{7,3},{8,12},{10,14},{12... | collective-permute-start | bytes 737288 | tf_op jit(solution)/shard_map/ppermute | solution.py:381
  136.3 3.2 %collective-permute-done.19.refs_4_ = bf16[1200,128]{1,0:T(8,128)(2,1)S(1)} collective-permute-done((bf16[1200,128]{1,0:T(8,128)(2,1)S(1)}, bf16[1200,128]{1,0:T(8,128)(2,1)S(1)}, u32[]{:S(2)}, u32[]{:S(2)}) %collective-permute-start.19) | collective-permute-done | bytes 307232 | tf_op jit(solution)/shard_map/ppermute | solution.py:359
  139.5 2.7 %collective-permute-done.18 = bf16[3,32,1280]{2,1,0:T(8,128)(2,1)S(1)} collective-permute-done((bf16[3,32,1280]{2,1,0:T(8,128)(2,1)}, bf16[3,32,1280]{2,1,0:T(8,128)(2,1)S(1)}, u32[]{:S(2)}, u32[]{:S(2)}) %collective-permute-start.18) | collective-permute-done | bytes 245792 | tf_op jit(solution)/shard_map/ppermute | solution.py:381
  142.3 2.5 %convolution_convert_fusion = bf16[128,1280]{1,0:T(8,128)(2,1)S(1)} fusion(bf16[1200,128]{1,0:T(8,128)(2,1)S(1)} %collective-permute-done.20.refs_5_, bf16[1187,1280]{1,0:T(8,128)(2,1)} %bitcast.68), kind=kOutput, calls=%fused_computation | convolution fusion | flops 393379840 | bytes 3673600 | tf_op jit(solution)/shard_map/dot_general | solution.py:368
  144.9 2.9 %collective-permute-done.22 = bf16[3,32,1280]{2,1,0:T(8,128)(2,1)} collective-permute-done((bf16[3,32,1280]{2,1,0:T(8,128)(2,1)S(1)}, bf16[3,32,1280]{2,1,0:T(8,128)(2,1)}, u32[]{:S(2)}, u32[]{:S(2)}) %collective-permute-start.22) | collective-permute-done | bytes 245792 | tf_op jit(solution)/shard_map/ppermute | solution.py:381
  147.8 1.2 fusion.1
  149.8 1.1 collective-permute-start.24
  150.9 1.8 %collective-permute-start.25 = (bf16[1,32,1280]{2,1,0:T(8,128)(2,1)S(1)}, bf16[1,32,1280]{2,1,0:T(8,128)(2,1)S(1)}, u32[]{:S(2)}, u32[]{:S(2)}) collective-permute-start(bf16[1,32,1280]{2,1,0:T(8,128)(2,1)S(1)} %get-tuple-element.51), channel_id=1, source_target_pairs={{0,4},{2,6},{4,0},{6,2},{1,5},{3,7},{5,1},{7,3},{8,12},{10,14},{12... | collective-permute-start | bytes 245768 | tf_op jit(solution)/shard_map/ppermute | solution.py:381
  153.1 2.1 %collective-permute-done.24 = bf16[1,32,1280]{2,1,0:T(8,128)(2,1)S(1)} collective-permute-done((bf16[1,32,1280]{2,1,0:T(8,128)(2,1)S(1)}, bf16[1,32,1280]{2,1,0:T(8,128)(2,1)S(1)}, u32[]{:S(2)}, u32[]{:S(2)}) %collective-permute-start.24) | collective-permute-done | bytes 81952 | tf_op jit(solution)/shard_map/ppermute | solution.py:381
  155.1 2.5 %collective-permute-done.25 = bf16[1,32,1280]{2,1,0:T(8,128)(2,1)S(1)} collective-permute-done((bf16[1,32,1280]{2,1,0:T(8,128)(2,1)S(1)}, bf16[1,32,1280]{2,1,0:T(8,128)(2,1)S(1)}, u32[]{:S(2)}, u32[]{:S(2)}) %collective-permute-start.25) | collective-permute-done | bytes 81952 | tf_op jit(solution)/shard_map/ppermute | solution.py:381
  157.6 0.8 collective-permute-done.26
  159.4 6.7 %all-to-all-start.3 = ((bf16[32,4,1280]{2,1,0:T(4,128)(2,1)}), bf16[32,4,1280]{2,1,0:T(4,128)(2,1)S(1)}, u32[]{:S(2)}, u32[]{:S(2)}) async-start(bf16[32,4,1280]{2,1,0:T(4,128)(2,1)} %reshape.197), calls=%async_computation.3 | async-start | bytes 655360 | tf_op jit(solution)/shard_map/all_to_all | solution.py:393
  166.1 1.7 copy-done.3
  167.8 5.0 %shard_map.64 = bf16[1187,1280]{1,0:T(8,128)(2,1)} custom-call(bf16[1200,128]{1,0:T(8,128)(2,1)S(1)} %get-tuple-element.34.refs_0_, bf16[1200,128]{1,0:T(8,128)(2,1)S(1)} %get-tuple-element.35.refs_1_, bf16[1200,128]{1,0:T(8,128)(2,1)S(1)} %collective-permute-done.13.refs_2_, bf16[1200,128]{1,0:T(8,128)(2,1)S(1)} %collective-permute-done.15.refs_3_, ...), custom_call_target="tpu_custom_call" | custom-call | flops 3145728000 | bytes 9000000 | tf_op jit(solution)/shard_map/pallas_call | solution.py:98
  172.8 3.5 %all-to-all-done.3 = bf16[32,4,1280]{2,1,0:T(4,128)(2,1)S(1)} async-done(((bf16[32,4,1280]{2,1,0:T(4,128)(2,1)}), bf16[32,4,1280]{2,1,0:T(4,128)(2,1)S(1)}, u32[]{:S(2)}, u32[]{:S(2)}) %all-to-all-start.3) | async-done | bytes 327712 | tf_op jit(solution)/shard_map/all_to_all | solution.py:393
  (72 shorter events, 13.6 us)
Async XLA Ops:
  2.3 23.3 %all-to-all-start = ((bf16[32,4,1280]{2,1,0:T(4,128)(2,1)}), bf16[32,4,1280]{2,1,0:T(4,128)(2,1)S(1)}, u32[]{:S(2)}, u32[]{:S(2)}) async-start(bf16[32,4,1280]{2,1,0:T(4,128)(2,1)} %bitcast.2), calls=%async_computation | async-start | bytes 655360 | tf_op jit(solution)/shard_map/all_to_all | solution.py:38
  25.8 11.6 %collective-permute-start = (bf16[4,32,1280]{2,1,0:T(8,128)(2,1)S(1)}, bf16[4,32,1280]{2,1,0:T(8,128)(2,1)}, u32[]{:S(2)}, u32[]{:S(2)}) collective-permute-start(bf16[4,32,1280]{2,1,0:T(8,128)(2,1)S(1)} %fusion.2.refs_0_), channel_id=1, source_target_pairs={{0,2},{2,4},{4,6},{6,0},{1,3},{3,5},{5,7},{7,1},{8,10},{10,12},{12... | collective-permute-start | bytes 983048 | tf_op jit(solution)/shard_map/ppermute | solution.py:41
  27.4 15.3 %collective-permute-start.1 = (bf16[4,32,1280]{2,1,0:T(8,128)(2,1)S(1)}, bf16[4,32,1280]{2,1,0:T(8,128)(2,1)}, u32[]{:S(2)}, u32[]{:S(2)}) collective-permute-start(bf16[4,32,1280]{2,1,0:T(8,128)(2,1)S(1)} %fusion.2.refs_0_), channel_id=1, source_target_pairs={{0,4},{2,6},{4,0},{6,2},{1,5},{3,7},{5,1},{7,3},{8,12},{10,14},{12... | collective-permute-start | bytes 983048 | tf_op jit(solution)/shard_map/ppermute | solution.py:41
  30.3 12.5 %collective-permute-start.2 = (bf16[4,32,1280]{2,1,0:T(8,128)(2,1)S(1)}, bf16[4,32,1280]{2,1,0:T(8,128)(2,1)}, u32[]{:S(2)}, u32[]{:S(2)}) collective-permute-start(bf16[4,32,1280]{2,1,0:T(8,128)(2,1)S(1)} %fusion.2.refs_0_), channel_id=1, source_target_pairs={{0,6},{2,0},{4,2},{6,4},{1,7},{3,1},{5,3},{7,5},{8,14},{10,8},{12,... | collective-permute-start | bytes 983048 | tf_op jit(solution)/shard_map/ppermute | solution.py:41
  31.7 34.0 %all-to-all-start.1 = ((bf16[64,4,1200]{2,1,0:T(4,128)(2,1)}), bf16[64,4,1200]{2,1,0:T(4,128)(2,1)}, u32[]{:S(2)}, u32[]{:S(2)}) async-start(bf16[64,4,1200]{2,1,0:T(4,128)(2,1)} %maximum_bitcast_fusion), calls=%async_computation.1 | async-start | bytes 1310720 | tf_op jit(solution)/shard_map/all_to_all | solution.py:69
  37.2 8.2 %collective-permute-start.3 = (bf16[4,32,1280]{2,1,0:T(8,128)(2,1)S(1)}, bf16[4,32,1280]{2,1,0:T(8,128)(2,1)}, u32[]{:S(2)}, u32[]{:S(2)}) collective-permute-start(bf16[4,32,1280]{2,1,0:T(8,128)(2,1)S(1)} %fusion.2.refs_0_), channel_id=1, source_target_pairs={{0,1},{1,0},{2,3},{3,2},{4,5},{5,4},{6,7},{7,6},{8,9},{9,8},{10,11... | collective-permute-start | bytes 983048 | tf_op jit(solution)/shard_map/ppermute | solution.py:42
  37.4 8.0 %collective-permute-start.4 = (bf16[4,32,1280]{2,1,0:T(8,128)(2,1)}, bf16[4,32,1280]{2,1,0:T(8,128)(2,1)}, u32[]{:S(2)}, u32[]{:S(2)}) collective-permute-start(bf16[4,32,1280]{2,1,0:T(8,128)(2,1)} %collective-permute-done.refs_1_), channel_id=1, source_target_pairs={{0,1},{1,0},{2,3},{3,2},{4,5},{5,4},{6,7},{7,6},{8,9},{9,8},{10,11... | collective-permute-start | bytes 983048 | tf_op jit(solution)/shard_map/ppermute | solution.py:42
  42.8 2.6 %collective-permute-start.5 = (bf16[4,32,1280]{2,1,0:T(8,128)(2,1)}, bf16[4,32,1280]{2,1,0:T(8,128)(2,1)}, u32[]{:S(2)}, u32[]{:S(2)}) collective-permute-start(bf16[4,32,1280]{2,1,0:T(8,128)(2,1)} %collective-permute-done.1.refs_2_), channel_id=1, source_target_pairs={{0,1},{1,0},{2,3},{3,2},{4,5},{5,4},{6,7},{7,6},{8,9},{9,8},{10,11... | collective-permute-start | bytes 983048 | tf_op jit(solution)/shard_map/ppermute | solution.py:42
  42.8 2.6 %collective-permute-start.6 = (bf16[4,32,1280]{2,1,0:T(8,128)(2,1)}, bf16[4,32,1280]{2,1,0:T(8,128)(2,1)}, u32[]{:S(2)}, u32[]{:S(2)}) collective-permute-start(bf16[4,32,1280]{2,1,0:T(8,128)(2,1)} %collective-permute-done.2.refs_3_), channel_id=1, source_target_pairs={{0,1},{1,0},{2,3},{3,2},{4,5},{5,4},{6,7},{7,6},{8,9},{9,8},{10,11... | collective-permute-start | bytes 983048 | tf_op jit(solution)/shard_map/ppermute | solution.py:42
  48.6 12.8 %collective-permute-start.8 = (bf16[1200,128]{1,0:T(8,128)(2,1)S(1)}, bf16[1200,128]{1,0:T(8,128)(2,1)S(1)}, u32[]{:S(2)}, u32[]{:S(2)}) collective-permute-start(bf16[1200,128]{1,0:T(8,128)(2,1)S(1)} %get-tuple-element.26), channel_id=1, source_target_pairs={{0,64},{64,128},{128,192},{192,0},{1,65},{65,129},{129,193},{193,1... | collective-permute-start | bytes 921608 | tf_op jit(solution)/shard_map/ppermute | solution.py:345
  49.5 11.9 %collective-permute-start.9 = (bf16[1200,128]{1,0:T(8,128)(2,1)S(1)}, bf16[1200,128]{1,0:T(8,128)(2,1)S(1)}, u32[]{:S(2)}, u32[]{:S(2)}) collective-permute-start(bf16[1200,128]{1,0:T(8,128)(2,1)S(1)} %get-tuple-element.27), channel_id=1, source_target_pairs={{0,192},{64,0},{128,64},{192,128},{1,193},{65,1},{129,65},{193,129... | collective-permute-start | bytes 921608 | tf_op jit(solution)/shard_map/ppermute | solution.py:345
  56.9 1.0 copy-start
  57.9 1.5 copy-start.2
  59.4 18.4 %copy-start.1 = (f32[1200,256]{1,0:T(8,128)S(1)}, f32[1200,256]{1,0:T(8,128)}, u32[]{:S(2)}) copy-start(f32[1200,256]{1,0:T(8,128)} %copy-done) | copy-start | bytes 3686404
  59.4 10.4 %collective-permute-start.11 = (bf16[1200,128]{1,0:T(8,128)(2,1)}, bf16[1200,128]{1,0:T(8,128)(2,1)S(1)}, u32[]{:S(2)}, u32[]{:S(2)}) collective-permute-start(bf16[1200,128]{1,0:T(8,128)(2,1)} %get-tuple-element.29), channel_id=1, source_target_pairs={{0,64},{64,128},{128,192},{192,0},{1,65},{65,129},{129,193},{193,1... | collective-permute-start | bytes 921608 | tf_op jit(solution)/shard_map/ppermute | solution.py:345
  61.4 11.6 %collective-permute-start.7 = (bf16[1200,128]{1,0:T(8,128)(2,1)}, bf16[1200,128]{1,0:T(8,128)(2,1)S(1)}, u32[]{:S(2)}, u32[]{:S(2)}) collective-permute-start(bf16[1200,128]{1,0:T(8,128)(2,1)} %get-tuple-element.23), channel_id=1, source_target_pairs={{0,192},{64,0},{128,64},{192,128},{1,193},{65,1},{129,65},{193,129... | collective-permute-start | bytes 921608 | tf_op jit(solution)/shard_map/ppermute | solution.py:345
  62.3 12.5 %collective-permute-start.10 = (bf16[1200,128]{1,0:T(8,128)(2,1)S(1)}, bf16[1200,128]{1,0:T(8,128)(2,1)S(1)}, u32[]{:S(2)}, u32[]{:S(2)}) collective-permute-start(bf16[1200,128]{1,0:T(8,128)(2,1)S(1)} %get-tuple-element.28), channel_id=1, source_target_pairs={{0,64},{64,128},{128,192},{192,0},{1,65},{65,129},{129,193},{193,1... | collective-permute-start | bytes 921608 | tf_op jit(solution)/shard_map/ppermute | solution.py:345
  65.6 12.2 %collective-permute-start.12 = (bf16[1200,128]{1,0:T(8,128)(2,1)S(1)}, bf16[1200,128]{1,0:T(8,128)(2,1)S(1)}, u32[]{:S(2)}, u32[]{:S(2)}) collective-permute-start(bf16[1200,128]{1,0:T(8,128)(2,1)S(1)} %get-tuple-element.30), channel_id=1, source_target_pairs={{0,192},{64,0},{128,64},{192,128},{1,193},{65,1},{129,65},{193,129... | collective-permute-start | bytes 921608 | tf_op jit(solution)/shard_map/ppermute | solution.py:345
  77.8 31.9 %copy-start.4 = (bf16[1280,1187]{0,1:T(8,128)(2,1)S(1)}, bf16[1280,1187]{0,1:T(8,128)(2,1)}, u32[]{:S(2)}) copy-start(bf16[1280,1187]{0,1:T(8,128)(2,1)} %param.6) | copy-start | bytes 9116164
  106.4 10.7 %collective-permute-start.15 = (bf16[1200,128]{1,0:T(8,128)(2,1)S(1)}, bf16[1200,128]{1,0:T(8,128)(2,1)S(1)}, u32[]{:S(2)}, u32[]{:S(2)}) collective-permute-start(bf16[1200,128]{1,0:T(8,128)(2,1)S(1)} %get-tuple-element.35.refs_1_), channel_id=1, source_target_pairs={{0,192},{64,0},{128,64},{192,128},{1,193},{65,1},{129,65},{193,129... | collective-permute-start | bytes 921608 | tf_op jit(solution)/shard_map/ppermute | solution.py:359
  106.5 11.3 %collective-permute-start.16 = (bf16[1200,128]{1,0:T(8,128)(2,1)S(1)}, bf16[1200,128]{1,0:T(8,128)(2,1)S(1)}, u32[]{:S(2)}, u32[]{:S(2)}) collective-permute-start(bf16[1200,128]{1,0:T(8,128)(2,1)S(1)} %get-tuple-element.35.refs_1_), channel_id=1, source_target_pairs={{0,64},{64,128},{128,192},{192,0},{1,65},{65,129},{129,193},{193,1... | collective-permute-start | bytes 921608 | tf_op jit(solution)/shard_map/ppermute | solution.py:359
  118.5 12.3 %collective-permute-start.17 = (bf16[3,4,32,1280]{3,2,1,0:T(8,128)(2,1)S(1)}, bf16[3,4,32,1280]{3,2,1,0:T(8,128)(2,1)S(1)}, u32[]{:S(2)}, u32[]{:S(2)}) collective-permute-start(bf16[3,4,32,1280]{3,2,1,0:T(8,128)(2,1)S(1)} %pad_maximum_fusion), channel_id=1, source_target_pairs={{0,1},{1,0},{2,3},{3,2},{4,5},{5,4},{6,7},{7,6},{8,9},{9,8},{10,11... | collective-permute-start | bytes 2949128 | tf_op jit(solution)/shard_map/ppermute | solution.py:376
  118.6 10.9 %collective-permute-start.13 = (bf16[1200,128]{1,0:T(8,128)(2,1)S(1)}, bf16[1200,128]{1,0:T(8,128)(2,1)S(1)}, u32[]{:S(2)}, u32[]{:S(2)}) collective-permute-start(bf16[1200,128]{1,0:T(8,128)(2,1)S(1)} %get-tuple-element.34.refs_0_), channel_id=1, source_target_pairs={{0,192},{64,0},{128,64},{192,128},{1,193},{65,1},{129,65},{193,129... | collective-permute-start | bytes 921608 | tf_op jit(solution)/shard_map/ppermute | solution.py:359
  118.7 11.4 %collective-permute-start.14 = (bf16[1200,128]{1,0:T(8,128)(2,1)S(1)}, bf16[1200,128]{1,0:T(8,128)(2,1)S(1)}, u32[]{:S(2)}, u32[]{:S(2)}) collective-permute-start(bf16[1200,128]{1,0:T(8,128)(2,1)S(1)} %get-tuple-element.34.refs_0_), channel_id=1, source_target_pairs={{0,64},{64,128},{128,192},{192,0},{1,65},{65,129},{129,193},{193,1... | collective-permute-start | bytes 921608 | tf_op jit(solution)/shard_map/ppermute | solution.py:359
  122.6 17.0 %collective-permute-start.20 = (bf16[1200,128]{1,0:T(8,128)(2,1)S(1)}, bf16[1200,128]{1,0:T(8,128)(2,1)S(1)}, u32[]{:S(2)}, u32[]{:S(2)}) collective-permute-start(bf16[1200,128]{1,0:T(8,128)(2,1)S(1)} %collective-permute-done.16.refs_7_), channel_id=1, source_target_pairs={{0,64},{64,128},{128,192},{192,0},{1,65},{65,129},{129,193},{193,1... | collective-permute-start | bytes 921608 | tf_op jit(solution)/shard_map/ppermute | solution.py:359
  129.5 10.0 %collective-permute-start.19 = (bf16[1200,128]{1,0:T(8,128)(2,1)S(1)}, bf16[1200,128]{1,0:T(8,128)(2,1)S(1)}, u32[]{:S(2)}, u32[]{:S(2)}) collective-permute-start(bf16[1200,128]{1,0:T(8,128)(2,1)S(1)} %collective-permute-done.13.refs_2_), channel_id=1, source_target_pairs={{0,192},{64,0},{128,64},{192,128},{1,193},{65,1},{129,65},{193,129... | collective-permute-start | bytes 921608 | tf_op jit(solution)/shard_map/ppermute | solution.py:359
  133.2 9.1 %collective-permute-start.18 = (bf16[3,32,1280]{2,1,0:T(8,128)(2,1)}, bf16[3,32,1280]{2,1,0:T(8,128)(2,1)S(1)}, u32[]{:S(2)}, u32[]{:S(2)}) collective-permute-start(bf16[3,32,1280]{2,1,0:T(8,128)(2,1)} %get-tuple-element.46), channel_id=1, source_target_pairs={{0,6},{2,0},{4,2},{6,4},{1,7},{3,1},{5,3},{7,5},{8,14},{10,8},{12,... | collective-permute-start | bytes 737288 | tf_op jit(solution)/shard_map/ppermute | solution.py:381
  133.7 11.1 %collective-permute-start.21 = (bf16[3,32,1280]{2,1,0:T(8,128)(2,1)S(1)}, bf16[3,32,1280]{2,1,0:T(8,128)(2,1)S(1)}, u32[]{:S(2)}, u32[]{:S(2)}) collective-permute-start(bf16[3,32,1280]{2,1,0:T(8,128)(2,1)S(1)} %get-tuple-element.48), channel_id=1, source_target_pairs={{0,4},{2,6},{4,0},{6,2},{1,5},{3,7},{5,1},{7,3},{8,12},{10,14},{12... | collective-permute-start | bytes 737288 | tf_op jit(solution)/shard_map/ppermute | solution.py:381
  136.0 11.9 %collective-permute-start.22 = (bf16[3,32,1280]{2,1,0:T(8,128)(2,1)S(1)}, bf16[3,32,1280]{2,1,0:T(8,128)(2,1)}, u32[]{:S(2)}, u32[]{:S(2)}) collective-permute-start(bf16[3,32,1280]{2,1,0:T(8,128)(2,1)S(1)} %get-tuple-element.47), channel_id=1, source_target_pairs={{0,2},{2,4},{4,6},{6,0},{1,3},{3,5},{5,7},{7,1},{8,10},{10,12},{12... | collective-permute-start | bytes 737288 | tf_op jit(solution)/shard_map/ppermute | solution.py:381
  136.3 12.7 %copy-start.5 = (bf16[1280,1187]{0,1:T(8,128)(2,1)S(1)}, bf16[1280,1187]{0,1:T(8,128)(2,1)}, u32[]{:S(2)}) copy-start(bf16[1280,1187]{0,1:T(8,128)(2,1)} %param.6) | copy-start | bytes 9116164
  144.8 4.9 %collective-permute-start.23 = (bf16[1,4,32,1280]{3,2,1,0:T(8,128)(2,1)S(1)}, bf16[1,4,32,1280]{3,2,1,0:T(8,128)(2,1)S(1)}, u32[]{:S(2)}, u32[]{:S(2)}) collective-permute-start(bf16[1,4,32,1280]{3,2,1,0:T(8,128)(2,1)S(1)} %bitcast.83), channel_id=1, source_target_pairs={{0,1},{1,0},{2,3},{3,2},{4,5},{5,4},{6,7},{7,6},{8,9},{9,8},{10,11... | collective-permute-start | bytes 983048 | tf_op jit(solution)/shard_map/ppermute | solution.py:376
  149.8 5.3 %collective-permute-start.24 = (bf16[1,32,1280]{2,1,0:T(8,128)(2,1)S(1)}, bf16[1,32,1280]{2,1,0:T(8,128)(2,1)S(1)}, u32[]{:S(2)}, u32[]{:S(2)}) collective-permute-start(bf16[1,32,1280]{2,1,0:T(8,128)(2,1)S(1)} %get-tuple-element.49), channel_id=1, source_target_pairs={{0,6},{2,0},{4,2},{6,4},{1,7},{3,1},{5,3},{7,5},{8,14},{10,8},{12,... | collective-permute-start | bytes 245768 | tf_op jit(solution)/shard_map/ppermute | solution.py:381
  150.9 6.7 %collective-permute-start.25 = (bf16[1,32,1280]{2,1,0:T(8,128)(2,1)S(1)}, bf16[1,32,1280]{2,1,0:T(8,128)(2,1)S(1)}, u32[]{:S(2)}, u32[]{:S(2)}) collective-permute-start(bf16[1,32,1280]{2,1,0:T(8,128)(2,1)S(1)} %get-tuple-element.51), channel_id=1, source_target_pairs={{0,4},{2,6},{4,0},{6,2},{1,5},{3,7},{5,1},{7,3},{8,12},{10,14},{12... | collective-permute-start | bytes 245768 | tf_op jit(solution)/shard_map/ppermute | solution.py:381
  152.7 5.7 %collective-permute-start.26 = (bf16[1,32,1280]{2,1,0:T(8,128)(2,1)S(1)}, bf16[1,32,1280]{2,1,0:T(8,128)(2,1)S(1)}, u32[]{:S(2)}, u32[]{:S(2)}) collective-permute-start(bf16[1,32,1280]{2,1,0:T(8,128)(2,1)S(1)} %get-tuple-element.50), channel_id=1, source_target_pairs={{0,2},{2,4},{4,6},{6,0},{1,3},{3,5},{5,7},{7,1},{8,10},{10,12},{12... | collective-permute-start | bytes 245768 | tf_op jit(solution)/shard_map/ppermute | solution.py:381
  159.4 16.9 %all-to-all-start.3 = ((bf16[32,4,1280]{2,1,0:T(4,128)(2,1)}), bf16[32,4,1280]{2,1,0:T(4,128)(2,1)S(1)}, u32[]{:S(2)}, u32[]{:S(2)}) async-start(bf16[32,4,1280]{2,1,0:T(4,128)(2,1)} %reshape.197), calls=%async_computation.3 | async-start | bytes 655360 | tf_op jit(solution)/shard_map/all_to_all | solution.py:393
  166.1 1.7 copy-start.3

commit v4 on v3

--- a/solution.py
+++ b/solution.py
@@ -18,7 +18,8 @@
 SLICE = 1187
 PADDED = 1200
 TILE = 240
-CHUNK = 80
+CHUNK = 240
+LONG = 600
 SPAN = 256
 HALF = 128
 
@@ -32,15 +33,15 @@
     return lax.dynamic_slice_in_dim(jnp.concatenate([value, value], axis=0), by, count, axis=0)
 
 
-def gather_hidden(hidden, x, taught):
+def gather_hidden(hidden, x, *ready):
     pieces = hidden.reshape(OWN, NX, COLS).transpose(1, 0, 2)
     spread = jnp.broadcast_to(pieces[:, None], (NX, NZ, OWN, COLS)).reshape(NX * NZ, OWN, COLS)
     got = lax.all_to_all(spread, ("x", "z"), 0, 0, tiled=True)
     mine = rolled(got.reshape(NX, NZ * OWN, COLS), x)
-    mine, taught = lax.optimization_barrier((mine, taught))
+    mine, *ready = lax.optimization_barrier((mine, *ready))
     near = [mine] + [lax.ppermute(mine, "y", shift(NY, by)) for by in range(1, NY)]
     far = [lax.ppermute(block, "c", shift(NC, 1)) for block in near]
-    return near + far, taught
+    return near + far, *ready
 
 
 def order(y, c):
@@ -84,8 +85,8 @@
 def decode(coded):
     value = coded.astype(jnp.float32)
     size = jnp.abs(value)
-    root = jnp.where(size > 1e-36, jnp.exp(jnp.log(jnp.maximum(size, 1e-36)) * (1.0 / 9.0)), 0.0)
-    return jnp.where(value < 0.0, -root, root)
+    root = jnp.exp2(jnp.log2(jnp.maximum(size, 1e-37)) * (1.0 / 9.0))
+    return jnp.where(value < 0.0, -root, jnp.where(value > 0.0, root, 0.0))
 
 
 def times(left, right):
@@ -94,53 +95,61 @@
     )
 
 
-def call(kernel, grid, ins, outs, scratch, flops, moved, *args):
+def local(kernel, outs, scratch, flops, *args):
+    place = pl.BlockSpec(memory_space=pltpu.VMEM)
     return pl.pallas_call(
         kernel,
-        grid=grid,
-        in_specs=ins,
-        out_specs=[spec for spec, _ in outs],
-        out_shape=[jax.ShapeDtypeStruct(shape, dtype) for _, (shape, dtype) in outs],
+        in_specs=[place] * len(args),
+        out_specs=[place] * len(outs),
+        out_shape=[jax.ShapeDtypeStruct(shape, dtype) for shape, dtype in outs],
         scratch_shapes=scratch,
-        cost_estimate=pl.CostEstimate(flops=flops, bytes_accessed=moved, transcendentals=0),
+        cost_estimate=pl.CostEstimate(flops=flops, bytes_accessed=10**6, transcendentals=0),
+        compiler_params=pltpu.CompilerParams(vmem_limit_bytes=12 * 2**20),
+    )(*args)
+
+
+def whole(shape):
+    return pl.BlockSpec(shape, lambda *_: (0,) * len(shape))
+
+
+def streamed(kernel, outs, flops, *args):
+    return pl.pallas_call(
+        kernel,
+        grid=(1,),
+        in_specs=[whole(arg.shape) for arg in args],
+        out_specs=[whole(shape) for shape, _ in outs],
+        out_shape=[jax.ShapeDtypeStruct(shape, dtype) for shape, dtype in outs],
+        cost_estimate=pl.CostEstimate(flops=flops, bytes_accessed=5 * 10**6, transcendentals=0),
         compiler_params=pltpu.CompilerParams(vmem_limit_bytes=40 * 2**20),
     )(*args)
 
 
-def whole(*shape):
-    return pl.BlockSpec(shape, lambda *_: (0,) * len(shape))
-
-
-def tiled(width):
-    return pl.BlockSpec((TILE, width), lambda i: (i, 0))
-
-
-BLOCK = (NX, NZ * OWN, COLS)
 PIECE = ((PADDED, HALF), jnp.bfloat16)
 KEPT = ((PADDED, HALF), jnp.float32)
+
+
+def chunks(size, step, start):
+    def at(i, carry):
+        return step(pl.ds(pl.multiple_of(i * size, size), size), i, carry)
+
+    return lax.fori_loop(0, PADDED // size, at, start)
 
 
 def relayed_partials(head, blocks):
     def kernel(head_ref, *refs):
         refs, (near_ref, far_ref, rows_ref) = refs[:8], refs[8:]
-
-        @pl.when(pl.program_id(0) == 0)
-        def _():
-            for at, ref in enumerate(refs):
-                rows_ref[32 * at : 32 * at + 32] = ref[0]
+        for at, ref in enumerate(refs):
+            rows_ref[32 * at : 32 * at + 32] = ref[2]
 
         got = times(head_ref[...], rows_ref[...])
         near_ref[...] = code(got[:, :HALF])
         far_ref[...] = code(got[:, HALF:])
 
-    return call(
-        kernel,
-        (PADDED // TILE,),
-        [tiled(COLS)] + [pl.BlockSpec((1, NZ * OWN, COLS), lambda i: (2, 0, 0))] * 8,
-        [(tiled(HALF), PIECE), (tiled(HALF), PIECE)],
+    return local(
+        kernel,
+        [PIECE, PIECE],
         [pltpu.VMEM((SPAN, COLS), jnp.bfloat16)],
         2 * PADDED * SPAN * COLS,
-        4 * 10**6,
         head,
         *blocks,
     )
@@ -148,60 +157,55 @@
 
 def other_partials(head, blocks):
     def kernel(head_ref, *refs):
-        refs, (rows_ref, near3_ref, far1_ref, near1_ref, far3_ref, own_ref) = refs[:8], refs[8:]
-
-        @pl.when(pl.program_id(0) == 0)
-        def _():
-            for at, ref in enumerate(refs):
-                rows_ref[:, 32 * at : 32 * at + 32] = ref[...]
-
-        left = head_ref[...]
-        got = times(left, rows_ref[3])
-        near3_ref[...] = code(got[:, :HALF])
-        far3_ref[...] = got[:, HALF:]
-        got = times(left, rows_ref[1])
-        near1_ref[...] = got[:, :HALF]
-        far1_ref[...] = code(got[:, HALF:])
-        own_ref[...] = times(left, rows_ref[0])
-
-    return call(
-        kernel,
-        (PADDED // TILE,),
-        [tiled(COLS)] + [whole(*BLOCK)] * 8,
-        [(whole(NX, SPAN, COLS), ((NX, SPAN, COLS), jnp.bfloat16))]
-        + [(tiled(HALF), PIECE)] * 2
-        + [(tiled(HALF), KEPT)] * 2
-        + [(tiled(SPAN), ((PADDED, SPAN), jnp.float32))],
-        [],
-        6 * PADDED * SPAN * COLS,
-        12 * 10**6,
-        head,
-        *blocks,
-    )
+        refs, (out_ref, near3_ref, far1_ref, near1_ref, far3_ref, own_ref, rows_ref, done) = (
+            refs[:8],
+            refs[8:],
+        )
+        for at, ref in enumerate(refs):
+            rows_ref[:, 32 * at : 32 * at + 32] = ref[...]
+        copy = pltpu.make_async_copy(rows_ref, out_ref, done)
+        copy.start()
+
+        def step(rows, i, carry):
+            left = head_ref[rows, :]
+            got = times(left, rows_ref[3])
+            near3_ref[rows, :] = code(got[:, :HALF])
+            far3_ref[rows, :] = got[:, HALF:]
+            got = times(left, rows_ref[1])
+            near1_ref[rows, :] = got[:, :HALF]
+            far1_ref[rows, :] = code(got[:, HALF:])
+            own_ref[rows, :] = times(left, rows_ref[0])
+            return carry
+
+        chunks(LONG, step, 0)
+        copy.wait()
+
+    place = pl.BlockSpec(memory_space=pltpu.VMEM)
+    every = ((NX, SPAN, COLS), jnp.bfloat16)
+    outs = [every, PIECE, PIECE, KEPT, KEPT, ((PADDED, SPAN), jnp.float32)]
+    return pl.pallas_call(
+        kernel,
+        in_specs=[place] * 9,
+        out_specs=[pl.BlockSpec(memory_space=pl.ANY)] + [place] * 5,
+        out_shape=[jax.ShapeDtypeStruct(shape, dtype) for shape, dtype in outs],
+        scratch_shapes=[pltpu.VMEM(*every), pltpu.SemaphoreType.DMA],
+        cost_estimate=pl.CostEstimate(
+            flops=6 * PADDED * SPAN * COLS, bytes_accessed=4 * 10**6, transcendentals=0
+        ),
+        compiler_params=pltpu.CompilerParams(vmem_limit_bytes=16 * 2**20),
+    )(head, *blocks)
 
 
 def added(kept, arrived):
     def kernel(*refs):
-        for ours, theirs, out in zip(refs[:2], refs[2:4], refs[4:]):
-            out[...] = code(ours[...] + decode(theirs[...]))
-
-    return call(
-        kernel,
-        (PADDED // TILE,),
-        [tiled(HALF)] * 4,
-        [(tiled(HALF), PIECE)] * 2,
-        [],
-        40 * PADDED * SPAN,
-        2 * 10**6,
-        *kept,
-        *arrived,
-    )
-
-
-def chunks(step, start):
-    return lax.fori_loop(
-        0, PADDED // CHUNK, lambda i, carry: step(pl.ds(pl.multiple_of(i * CHUNK, CHUNK), CHUNK), i, carry), start
-    )
+        def step(rows, i, carry):
+            for ours, theirs, out in zip(refs[:2], refs[2:4], refs[4:]):
+                out[rows, :] = code(ours[rows, :] + decode(theirs[rows, :]))
+            return carry
+
+        chunks(CHUNK, step, 0)
+
+    return local(kernel, [PIECE, PIECE], [], 40 * PADDED * SPAN, *kept, *arrived)
 
 
 def valid(i):
@@ -234,7 +238,7 @@
             )
 
         lowest = jnp.full((8, SPAN), far_below, jnp.float32)
-        top_s, top_t = chunks(first, (lowest, lowest))
+        top_s, top_t = chunks(CHUNK, first, (lowest, lowest))
         top_s = jnp.max(top_s, axis=0, keepdims=True)
         top_t = jnp.max(top_t, axis=0, keepdims=True)
 
@@ -244,7 +248,7 @@
             terms = (s, t, alpha_power * t + beta_power * s, joint_power * s)
             return tuple(so_far + folded(jnp.exp(term), jnp.sum) for so_far, term in zip(sums, terms))
 
-        sums = chunks(second, (jnp.zeros((8, SPAN), jnp.float32),) * 4)
+        sums = chunks(CHUNK, second, (jnp.zeros((8, SPAN), jnp.float32),) * 4)
         tops = (top_s, top_t, alpha_power * top_t + beta_power * top_s, joint_power * top_s)
         rows = [
             top + jnp.log(jnp.maximum(jnp.sum(total, axis=0, keepdims=True), smallest))
@@ -254,16 +258,10 @@
         packed = jnp.concatenate([rows[:4, :HALF], rows[:4, HALF:]], axis=0)
         sums_ref[...] = jnp.broadcast_to(packed[None], sums_ref.shape)
 
-    logits = ((PADDED, SPAN), jnp.float32)
-    sums = ((NZ * NY * NC, 8, HALF), jnp.float32)
-    return call(
-        kernel,
-        (1,),
-        [whole(PADDED, SPAN)] + [whole(PADDED, HALF)] * 4 + [whole(PADDED, SPAN), whole(SPAN, SPAN)],
-        [(whole(*logits[0]), logits), (whole(*sums[0]), sums)],
-        [],
+    return streamed(
+        kernel,
+        [((PADDED, SPAN), jnp.float32), ((NZ * NY * NC, 8, HALF), jnp.float32)],
         100 * PADDED * SPAN,
-        5 * 10**6,
         own,
         *parts,
         teacher,
@@ -298,20 +296,10 @@
             far_ref[rows, :] = got[:, HALF:]
             return carry
 
-        chunks(step, 0)
-
-    return call(
-        kernel,
-        (1,),
-        [whole(NZ * NY * NC, 8, HALF)] + [whole(PADDED, SPAN)] * 2 + [whole(SPAN, SPAN)],
-        [(whole(PADDED, HALF), PIECE)] * 2,
-        [],
-        60 * PADDED * SPAN,
-        4 * 10**6,
-        every,
-        logits,
-        teacher,
-        chosen,
+        chunks(CHUNK, step, 0)
+
+    return streamed(
+        kernel, [PIECE, PIECE], 60 * PADDED * SPAN, every, logits, teacher, chosen
     )
 
 
@@ -322,24 +310,30 @@
             jnp.bfloat16
         )
 
-    return call(
-        kernel,
-        (PADDED // TILE,),
-        [tiled(HALF)] * 8 + [whole(NX * SPAN, COLS)],
-        [(tiled(COLS), ((SLICE, COLS), jnp.bfloat16))],
-        [],
-        2 * PADDED * COLS * NX * SPAN,
-        9 * 10**6,
-        *pieces,
-        rows,
-    )[0]
+    def tiled(width):
+        return pl.BlockSpec((TILE, width), lambda i: (i, 0))
+
+    return pl.pallas_call(
+        kernel,
+        grid=(PADDED // TILE,),
+        in_specs=[tiled(HALF)] * 8 + [pl.BlockSpec((NX * SPAN, COLS), lambda i: (0, 0))],
+        out_specs=tiled(COLS),
+        out_shape=jax.ShapeDtypeStruct((SLICE, COLS), jnp.bfloat16),
+        cost_estimate=pl.CostEstimate(
+            flops=2 * PADDED * COLS * NX * SPAN, bytes_accessed=9 * 10**6, transcendentals=0
+        ),
+        compiler_params=pltpu.CompilerParams(vmem_limit_bytes=20 * 2**20),
+    )(*pieces, rows)
 
 
 def body(hidden, teacher, head_weight, loss_weight):
     x, y, c = lax.axis_index("x"), lax.axis_index("y"), lax.axis_index("c")
     head = jnp.pad(head_weight.T, ((0, PADDED - SLICE), (0, 0)))
     chosen = order(y, c).astype(jnp.float32)
-    blocks, taught = gather_hidden(hidden, x, teacher_rows(teacher, loss_weight))
+    back = lax.rem(NX - x, NX).astype(jnp.uint32)
+    blocks, taught, head, back = gather_hidden(
+        hidden, x, teacher_rows(teacher, loss_weight), head, back
+    )
 
     def sent(value, by):
         return lax.ppermute(value, "x", shift(NX, by))
@@ -383,13 +377,14 @@
     def shared(mine, others):
         return (mine + sum(part.astype(jnp.float32) for part in others)).astype(jnp.bfloat16)
 
-    mine, others = across((0, 1, 3))
-    others = along(others)
-    others[0], near[2], far[2] = lax.optimization_barrier((others[0], near[2], far[2]))
-    late, far_others = across((2,))
-    early, late = shared(mine, others), shared(late, along(far_others))
-    early = jnp.concatenate([early[:2], late, early[2:]], axis=0)
-    mine = rolled(early, (NX - x) % NX)
+    first, others = across((0,))
+    first_others = along(others)
+    first, near[1], far[1] = lax.optimization_barrier((first, near[1], far[1]))
+    first_others, near[2], far[2] = lax.optimization_barrier((first_others, near[2], far[2]))
+    rest, others = across((1, 2, 3))
+    rest = shared(rest, along(others))
+    mine = jnp.concatenate([shared(first, first_others), rest], axis=0)
+    mine = rolled(mine, back)
     got = lax.all_to_all(mine.reshape(NX * NZ, OWN, COLS), ("x", "z"), 0, 0, tiled=True)
     total = jnp.sum(got.reshape(NX, NZ, OWN, COLS).astype(jnp.float32), axis=1)
     grad_hidden = total.transpose(1, 0, 2).reshape(OWN, NX * COLS).astype(jnp.bfloat16)

time: 179 us -> 175 us (0.978)
  waiting for transfers between devices: 50.8 us -> 48.7 us
  matrix products: 8.41 us -> 6.54 us
    ppermute x6, waiting for transfers between devices: 15.8 us -> 11.7 us  [passed(): return lax.ppermute(value, 'x', shift(NX, by))]
    all_to_all x1, waiting for transfers between devices: 6.93 us -> 2.93 us  [gather_hidden(): got = lax.all_to_all(spread, ('x', 'z'), 0, 0, tiled=True)]
    ppermute x6, waiting for transfers between devices: 11 us -> 14.6 us  [along(): lax.ppermute(part, 'y', shift(NY, -by))]
    ppermute x6, starting transfers between devices: 7.78 us -> 5.43 us  [passed(): return lax.ppermute(value, 'x', shift(NX, by))]
    ppermute x4, waiting for transfers between devices: 0.01 us -> 1.92 us  [gather_hidden(): far = [lax.ppermute(block, 'c', shift(NC, 1)) for block in near]]
    dot_general x8, matrix products: 6.96 us -> 5.09 us  [rows_of(): lax.dot_general(parts[r], head, (((0,), (0,)), ((), ())), preferred_eleme...]
    unnamed x17 -> x37, local copies, waits for them, and re-layouts: 4.44 us -> 4.68 us
  transfers between devices with their start and end apart: 30 -> 30, of which waited for: 16 -> 17; matrix products, arithmetic and copies ran while one was open for 12% -> 10% of each run, Pallas kernels for 9% -> 9%
where the time goes in v4:
time: 175 us; the launch traced here: 173 us
  starting transfers between devices  51.2 us (29%)
  waiting for transfers between devices  48.7 us (28%)
  blocking collectives  23.9 us (14%)
  Pallas kernels  19.7 us (11%)
  local copies, waits for them, and re-layouts  15.8 us (9%)
  matrix products  6.54 us (4%)
  other arithmetic  5.78 us (3%)
    all_to_all x1, blocking collectives, body(): every = lax.all_to_all(sums, VOCAB, 0, 0, tiled=True)  23.9 us
    ppermute x6, waiting for transfers between devices, along(): lax.ppermute(part, 'y', shift(NY, -by))  14.6 us
    ppermute x6, waiting for transfers between devices, passed(): return lax.ppermute(value, 'x', shift(NX, by))  11.7 us
    all_to_all x1, starting transfers between devices, gather_hidden(): got = lax.all_to_all(spread, ('x', 'z'), 0, 0, tiled=True)  11.6 us
    ppermute x6, waiting for transfers between devices, sent(): return lax.ppermute(value, 'x', shift(NX, by))  8.07 us
    ppermute x6, starting transfers between devices, along(): lax.ppermute(part, 'y', shift(NY, -by))  7.46 us
    ppermute x6, starting transfers between devices, sent(): return lax.ppermute(value, 'x', shift(NX, by))  7.36 us
    all_to_all x1, starting transfers between devices, body(): lax.all_to_all(mine.reshape(NX * NZ, OWN, COLS), ('x', 'z'), 0, 0, tiled=...  6.8 us
  transfers between devices with their start and end apart: 30, of which 17 were waited for; matrix products, arithmetic and copies ran while one was open for 10% of the time, Pallas kernels for 9%

profile of v4, /device:TPU:6, one launch (start us, length us, event | category | flops | bytes accessed | tf_op | source)
XLA Modules:
  0.0 172.7 jit_solution(3743533368626082807)
XLA Ops:
  2.3 11.6 %all-to-all-start = ((bf16[32,4,1280]{2,1,0:T(4,128)(2,1)}), bf16[32,4,1280]{2,1,0:T(4,128)(2,1)S(1)}, u32[]{:S(2)}, u32[]{:S(2)}) async-start(bf16[32,4,1280]{2,1,0:T(4,128)(2,1)} %bitcast.1), calls=%async_computation | async-start | bytes 655360 | tf_op jit(solution)/shard_map/all_to_all | solution.py:39
  14.7 2.1 %reshape.195 = bf16[4,64,1187]{2,1,0:T(8,128)(2,1)S(1)} reshape(bf16[4,75968]{1,0:T(4,128)(2,1)} %param.5) | data formatting | bytes 1215488 | tf_op jit(solution)/shard_map/reshape | solution.py:63
  16.9 1.3 copy.19
  18.2 2.1 %pad.9.head_ref = bf16[1200,1280]{1,0:T(8,128)(2,1)S(1)} pad(bf16[1187,1280]{1,0:T(8,128)(2,1)} %bitcast.70, bf16[]{:T(256)} %constant.96.clone.1), padding=0_13x0_0 | pad | bytes 6110722 | tf_op jit(solution)/shard_map/jit(_pad)/pad | solution.py:331
  20.3 2.3 %maximum_bitcast_fusion = bf16[64,4,1200]{2,1,0:T(4,128)(2,1)} fusion(bf16[4,64,13]{2,0,1:T(4,128)(2,1)S(1)} %broadcast_in_dim.5, bf16[4,64,1187]{2,0,1:T(4,128)(2,1)} %copy.19), kind=kLoop, calls=%fused_computation.8 | loop fusion | flops 1228800 | bytes 1228800 | tf_op jit(solution)/shard_map/transpose | solution.py:66
  22.6 2.9 %all-to-all-done = bf16[32,4,1280]{2,1,0:T(4,128)(2,1)S(1)} async-done(((bf16[32,4,1280]{2,1,0:T(4,128)(2,1)}), bf16[32,4,1280]{2,1,0:T(4,128)(2,1)S(1)}, u32[]{:S(2)}, u32[]{:S(2)}) %all-to-all-start) | async-done | bytes 327712 | tf_op jit(solution)/shard_map/all_to_all | solution.py:39
  26.3 1.1 fusion.5.refs_0_
  27.5 1.7 collective-permute-start
  29.1 2.9 %collective-permute-start.1 = (bf16[4,32,1280]{2,1,0:T(8,128)(2,1)S(1)}, bf16[4,32,1280]{2,1,0:T(8,128)(2,1)}, u32[]{:S(2)}, u32[]{:S(2)}) collective-permute-start(bf16[4,32,1280]{2,1,0:T(8,128)(2,1)S(1)} %fusion.5.refs_0_), channel_id=1, source_target_pairs={{0,4},{2,6},{4,0},{6,2},{1,5},{3,7},{5,1},{7,3},{8,12},{10,14},{12... | collective-permute-start | bytes 983048 | tf_op jit(solution)/shard_map/ppermute | solution.py:42
  32.0 1.3 collective-permute-start.2
  33.4 5.5 %all-to-all-start.1 = ((bf16[64,4,1200]{2,1,0:T(4,128)(2,1)}), bf16[64,4,1200]{2,1,0:T(4,128)(2,1)}, u32[]{:S(2)}, u32[]{:S(2)}) async-start(bf16[64,4,1200]{2,1,0:T(4,128)(2,1)} %maximum_bitcast_fusion), calls=%async_computation.1 | async-start | bytes 1310720 | tf_op jit(solution)/shard_map/all_to_all | solution.py:70
  39.4 5.0 %collective-permute-done.1.refs_2_ = bf16[4,32,1280]{2,1,0:T(8,128)(2,1)} collective-permute-done((bf16[4,32,1280]{2,1,0:T(8,128)(2,1)S(1)}, bf16[4,32,1280]{2,1,0:T(8,128)(2,1)}, u32[]{:S(2)}, u32[]{:S(2)}) %collective-permute-start.1) | collective-permute-done | bytes 327712 | tf_op jit(solution)/shard_map/ppermute | solution.py:42
  45.0 1.5 collective-permute-done.5.refs_6_
  46.9 2.6 %shard_map.60 = (bf16[1200,128]{1,0:T(8,128)(2,1)S(1)}, bf16[1200,128]{1,0:T(8,128)(2,1)S(1)}) custom-call(bf16[1200,1280]{1,0:T(8,128)(2,1)S(1)} %pad.9.head_ref, bf16[4,32,1280]{2,1,0:T(8,128)(2,1)S(1)} %fusion.5.refs_0_, bf16[4,32,1280]{2,1,0:T(8,128)(2,1)} %collective-permute-done.refs_1_, bf16[4,32,1280]{2,1,0:T(8,128)(2,1)} %collective-permute-done.1.refs_2_, ...), custom_call_target="tpu_custom_call" | custom-call | flops 786432000 | bytes 1000000 | tf_op jit(solution)/shard_map/pallas_call | solution.py:100
  49.5 0.9 collective-permute-start.8
  50.4 1.2 collective-permute-start.9
  51.6 5.6 %shard_map.59 = (bf16[4,256,1280]{2,1,0:T(8,128)(2,1)S(1)}, bf16[1200,128]{1,0:T(8,128)(2,1)}, bf16[1200,128]{1,0:T(8,128)(2,1)}, f32[1200,128]{1,0:T(8,128)S(1)...) custom-call(bf16[1200,1280]{1,0:T(8,128)(2,1)S(1)} %pad.9.head_ref, bf16[4,32,1280]{2,1,0:T(8,128)(2,1)S(1)} %fusion.5.refs_0_, ...), custom_call_target="tpu_custom_call" | custom-call | flops 2359296000 | bytes 4000000 | tf_op jit(solution)/shard_map/pallas_call | solution.py:186
  57.2 1.5 copy-done.16
  58.7 2.0 %collective-permute-start.11 = (bf16[1200,128]{1,0:T(8,128)(2,1)}, bf16[1200,128]{1,0:T(8,128)(2,1)}, u32[]{:S(2)}, u32[]{:S(2)}) collective-permute-start(bf16[1200,128]{1,0:T(8,128)(2,1)} %get-tuple-element.37), channel_id=1, source_target_pairs={{0,64},{64,128},{128,192},{192,0},{1,65},{65,129},{129,193},{193,1... | collective-permute-start | bytes 921608 | tf_op jit(solution)/shard_map/ppermute | solution.py:339
  60.8 1.5 shard_map.61
  62.3 3.2 %collective-permute-start.10 = (bf16[1200,128]{1,0:T(8,128)(2,1)}, bf16[1200,128]{1,0:T(8,128)(2,1)}, u32[]{:S(2)}, u32[]{:S(2)}) collective-permute-start(bf16[1200,128]{1,0:T(8,128)(2,1)} %get-tuple-element.36), channel_id=1, source_target_pairs={{0,64},{64,128},{128,192},{192,0},{1,65},{65,129},{129,193},{193,1... | collective-permute-start | bytes 921608 | tf_op jit(solution)/shard_map/ppermute | solution.py:339
  65.6 2.2 %reshape.196 = bf16[256,1200]{1,0:T(8,128)(2,1)} reshape(bf16[64,4,1200]{2,1,0:T(4,128)(2,1)} %all-to-all-done.1) | data formatting | bytes 1228800 | tf_op jit(solution)/shard_map/reshape | solution.py:70
  67.8 1.5 fusion.7.teacher_ref
  69.3 3.2 %collective-permute-done.7.a0 = bf16[1200,128]{1,0:T(8,128)(2,1)} collective-permute-done((bf16[1200,128]{1,0:T(8,128)(2,1)}, bf16[1200,128]{1,0:T(8,128)(2,1)}, u32[]{:S(2)}, u32[]{:S(2)}) %collective-permute-start.7) | collective-permute-done | bytes 307232 | tf_op jit(solution)/shard_map/ppermute | solution.py:339
  72.5 1.9 %collective-permute-done.10.a1 = bf16[1200,128]{1,0:T(8,128)(2,1)} collective-permute-done((bf16[1200,128]{1,0:T(8,128)(2,1)}, bf16[1200,128]{1,0:T(8,128)(2,1)}, u32[]{:S(2)}, u32[]{:S(2)}) %collective-permute-start.10) | collective-permute-done | bytes 307232 | tf_op jit(solution)/shard_map/ppermute | solution.py:339
  74.4 3.0 %collective-permute-done.12.b1 = bf16[1200,128]{1,0:T(8,128)(2,1)} collective-permute-done((bf16[1200,128]{1,0:T(8,128)(2,1)}, bf16[1200,128]{1,0:T(8,128)(2,1)}, u32[]{:S(2)}, u32[]{:S(2)}) %collective-permute-start.12) | collective-permute-done | bytes 307232 | tf_op jit(solution)/shard_map/ppermute | solution.py:339
  77.3 1.3 copy-done.1
  78.6 3.8 %shard_map.62 = (f32[1200,256]{1,0:T(8,128)S(1)}, f32[64,8,128]{2,1,0:T(8,128)S(1)}) custom-call(f32[1200,256]{1,0:T(8,128)S(1)} %copy-done.1, bf16[1200,128]{1,0:T(8,128)(2,1)} %collective-permute-done.7.a0, bf16[1200,128]{1,0:T(8,128)(2,1)} %collective-permute-done.10.a1, bf16[1200,128]{1,0:T(8,128)(2,1)} %collective-permute-done.11.b0, ...), custom_call_target="tpu_custom_call" | custom-call | flops 30720000 | bytes 5000000 | tf_op jit(solution)/shard_map/pallas_call | solution.py:116
  82.4 23.9 %all_to_all.20.every_ref = f32[64,8,128]{2,1,0:T(8,128)S(1)} all-to-all(f32[64,8,128]{2,1,0:T(8,128)S(1)} %get-tuple-element.40), channel_id=1, replica_groups=mesh['x'=4,'z'=8,'y'=4,'c'=2] {'z','y','c'}, dimensions={0} | all-to-all | bytes 524288 | tf_op jit(solution)/shard_map/all_to_all | solution.py:349
  106.3 1.2 shard_map.63
  108.6 1.7 collective-permute-start.14
  111.0 8.9 %collective-permute-done.14.refs_2_ = bf16[1200,128]{1,0:T(8,128)(2,1)S(1)} collective-permute-done((bf16[1200,128]{1,0:T(8,128)(2,1)S(1)}, bf16[1200,128]{1,0:T(8,128)(2,1)S(1)}, u32[]{:S(2)}, u32[]{:S(2)}) %collective-permute-start.14) | collective-permute-done | bytes 307232 | tf_op jit(solution)/shard_map/ppermute | solution.py:353
  120.3 2.8 %collective-permute-start.21 = (bf16[1200,128]{1,0:T(8,128)(2,1)S(1)}, bf16[1200,128]{1,0:T(8,128)(2,1)S(1)}, u32[]{:S(2)}, u32[]{:S(2)}) collective-permute-start(bf16[1200,128]{1,0:T(8,128)(2,1)S(1)} %collective-permute-done.20.refs_7_), channel_id=1, source_target_pairs={{0,64},{64,128},{128,192},{192,0},{1,65},{65,129},{129,193},{193,1... | collective-permute-start | bytes 921608 | tf_op jit(solution)/shard_map/ppermute | solution.py:353
  123.9 1.8 %collective-permute-start.16 = (bf16[1,32,1280]{2,1,0:T(8,128)(2,1)S(1)}, bf16[1,32,1280]{2,1,0:T(8,128)(2,1)S(1)}, u32[]{:S(2)}, u32[]{:S(2)}) collective-permute-start(bf16[1,32,1280]{2,1,0:T(8,128)(2,1)S(1)} %get-tuple-element.63), channel_id=1, source_target_pairs={{0,6},{2,0},{4,2},{6,4},{1,7},{3,1},{5,3},{7,5},{8,14},{10,8},{12,... | collective-permute-start | bytes 245768 | tf_op jit(solution)/shard_map/ppermute | solution.py:375
  125.7 1.1 collective-permute-start.17
  128.5 3.1 %collective-permute-done.17 = bf16[1,32,1280]{2,1,0:T(8,128)(2,1)S(1)} collective-permute-done((bf16[1,32,1280]{2,1,0:T(8,128)(2,1)S(1)}, bf16[1,32,1280]{2,1,0:T(8,128)(2,1)S(1)}, u32[]{:S(2)}, u32[]{:S(2)}) %collective-permute-start.17) | collective-permute-done | bytes 81952 | tf_op jit(solution)/shard_map/ppermute | solution.py:375
  131.6 0.9 collective-permute-done.18
  133.4 2.7 %collective-permute-done.22.refs_6_ = bf16[1200,128]{1,0:T(8,128)(2,1)S(1)} collective-permute-done((bf16[1200,128]{1,0:T(8,128)(2,1)S(1)}, bf16[1200,128]{1,0:T(8,128)(2,1)S(1)}, u32[]{:S(2)}, u32[]{:S(2)}) %collective-permute-start.22) | collective-permute-done | bytes 307232 | tf_op jit(solution)/shard_map/ppermute | solution.py:353
  138.6 2.4 %collective-permute-start.24 = (bf16[3,32,1280]{2,1,0:T(8,128)(2,1)S(1)}, bf16[3,32,1280]{2,1,0:T(8,128)(2,1)S(1)}, u32[]{:S(2)}, u32[]{:S(2)}) collective-permute-start(bf16[3,32,1280]{2,1,0:T(8,128)(2,1)S(1)} %get-tuple-element.58), channel_id=1, source_target_pairs={{0,6},{2,0},{4,2},{6,4},{1,7},{3,1},{5,3},{7,5},{8,14},{10,8},{12,... | collective-permute-start | bytes 737288 | tf_op jit(solution)/shard_map/ppermute | solution.py:375
  141.0 0.9 collective-permute-start.25
  142.5 6.7 %collective-permute-done.24 = bf16[3,32,1280]{2,1,0:T(8,128)(2,1)S(1)} collective-permute-done((bf16[3,32,1280]{2,1,0:T(8,128)(2,1)S(1)}, bf16[3,32,1280]{2,1,0:T(8,128)(2,1)S(1)}, u32[]{:S(2)}, u32[]{:S(2)}) %collective-permute-start.24) | collective-permute-done | bytes 245792 | tf_op jit(solution)/shard_map/ppermute | solution.py:375
  149.2 1.1 collective-permute-done.25
  150.3 2.5 %collective-permute-done.26 = bf16[3,32,1280]{2,1,0:T(8,128)(2,1)S(1)} collective-permute-done((bf16[3,32,1280]{2,1,0:T(8,128)(2,1)S(1)}, bf16[3,32,1280]{2,1,0:T(8,128)(2,1)S(1)}, u32[]{:S(2)}, u32[]{:S(2)}) %collective-permute-start.26) | collective-permute-done | bytes 245792 | tf_op jit(solution)/shard_map/ppermute | solution.py:375
  153.1 0.8 reshape.197
  153.9 6.8 %all-to-all-start.3 = ((bf16[32,4,1280]{2,1,0:T(4,128)(2,1)}), bf16[32,4,1280]{2,1,0:T(4,128)(2,1)S(1)}, u32[]{:S(2)}, u32[]{:S(2)}) async-start(bf16[32,4,1280]{2,1,0:T(4,128)(2,1)} %reshape.197), calls=%async_computation.3 | async-start | bytes 655360 | tf_op jit(solution)/shard_map/all_to_all | solution.py:388
  160.8 1.7 %copy-done.17 = bf16[4,256,1280]{2,1,0:T(8,128)(2,1)S(1)} copy-done((bf16[4,256,1280]{2,1,0:T(8,128)(2,1)S(1)}, bf16[4,256,1280]{2,1,0:T(8,128)(2,1)}, u32[]{:S(2)}) %copy-start.17) | copy-done | bytes 2621464
  162.5 5.0 %shard_map.64 = bf16[1187,1280]{1,0:T(8,128)(2,1)} custom-call(bf16[1200,128]{1,0:T(8,128)(2,1)S(1)} %copy-done.3, bf16[1200,128]{1,0:T(8,128)(2,1)S(1)} %copy-done.5, bf16[1200,128]{1,0:T(8,128)(2,1)S(1)} %copy-done.7, bf16[1200,128]{1,0:T(8,128)(2,1)S(1)} %copy-done.9, bf16[1200,128]{1,0:T(8,128)(2,1)S(1)} %copy-done.11, bf16[1200,128]{1,0:T(8,128)(2,1)S(1)} %copy-done.13, ...), custom_call_target="tpu_custom_call" | custom-call | flops 3145728000 | bytes 9000000 | tf_op jit(solution)/shard_map/pallas_call | solution.py:316
  167.6 4.4 %all-to-all-done.3 = bf16[32,4,1280]{2,1,0:T(4,128)(2,1)S(1)} async-done(((bf16[32,4,1280]{2,1,0:T(4,128)(2,1)}), bf16[32,4,1280]{2,1,0:T(4,128)(2,1)S(1)}, u32[]{:S(2)}, u32[]{:S(2)}) %all-to-all-start.3) | async-done | bytes 327712 | tf_op jit(solution)/shard_map/all_to_all | solution.py:388
  (92 shorter events, 14.5 us)
Async XLA Ops:
  2.3 23.3 %all-to-all-start = ((bf16[32,4,1280]{2,1,0:T(4,128)(2,1)}), bf16[32,4,1280]{2,1,0:T(4,128)(2,1)S(1)}, u32[]{:S(2)}, u32[]{:S(2)}) async-start(bf16[32,4,1280]{2,1,0:T(4,128)(2,1)} %bitcast.1), calls=%async_computation | async-start | bytes 655360 | tf_op jit(solution)/shard_map/all_to_all | solution.py:39
  27.5 11.6 %collective-permute-start = (bf16[4,32,1280]{2,1,0:T(8,128)(2,1)S(1)}, bf16[4,32,1280]{2,1,0:T(8,128)(2,1)}, u32[]{:S(2)}, u32[]{:S(2)}) collective-permute-start(bf16[4,32,1280]{2,1,0:T(8,128)(2,1)S(1)} %fusion.5.refs_0_), channel_id=1, source_target_pairs={{0,2},{2,4},{4,6},{6,0},{1,3},{3,5},{5,7},{7,1},{8,10},{10,12},{12... | collective-permute-start | bytes 983048 | tf_op jit(solution)/shard_map/ppermute | solution.py:42
  29.1 15.3 %collective-permute-start.1 = (bf16[4,32,1280]{2,1,0:T(8,128)(2,1)S(1)}, bf16[4,32,1280]{2,1,0:T(8,128)(2,1)}, u32[]{:S(2)}, u32[]{:S(2)}) collective-permute-start(bf16[4,32,1280]{2,1,0:T(8,128)(2,1)S(1)} %fusion.5.refs_0_), channel_id=1, source_target_pairs={{0,4},{2,6},{4,0},{6,2},{1,5},{3,7},{5,1},{7,3},{8,12},{10,14},{12... | collective-permute-start | bytes 983048 | tf_op jit(solution)/shard_map/ppermute | solution.py:42
  32.0 12.5 %collective-permute-start.2 = (bf16[4,32,1280]{2,1,0:T(8,128)(2,1)S(1)}, bf16[4,32,1280]{2,1,0:T(8,128)(2,1)}, u32[]{:S(2)}, u32[]{:S(2)}) collective-permute-start(bf16[4,32,1280]{2,1,0:T(8,128)(2,1)S(1)} %fusion.5.refs_0_), channel_id=1, source_target_pairs={{0,6},{2,0},{4,2},{6,4},{1,7},{3,1},{5,3},{7,5},{8,14},{10,8},{12,... | collective-permute-start | bytes 983048 | tf_op jit(solution)/shard_map/ppermute | solution.py:42
  33.4 32.2 %all-to-all-start.1 = ((bf16[64,4,1200]{2,1,0:T(4,128)(2,1)}), bf16[64,4,1200]{2,1,0:T(4,128)(2,1)}, u32[]{:S(2)}, u32[]{:S(2)}) async-start(bf16[64,4,1200]{2,1,0:T(4,128)(2,1)} %maximum_bitcast_fusion), calls=%async_computation.1 | async-start | bytes 1310720 | tf_op jit(solution)/shard_map/all_to_all | solution.py:70
  38.8 6.1 %collective-permute-start.3 = (bf16[4,32,1280]{2,1,0:T(8,128)(2,1)S(1)}, bf16[4,32,1280]{2,1,0:T(8,128)(2,1)}, u32[]{:S(2)}, u32[]{:S(2)}) collective-permute-start(bf16[4,32,1280]{2,1,0:T(8,128)(2,1)S(1)} %fusion.5.refs_0_), channel_id=1, source_target_pairs={{0,1},{1,0},{2,3},{3,2},{4,5},{5,4},{6,7},{7,6},{8,9},{9,8},{10,11... | collective-permute-start | bytes 983048 | tf_op jit(solution)/shard_map/ppermute | solution.py:43
  39.0 5.9 %collective-permute-start.4 = (bf16[4,32,1280]{2,1,0:T(8,128)(2,1)}, bf16[4,32,1280]{2,1,0:T(8,128)(2,1)}, u32[]{:S(2)}, u32[]{:S(2)}) collective-permute-start(bf16[4,32,1280]{2,1,0:T(8,128)(2,1)} %collective-permute-done.refs_1_), channel_id=1, source_target_pairs={{0,1},{1,0},{2,3},{3,2},{4,5},{5,4},{6,7},{7,6},{8,9},{9,8},{10,11... | collective-permute-start | bytes 983048 | tf_op jit(solution)/shard_map/ppermute | solution.py:43
  44.5 2.0 %collective-permute-start.5 = (bf16[4,32,1280]{2,1,0:T(8,128)(2,1)}, bf16[4,32,1280]{2,1,0:T(8,128)(2,1)}, u32[]{:S(2)}, u32[]{:S(2)}) collective-permute-start(bf16[4,32,1280]{2,1,0:T(8,128)(2,1)} %collective-permute-done.1.refs_2_), channel_id=1, source_target_pairs={{0,1},{1,0},{2,3},{3,2},{4,5},{5,4},{6,7},{7,6},{8,9},{9,8},{10,11... | collective-permute-start | bytes 983048 | tf_op jit(solution)/shard_map/ppermute | solution.py:43
  44.5 2.4 %collective-permute-start.6 = (bf16[4,32,1280]{2,1,0:T(8,128)(2,1)}, bf16[4,32,1280]{2,1,0:T(8,128)(2,1)}, u32[]{:S(2)}, u32[]{:S(2)}) collective-permute-start(bf16[4,32,1280]{2,1,0:T(8,128)(2,1)} %collective-permute-done.2.refs_3_), channel_id=1, source_target_pairs={{0,1},{1,0},{2,3},{3,2},{4,5},{5,4},{6,7},{7,6},{8,9},{9,8},{10,11... | collective-permute-start | bytes 983048 | tf_op jit(solution)/shard_map/ppermute | solution.py:43
  49.5 11.3 %collective-permute-start.8 = (bf16[1200,128]{1,0:T(8,128)(2,1)S(1)}, bf16[1200,128]{1,0:T(8,128)(2,1)S(1)}, u32[]{:S(2)}, u32[]{:S(2)}) collective-permute-start(bf16[1200,128]{1,0:T(8,128)(2,1)S(1)} %get-tuple-element.34), channel_id=1, source_target_pairs={{0,64},{64,128},{128,192},{192,0},{1,65},{65,129},{129,193},{193,1... | collective-permute-start | bytes 921608 | tf_op jit(solution)/shard_map/ppermute | solution.py:339
  50.4 10.4 %collective-permute-start.9 = (bf16[1200,128]{1,0:T(8,128)(2,1)S(1)}, bf16[1200,128]{1,0:T(8,128)(2,1)S(1)}, u32[]{:S(2)}, u32[]{:S(2)}) collective-permute-start(bf16[1200,128]{1,0:T(8,128)(2,1)S(1)} %get-tuple-element.35), channel_id=1, source_target_pairs={{0,192},{64,0},{128,64},{192,128},{1,193},{65,1},{129,65},{193,129... | collective-permute-start | bytes 921608 | tf_op jit(solution)/shard_map/ppermute | solution.py:339
  57.2 1.5 copy-start.16
  58.7 6.8 %copy-start = (f32[1200,256]{1,0:T(8,128)}, f32[1200,256]{1,0:T(8,128)S(1)}, u32[]{:S(2)}) copy-start(f32[1200,256]{1,0:T(8,128)S(1)} %get-tuple-element.30.own_ref) | copy-start | bytes 3686404
  58.7 10.5 %collective-permute-start.11 = (bf16[1200,128]{1,0:T(8,128)(2,1)}, bf16[1200,128]{1,0:T(8,128)(2,1)}, u32[]{:S(2)}, u32[]{:S(2)}) collective-permute-start(bf16[1200,128]{1,0:T(8,128)(2,1)} %get-tuple-element.37), channel_id=1, source_target_pairs={{0,64},{64,128},{128,192},{192,0},{1,65},{65,129},{129,193},{193,1... | collective-permute-start | bytes 921608 | tf_op jit(solution)/shard_map/ppermute | solution.py:339
  60.7 11.7 %collective-permute-start.7 = (bf16[1200,128]{1,0:T(8,128)(2,1)}, bf16[1200,128]{1,0:T(8,128)(2,1)}, u32[]{:S(2)}, u32[]{:S(2)}) collective-permute-start(bf16[1200,128]{1,0:T(8,128)(2,1)} %get-tuple-element.31), channel_id=1, source_target_pairs={{0,192},{64,0},{128,64},{192,128},{1,193},{65,1},{129,65},{193,129... | collective-permute-start | bytes 921608 | tf_op jit(solution)/shard_map/ppermute | solution.py:339
  62.3 12.1 %collective-permute-start.10 = (bf16[1200,128]{1,0:T(8,128)(2,1)}, bf16[1200,128]{1,0:T(8,128)(2,1)}, u32[]{:S(2)}, u32[]{:S(2)}) collective-permute-start(bf16[1200,128]{1,0:T(8,128)(2,1)} %get-tuple-element.36), channel_id=1, source_target_pairs={{0,64},{64,128},{128,192},{192,0},{1,65},{65,129},{129,193},{193,1... | collective-permute-start | bytes 921608 | tf_op jit(solution)/shard_map/ppermute | solution.py:339
  65.5 11.8 %collective-permute-start.12 = (bf16[1200,128]{1,0:T(8,128)(2,1)}, bf16[1200,128]{1,0:T(8,128)(2,1)}, u32[]{:S(2)}, u32[]{:S(2)}) collective-permute-start(bf16[1200,128]{1,0:T(8,128)(2,1)} %get-tuple-element.38), channel_id=1, source_target_pairs={{0,192},{64,0},{128,64},{192,128},{1,193},{65,1},{129,65},{193,129... | collective-permute-start | bytes 921608 | tf_op jit(solution)/shard_map/ppermute | solution.py:339
  77.3 1.3 copy-start.1
  107.5 3.4 %copy-start.4 = (bf16[1200,128]{1,0:T(8,128)(2,1)}, bf16[1200,128]{1,0:T(8,128)(2,1)S(1)}, u32[]{:S(2)}) copy-start(bf16[1200,128]{1,0:T(8,128)(2,1)S(1)} %get-tuple-element.43.refs_1_) | copy-start | bytes 921604
  107.5 20.9 %copy-start.2 = (bf16[1200,128]{1,0:T(8,128)(2,1)}, bf16[1200,128]{1,0:T(8,128)(2,1)S(1)}, u32[]{:S(2)}) copy-start(bf16[1200,128]{1,0:T(8,128)(2,1)S(1)} %get-tuple-element.42.refs_0_) | copy-start | bytes 921604
  108.1 12.2 %collective-permute-start.20 = (bf16[1200,128]{1,0:T(8,128)(2,1)S(1)}, bf16[1200,128]{1,0:T(8,128)(2,1)S(1)}, u32[]{:S(2)}, u32[]{:S(2)}) collective-permute-start(bf16[1200,128]{1,0:T(8,128)(2,1)S(1)} %get-tuple-element.43.refs_1_), channel_id=1, source_target_pairs={{0,64},{64,128},{128,192},{192,0},{1,65},{65,129},{129,193},{193,1... | collective-permute-start | bytes 921608 | tf_op jit(solution)/shard_map/ppermute | solution.py:353
  108.5 15.3 %collective-permute-start.13 = (bf16[1,4,32,1280]{3,2,1,0:T(8,128)(2,1)S(1)}, bf16[1,4,32,1280]{3,2,1,0:T(8,128)(2,1)S(1)}, u32[]{:S(2)}, u32[]{:S(2)}) collective-permute-start(bf16[1,4,32,1280]{3,2,1,0:T(8,128)(2,1)S(1)} %bitcast.78), channel_id=1, source_target_pairs={{0,1},{1,0},{2,3},{3,2},{4,5},{5,4},{6,7},{7,6},{8,9},{9,8},{10,11... | collective-permute-start | bytes 983048 | tf_op jit(solution)/shard_map/ppermute | solution.py:370
  108.6 11.3 %collective-permute-start.14 = (bf16[1200,128]{1,0:T(8,128)(2,1)S(1)}, bf16[1200,128]{1,0:T(8,128)(2,1)S(1)}, u32[]{:S(2)}, u32[]{:S(2)}) collective-permute-start(bf16[1200,128]{1,0:T(8,128)(2,1)S(1)} %get-tuple-element.42.refs_0_), channel_id=1, source_target_pairs={{0,192},{64,0},{128,64},{192,128},{1,193},{65,1},{129,65},{193,129... | collective-permute-start | bytes 921608 | tf_op jit(solution)/shard_map/ppermute | solution.py:353
  110.9 15.9 %collective-permute-start.15 = (bf16[1200,128]{1,0:T(8,128)(2,1)S(1)}, bf16[1200,128]{1,0:T(8,128)(2,1)S(1)}, u32[]{:S(2)}, u32[]{:S(2)}) collective-permute-start(bf16[1200,128]{1,0:T(8,128)(2,1)S(1)} %get-tuple-element.43.refs_1_), channel_id=1, source_target_pairs={{0,192},{64,0},{128,64},{192,128},{1,193},{65,1},{129,65},{193,129... | collective-permute-start | bytes 921608 | tf_op jit(solution)/shard_map/ppermute | solution.py:353
  119.9 17.0 %copy-start.6 = (bf16[1200,128]{1,0:T(8,128)(2,1)}, bf16[1200,128]{1,0:T(8,128)(2,1)S(1)}, u32[]{:S(2)}) copy-start(bf16[1200,128]{1,0:T(8,128)(2,1)S(1)} %collective-permute-done.14.refs_2_) | copy-start | bytes 921604
  119.9 12.7 %collective-permute-start.19 = (bf16[1200,128]{1,0:T(8,128)(2,1)S(1)}, bf16[1200,128]{1,0:T(8,128)(2,1)S(1)}, u32[]{:S(2)}, u32[]{:S(2)}) collective-permute-start(bf16[1200,128]{1,0:T(8,128)(2,1)S(1)} %collective-permute-done.14.refs_2_), channel_id=1, source_target_pairs={{0,192},{64,0},{128,64},{192,128},{1,193},{65,1},{129,65},{193,129... | collective-permute-start | bytes 921608 | tf_op jit(solution)/shard_map/ppermute | solution.py:353
  120.3 12.3 %collective-permute-start.21 = (bf16[1200,128]{1,0:T(8,128)(2,1)S(1)}, bf16[1200,128]{1,0:T(8,128)(2,1)S(1)}, u32[]{:S(2)}, u32[]{:S(2)}) collective-permute-start(bf16[1200,128]{1,0:T(8,128)(2,1)S(1)} %collective-permute-done.20.refs_7_), channel_id=1, source_target_pairs={{0,64},{64,128},{128,192},{192,0},{1,65},{65,129},{129,193},{193,1... | collective-permute-start | bytes 921608 | tf_op jit(solution)/shard_map/ppermute | solution.py:353
  123.9 4.5 %collective-permute-start.16 = (bf16[1,32,1280]{2,1,0:T(8,128)(2,1)S(1)}, bf16[1,32,1280]{2,1,0:T(8,128)(2,1)S(1)}, u32[]{:S(2)}, u32[]{:S(2)}) collective-permute-start(bf16[1,32,1280]{2,1,0:T(8,128)(2,1)S(1)} %get-tuple-element.63), channel_id=1, source_target_pairs={{0,6},{2,0},{4,2},{6,4},{1,7},{3,1},{5,3},{7,5},{8,14},{10,8},{12,... | collective-permute-start | bytes 245768 | tf_op jit(solution)/shard_map/ppermute | solution.py:375
  125.7 5.9 %collective-permute-start.17 = (bf16[1,32,1280]{2,1,0:T(8,128)(2,1)S(1)}, bf16[1,32,1280]{2,1,0:T(8,128)(2,1)S(1)}, u32[]{:S(2)}, u32[]{:S(2)}) collective-permute-start(bf16[1,32,1280]{2,1,0:T(8,128)(2,1)S(1)} %get-tuple-element.62), channel_id=1, source_target_pairs={{0,4},{2,6},{4,0},{6,2},{1,5},{3,7},{5,1},{7,3},{8,12},{10,14},{12... | collective-permute-start | bytes 245768 | tf_op jit(solution)/shard_map/ppermute | solution.py:375
  126.8 6.4 %copy-start.8 = (bf16[1200,128]{1,0:T(8,128)(2,1)}, bf16[1200,128]{1,0:T(8,128)(2,1)S(1)}, u32[]{:S(2)}) copy-start(bf16[1200,128]{1,0:T(8,128)(2,1)S(1)} %collective-permute-done.15.refs_3_) | copy-start | bytes 921604
  126.8 5.7 %collective-permute-start.18 = (bf16[1,32,1280]{2,1,0:T(8,128)(2,1)S(1)}, bf16[1,32,1280]{2,1,0:T(8,128)(2,1)S(1)}, u32[]{:S(2)}, u32[]{:S(2)}) collective-permute-start(bf16[1,32,1280]{2,1,0:T(8,128)(2,1)S(1)} %get-tuple-element.61), channel_id=1, source_target_pairs={{0,2},{2,4},{4,6},{6,0},{1,3},{3,5},{5,7},{7,1},{8,10},{10,12},{12... | collective-permute-start | bytes 245768 | tf_op jit(solution)/shard_map/ppermute | solution.py:375
  128.4 7.8 %collective-permute-start.22 = (bf16[1200,128]{1,0:T(8,128)(2,1)S(1)}, bf16[1200,128]{1,0:T(8,128)(2,1)S(1)}, u32[]{:S(2)}, u32[]{:S(2)}) collective-permute-start(bf16[1200,128]{1,0:T(8,128)(2,1)S(1)} %get-tuple-element.42.refs_0_), channel_id=1, source_target_pairs={{0,64},{64,128},{128,192},{192,0},{1,65},{65,129},{129,193},{193,1... | collective-permute-start | bytes 921608 | tf_op jit(solution)/shard_map/ppermute | solution.py:353
  132.6 4.9 %copy-start.10 = (bf16[1200,128]{1,0:T(8,128)(2,1)}, bf16[1200,128]{1,0:T(8,128)(2,1)S(1)}, u32[]{:S(2)}) copy-start(bf16[1200,128]{1,0:T(8,128)(2,1)S(1)} %collective-permute-done.19.refs_4_) | copy-start | bytes 921604
  132.6 4.3 %copy-start.12 = (bf16[1200,128]{1,0:T(8,128)(2,1)}, bf16[1200,128]{1,0:T(8,128)(2,1)S(1)}, u32[]{:S(2)}) copy-start(bf16[1200,128]{1,0:T(8,128)(2,1)S(1)} %collective-permute-done.21.refs_5_) | copy-start | bytes 921604
  133.3 4.8 %collective-permute-start.23 = (bf16[3,4,32,1280]{3,2,1,0:T(8,128)(2,1)S(1)}, bf16[3,4,32,1280]{3,2,1,0:T(8,128)(2,1)S(1)}, u32[]{:S(2)}, u32[]{:S(2)}) collective-permute-start(bf16[3,4,32,1280]{3,2,1,0:T(8,128)(2,1)S(1)} %pad_maximum_fusion), channel_id=1, source_target_pairs={{0,1},{1,0},{2,3},{3,2},{4,5},{5,4},{6,7},{7,6},{8,9},{9,8},{10,11... | collective-permute-start | bytes 2949128 | tf_op jit(solution)/shard_map/ppermute | solution.py:370
  136.2 1.3 copy-start.14
  138.4 22.3 %copy-start.3 = (bf16[1200,128]{1,0:T(8,128)(2,1)S(1)}, bf16[1200,128]{1,0:T(8,128)(2,1)}, u32[]{:S(2)}) copy-start(bf16[1200,128]{1,0:T(8,128)(2,1)} %copy-done.2) | copy-start | bytes 921604
  138.5 22.3 %copy-start.5 = (bf16[1200,128]{1,0:T(8,128)(2,1)S(1)}, bf16[1200,128]{1,0:T(8,128)(2,1)}, u32[]{:S(2)}) copy-start(bf16[1200,128]{1,0:T(8,128)(2,1)} %copy-done.4) | copy-start | bytes 921604
  138.5 22.3 %copy-start.7 = (bf16[1200,128]{1,0:T(8,128)(2,1)S(1)}, bf16[1200,128]{1,0:T(8,128)(2,1)}, u32[]{:S(2)}) copy-start(bf16[1200,128]{1,0:T(8,128)(2,1)} %copy-done.6) | copy-start | bytes 921604
  138.5 22.3 %copy-start.9 = (bf16[1200,128]{1,0:T(8,128)(2,1)S(1)}, bf16[1200,128]{1,0:T(8,128)(2,1)}, u32[]{:S(2)}) copy-start(bf16[1200,128]{1,0:T(8,128)(2,1)} %copy-done.8) | copy-start | bytes 921604
  138.5 22.3 %copy-start.11 = (bf16[1200,128]{1,0:T(8,128)(2,1)S(1)}, bf16[1200,128]{1,0:T(8,128)(2,1)}, u32[]{:S(2)}) copy-start(bf16[1200,128]{1,0:T(8,128)(2,1)} %copy-done.10) | copy-start | bytes 921604
  138.5 22.3 %copy-start.13 = (bf16[1200,128]{1,0:T(8,128)(2,1)S(1)}, bf16[1200,128]{1,0:T(8,128)(2,1)}, u32[]{:S(2)}) copy-start(bf16[1200,128]{1,0:T(8,128)(2,1)} %copy-done.12) | copy-start | bytes 921604
  138.5 22.3 %copy-start.15 = (bf16[1200,128]{1,0:T(8,128)(2,1)S(1)}, bf16[1200,128]{1,0:T(8,128)(2,1)}, u32[]{:S(2)}) copy-start(bf16[1200,128]{1,0:T(8,128)(2,1)} %copy-done.14) | copy-start | bytes 921604
  138.6 10.6 %collective-permute-start.24 = (bf16[3,32,1280]{2,1,0:T(8,128)(2,1)S(1)}, bf16[3,32,1280]{2,1,0:T(8,128)(2,1)S(1)}, u32[]{:S(2)}, u32[]{:S(2)}) collective-permute-start(bf16[3,32,1280]{2,1,0:T(8,128)(2,1)S(1)} %get-tuple-element.58), channel_id=1, source_target_pairs={{0,6},{2,0},{4,2},{6,4},{1,7},{3,1},{5,3},{7,5},{8,14},{10,8},{12,... | collective-permute-start | bytes 737288 | tf_op jit(solution)/shard_map/ppermute | solution.py:375
  141.0 9.3 %collective-permute-start.25 = (bf16[3,32,1280]{2,1,0:T(8,128)(2,1)S(1)}, bf16[3,32,1280]{2,1,0:T(8,128)(2,1)S(1)}, u32[]{:S(2)}, u32[]{:S(2)}) collective-permute-start(bf16[3,32,1280]{2,1,0:T(8,128)(2,1)S(1)} %get-tuple-element.60), channel_id=1, source_target_pairs={{0,4},{2,6},{4,0},{6,2},{1,5},{3,7},{5,1},{7,3},{8,12},{10,14},{12... | collective-permute-start | bytes 737288 | tf_op jit(solution)/shard_map/ppermute | solution.py:375
  141.9 10.9 %collective-permute-start.26 = (bf16[3,32,1280]{2,1,0:T(8,128)(2,1)S(1)}, bf16[3,32,1280]{2,1,0:T(8,128)(2,1)S(1)}, u32[]{:S(2)}, u32[]{:S(2)}) collective-permute-start(bf16[3,32,1280]{2,1,0:T(8,128)(2,1)S(1)} %get-tuple-element.59), channel_id=1, source_target_pairs={{0,2},{2,4},{4,6},{6,0},{1,3},{3,5},{5,7},{7,1},{8,10},{10,12},{12... | collective-permute-start | bytes 737288 | tf_op jit(solution)/shard_map/ppermute | solution.py:375
  153.9 18.0 %all-to-all-start.3 = ((bf16[32,4,1280]{2,1,0:T(4,128)(2,1)}), bf16[32,4,1280]{2,1,0:T(4,128)(2,1)S(1)}, u32[]{:S(2)}, u32[]{:S(2)}) async-start(bf16[32,4,1280]{2,1,0:T(4,128)(2,1)} %reshape.197), calls=%async_computation.3 | async-start | bytes 655360 | tf_op jit(solution)/shard_map/all_to_all | solution.py:388
  160.8 1.7 %copy-start.17 = (bf16[4,256,1280]{2,1,0:T(8,128)(2,1)S(1)}, bf16[4,256,1280]{2,1,0:T(8,128)(2,1)}, u32[]{:S(2)}) copy-start(bf16[4,256,1280]{2,1,0:T(8,128)(2,1)} %copy-done.16) | copy-start | bytes 7864324

commit v5 on v4

--- a/solution.py
+++ b/solution.py
@@ -379,7 +379,9 @@
 
     first, others = across((0,))
     first_others = along(others)
-    first, near[1], far[1] = lax.optimization_barrier((first, near[1], far[1]))
+    first, near[1], near[3], far[1], far[3] = lax.optimization_barrier(
+        (first, near[1], near[3], far[1], far[3])
+    )
     first_others, near[2], far[2] = lax.optimization_barrier((first_others, near[2], far[2]))
     rest, others = across((1, 2, 3))
     rest = shared(rest, along(others))

time: 175 us -> 174 us (level)
    ppermute x6, waiting for transfers between devices: 11.7 us -> 6.93 us  [passed(): return lax.ppermute(value, 'x', shift(NX, by))]
    ppermute x6, waiting for transfers between devices: 14.6 us -> 16.5 us  [along(): lax.ppermute(part, 'y', shift(NY, -by))]
    ppermute x6, starting transfers between devices: 5.43 us -> 7.29 us  [passed(): return lax.ppermute(value, 'x', shift(NX, by))]
where the time goes in v5:
time: 174 us; the launch traced here: 172 us
  starting transfers between devices  51.9 us (30%)
  waiting for transfers between devices  47.1 us (27%)
  blocking collectives  23.9 us (14%)
  Pallas kernels  19.7 us (11%)
  local copies, waits for them, and re-layouts  15.8 us (9%)
  matrix products  6.54 us (4%)
  other arithmetic  5.79 us (3%)
    all_to_all x1, blocking collectives, body(): every = lax.all_to_all(sums, VOCAB, 0, 0, tiled=True)  23.9 us
    ppermute x6, waiting for transfers between devices, along(): lax.ppermute(part, 'y', shift(NY, -by))  16.5 us
    all_to_all x1, starting transfers between devices, gather_hidden(): got = lax.all_to_all(spread, ('x', 'z'), 0, 0, tiled=True)  11.6 us
    ppermute x6, waiting for transfers between devices, sent(): return lax.ppermute(value, 'x', shift(NX, by))  8.07 us
    ppermute x6, starting transfers between devices, sent(): return lax.ppermute(value, 'x', shift(NX, by))  7.36 us
    ppermute x6, starting transfers between devices, passed(): return lax.ppermute(value, 'x', shift(NX, by))  7.29 us
    ppermute x6, starting transfers between devices, along(): lax.ppermute(part, 'y', shift(NY, -by))  7.27 us
    ppermute x6, waiting for transfers between devices, passed(): return lax.ppermute(value, 'x', shift(NX, by))  6.93 us
  transfers between devices with their start and end apart: 30, of which 17 were waited for; matrix products, arithmetic and copies ran while one was open for 10% of the time, Pallas kernels for 9%

profile of v5, /device:TPU:6, one launch (start us, length us, event | category | flops | bytes accessed | tf_op | source)
XLA Modules:
  0.0 171.8 jit_solution(17780214092927223201)
XLA Ops:
  2.3 11.6 %all-to-all-start = ((bf16[32,4,1280]{2,1,0:T(4,128)(2,1)}), bf16[32,4,1280]{2,1,0:T(4,128)(2,1)S(1)}, u32[]{:S(2)}, u32[]{:S(2)}) async-start(bf16[32,4,1280]{2,1,0:T(4,128)(2,1)} %bitcast.1), calls=%async_computation | async-start | bytes 655360 | tf_op jit(solution)/shard_map/all_to_all | solution.py:39
  14.7 2.1 %reshape.195 = bf16[4,64,1187]{2,1,0:T(8,128)(2,1)S(1)} reshape(bf16[4,75968]{1,0:T(4,128)(2,1)} %param.5) | data formatting | bytes 1215488 | tf_op jit(solution)/shard_map/reshape | solution.py:63
  16.9 1.3 copy.19
  18.2 2.1 %pad.9.head_ref = bf16[1200,1280]{1,0:T(8,128)(2,1)S(1)} pad(bf16[1187,1280]{1,0:T(8,128)(2,1)} %bitcast.70, bf16[]{:T(256)} %constant.96.clone.1), padding=0_13x0_0 | pad | bytes 6110722 | tf_op jit(solution)/shard_map/jit(_pad)/pad | solution.py:331
  20.3 2.3 %maximum_bitcast_fusion = bf16[64,4,1200]{2,1,0:T(4,128)(2,1)} fusion(bf16[4,64,13]{2,0,1:T(4,128)(2,1)S(1)} %broadcast_in_dim.5, bf16[4,64,1187]{2,0,1:T(4,128)(2,1)} %copy.19), kind=kLoop, calls=%fused_computation.8 | loop fusion | flops 1228800 | bytes 1228800 | tf_op jit(solution)/shard_map/transpose | solution.py:66
  22.6 2.9 %all-to-all-done = bf16[32,4,1280]{2,1,0:T(4,128)(2,1)S(1)} async-done(((bf16[32,4,1280]{2,1,0:T(4,128)(2,1)}), bf16[32,4,1280]{2,1,0:T(4,128)(2,1)S(1)}, u32[]{:S(2)}, u32[]{:S(2)}) %all-to-all-start) | async-done | bytes 327712 | tf_op jit(solution)/shard_map/all_to_all | solution.py:39
  26.3 1.1 fusion.5.refs_0_
  27.5 1.7 collective-permute-start
  29.1 2.9 %collective-permute-start.1 = (bf16[4,32,1280]{2,1,0:T(8,128)(2,1)S(1)}, bf16[4,32,1280]{2,1,0:T(8,128)(2,1)}, u32[]{:S(2)}, u32[]{:S(2)}) collective-permute-start(bf16[4,32,1280]{2,1,0:T(8,128)(2,1)S(1)} %fusion.5.refs_0_), channel_id=1, source_target_pairs={{0,4},{2,6},{4,0},{6,2},{1,5},{3,7},{5,1},{7,3},{8,12},{10,14},{12... | collective-permute-start | bytes 983048 | tf_op jit(solution)/shard_map/ppermute | solution.py:42
  32.0 1.3 collective-permute-start.2
  33.4 5.5 %all-to-all-start.1 = ((bf16[64,4,1200]{2,1,0:T(4,128)(2,1)}), bf16[64,4,1200]{2,1,0:T(4,128)(2,1)}, u32[]{:S(2)}, u32[]{:S(2)}) async-start(bf16[64,4,1200]{2,1,0:T(4,128)(2,1)} %maximum_bitcast_fusion), calls=%async_computation.1 | async-start | bytes 1310720 | tf_op jit(solution)/shard_map/all_to_all | solution.py:70
  39.4 5.0 %collective-permute-done.1.refs_2_ = bf16[4,32,1280]{2,1,0:T(8,128)(2,1)} collective-permute-done((bf16[4,32,1280]{2,1,0:T(8,128)(2,1)S(1)}, bf16[4,32,1280]{2,1,0:T(8,128)(2,1)}, u32[]{:S(2)}, u32[]{:S(2)}) %collective-permute-start.1) | collective-permute-done | bytes 327712 | tf_op jit(solution)/shard_map/ppermute | solution.py:42
  45.0 1.5 collective-permute-done.5.refs_6_
  46.9 2.6 %shard_map.60 = (bf16[1200,128]{1,0:T(8,128)(2,1)S(1)}, bf16[1200,128]{1,0:T(8,128)(2,1)S(1)}) custom-call(bf16[1200,1280]{1,0:T(8,128)(2,1)S(1)} %pad.9.head_ref, bf16[4,32,1280]{2,1,0:T(8,128)(2,1)S(1)} %fusion.5.refs_0_, bf16[4,32,1280]{2,1,0:T(8,128)(2,1)} %collective-permute-done.refs_1_, bf16[4,32,1280]{2,1,0:T(8,128)(2,1)} %collective-permute-done.1.refs_2_, ...), custom_call_target="tpu_custom_call" | custom-call | flops 786432000 | bytes 1000000 | tf_op jit(solution)/shard_map/pallas_call | solution.py:100
  49.5 0.9 collective-permute-start.8
  50.4 1.2 collective-permute-start.9
  51.6 5.6 %shard_map.59 = (bf16[4,256,1280]{2,1,0:T(8,128)(2,1)S(1)}, bf16[1200,128]{1,0:T(8,128)(2,1)}, bf16[1200,128]{1,0:T(8,128)(2,1)}, f32[1200,128]{1,0:T(8,128)S(1)...) custom-call(bf16[1200,1280]{1,0:T(8,128)(2,1)S(1)} %pad.9.head_ref, bf16[4,32,1280]{2,1,0:T(8,128)(2,1)S(1)} %fusion.5.refs_0_, ...), custom_call_target="tpu_custom_call" | custom-call | flops 2359296000 | bytes 4000000 | tf_op jit(solution)/shard_map/pallas_call | solution.py:186
  57.2 1.5 copy-done.16
  58.7 2.0 %collective-permute-start.11 = (bf16[1200,128]{1,0:T(8,128)(2,1)}, bf16[1200,128]{1,0:T(8,128)(2,1)}, u32[]{:S(2)}, u32[]{:S(2)}) collective-permute-start(bf16[1200,128]{1,0:T(8,128)(2,1)} %get-tuple-element.39), channel_id=1, source_target_pairs={{0,64},{64,128},{128,192},{192,0},{1,65},{65,129},{129,193},{193,1... | collective-permute-start | bytes 921608 | tf_op jit(solution)/shard_map/ppermute | solution.py:339
  60.8 1.5 shard_map.61
  62.3 3.2 %collective-permute-start.10 = (bf16[1200,128]{1,0:T(8,128)(2,1)}, bf16[1200,128]{1,0:T(8,128)(2,1)}, u32[]{:S(2)}, u32[]{:S(2)}) collective-permute-start(bf16[1200,128]{1,0:T(8,128)(2,1)} %get-tuple-element.38), channel_id=1, source_target_pairs={{0,64},{64,128},{128,192},{192,0},{1,65},{65,129},{129,193},{193,1... | collective-permute-start | bytes 921608 | tf_op jit(solution)/shard_map/ppermute | solution.py:339
  65.6 2.2 %reshape.196 = bf16[256,1200]{1,0:T(8,128)(2,1)} reshape(bf16[64,4,1200]{2,1,0:T(4,128)(2,1)} %all-to-all-done.1) | data formatting | bytes 1228800 | tf_op jit(solution)/shard_map/reshape | solution.py:70
  67.8 1.5 fusion.7.teacher_ref
  69.3 3.2 %collective-permute-done.7.a0 = bf16[1200,128]{1,0:T(8,128)(2,1)} collective-permute-done((bf16[1200,128]{1,0:T(8,128)(2,1)}, bf16[1200,128]{1,0:T(8,128)(2,1)}, u32[]{:S(2)}, u32[]{:S(2)}) %collective-permute-start.7) | collective-permute-done | bytes 307232 | tf_op jit(solution)/shard_map/ppermute | solution.py:339
  72.5 1.9 %collective-permute-done.10.a1 = bf16[1200,128]{1,0:T(8,128)(2,1)} collective-permute-done((bf16[1200,128]{1,0:T(8,128)(2,1)}, bf16[1200,128]{1,0:T(8,128)(2,1)}, u32[]{:S(2)}, u32[]{:S(2)}) %collective-permute-start.10) | collective-permute-done | bytes 307232 | tf_op jit(solution)/shard_map/ppermute | solution.py:339
  74.4 3.0 %collective-permute-done.12.b1 = bf16[1200,128]{1,0:T(8,128)(2,1)} collective-permute-done((bf16[1200,128]{1,0:T(8,128)(2,1)}, bf16[1200,128]{1,0:T(8,128)(2,1)}, u32[]{:S(2)}, u32[]{:S(2)}) %collective-permute-start.12) | collective-permute-done | bytes 307232 | tf_op jit(solution)/shard_map/ppermute | solution.py:339
  77.3 1.3 copy-done.1
  78.6 3.8 %shard_map.62 = (f32[1200,256]{1,0:T(8,128)S(1)}, f32[64,8,128]{2,1,0:T(8,128)S(1)}) custom-call(f32[1200,256]{1,0:T(8,128)S(1)} %copy-done.1, bf16[1200,128]{1,0:T(8,128)(2,1)} %collective-permute-done.7.a0, bf16[1200,128]{1,0:T(8,128)(2,1)} %collective-permute-done.10.a1, bf16[1200,128]{1,0:T(8,128)(2,1)} %collective-permute-done.11.b0, ...), custom_call_target="tpu_custom_call" | custom-call | flops 30720000 | bytes 5000000 | tf_op jit(solution)/shard_map/pallas_call | solution.py:116
  82.4 23.9 %all_to_all.20.every_ref = f32[64,8,128]{2,1,0:T(8,128)S(1)} all-to-all(f32[64,8,128]{2,1,0:T(8,128)S(1)} %get-tuple-element.42), channel_id=1, replica_groups=mesh['x'=4,'z'=8,'y'=4,'c'=2] {'z','y','c'}, dimensions={0} | all-to-all | bytes 524288 | tf_op jit(solution)/shard_map/all_to_all | solution.py:349
  106.3 1.1 shard_map.63
  108.8 1.7 %collective-permute-start.14 = (bf16[1200,128]{1,0:T(8,128)(2,1)S(1)}, bf16[1200,128]{1,0:T(8,128)(2,1)S(1)}, u32[]{:S(2)}, u32[]{:S(2)}) collective-permute-start(bf16[1200,128]{1,0:T(8,128)(2,1)S(1)} %get-tuple-element.44.refs_0_), channel_id=1, source_target_pairs={{0,192},{64,0},{128,64},{192,128},{1,193},{65,1},{129,65},{193,129... | collective-permute-start | bytes 921608 | tf_op jit(solution)/shard_map/ppermute | solution.py:353
  110.5 1.5 collective-permute-start.15
  113.2 6.9 %collective-permute-done.14.refs_2_ = bf16[1200,128]{1,0:T(8,128)(2,1)S(1)} collective-permute-done((bf16[1200,128]{1,0:T(8,128)(2,1)S(1)}, bf16[1200,128]{1,0:T(8,128)(2,1)S(1)}, u32[]{:S(2)}, u32[]{:S(2)}) %collective-permute-start.14) | collective-permute-done | bytes 307232 | tf_op jit(solution)/shard_map/ppermute | solution.py:353
  120.7 2.7 %collective-permute-start.22 = (bf16[1200,128]{1,0:T(8,128)(2,1)S(1)}, bf16[1200,128]{1,0:T(8,128)(2,1)S(1)}, u32[]{:S(2)}, u32[]{:S(2)}) collective-permute-start(bf16[1200,128]{1,0:T(8,128)(2,1)S(1)} %collective-permute-done.17.refs_7_), channel_id=1, source_target_pairs={{0,64},{64,128},{128,192},{192,0},{1,65},{65,129},{129,193},{193,1... | collective-permute-start | bytes 921608 | tf_op jit(solution)/shard_map/ppermute | solution.py:353
  123.5 1.9 %collective-permute-start.18 = (bf16[1,32,1280]{2,1,0:T(8,128)(2,1)S(1)}, bf16[1,32,1280]{2,1,0:T(8,128)(2,1)S(1)}, u32[]{:S(2)}, u32[]{:S(2)}) collective-permute-start(bf16[1,32,1280]{2,1,0:T(8,128)(2,1)S(1)} %get-tuple-element.67), channel_id=1, source_target_pairs={{0,6},{2,0},{4,2},{6,4},{1,7},{3,1},{5,3},{7,5},{8,14},{10,8},{12,... | collective-permute-start | bytes 245768 | tf_op jit(solution)/shard_map/ppermute | solution.py:375
  125.4 1.6 collective-permute-start.19
  129.0 2.4 %collective-permute-done.19 = bf16[1,32,1280]{2,1,0:T(8,128)(2,1)S(1)} collective-permute-done((bf16[1,32,1280]{2,1,0:T(8,128)(2,1)S(1)}, bf16[1,32,1280]{2,1,0:T(8,128)(2,1)S(1)}, u32[]{:S(2)}, u32[]{:S(2)}) %collective-permute-start.19) | collective-permute-done | bytes 81952 | tf_op jit(solution)/shard_map/ppermute | solution.py:375
  131.5 1.2 collective-permute-done.20
  136.5 1.5 collective-permute-start.24
  138.0 1.1 collective-permute-start.25
  139.7 5.7 %collective-permute-done.24 = bf16[3,32,1280]{2,1,0:T(8,128)(2,1)S(1)} collective-permute-done((bf16[3,32,1280]{2,1,0:T(8,128)(2,1)S(1)}, bf16[3,32,1280]{2,1,0:T(8,128)(2,1)S(1)}, u32[]{:S(2)}, u32[]{:S(2)}) %collective-permute-start.24) | collective-permute-done | bytes 245792 | tf_op jit(solution)/shard_map/ppermute | solution.py:375
  145.4 3.0 %collective-permute-done.25 = bf16[3,32,1280]{2,1,0:T(8,128)(2,1)S(1)} collective-permute-done((bf16[3,32,1280]{2,1,0:T(8,128)(2,1)S(1)}, bf16[3,32,1280]{2,1,0:T(8,128)(2,1)S(1)}, u32[]{:S(2)}, u32[]{:S(2)}) %collective-permute-start.25) | collective-permute-done | bytes 245792 | tf_op jit(solution)/shard_map/ppermute | solution.py:375
  148.4 4.1 %collective-permute-done.26 = bf16[3,32,1280]{2,1,0:T(8,128)(2,1)S(1)} collective-permute-done((bf16[3,32,1280]{2,1,0:T(8,128)(2,1)S(1)}, bf16[3,32,1280]{2,1,0:T(8,128)(2,1)S(1)}, u32[]{:S(2)}, u32[]{:S(2)}) %collective-permute-start.26) | collective-permute-done | bytes 245792 | tf_op jit(solution)/shard_map/ppermute | solution.py:375
  152.8 0.8 reshape.197
  153.6 5.6 %all-to-all-start.3 = ((bf16[32,4,1280]{2,1,0:T(4,128)(2,1)}), bf16[32,4,1280]{2,1,0:T(4,128)(2,1)S(1)}, u32[]{:S(2)}, u32[]{:S(2)}) async-start(bf16[32,4,1280]{2,1,0:T(4,128)(2,1)} %reshape.197), calls=%async_computation.3 | async-start | bytes 655360 | tf_op jit(solution)/shard_map/all_to_all | solution.py:390
  159.3 1.7 %copy-done.17 = bf16[4,256,1280]{2,1,0:T(8,128)(2,1)S(1)} copy-done((bf16[4,256,1280]{2,1,0:T(8,128)(2,1)S(1)}, bf16[4,256,1280]{2,1,0:T(8,128)(2,1)}, u32[]{:S(2)}) %copy-start.17) | copy-done | bytes 2621464
  161.0 5.0 %shard_map.64 = bf16[1187,1280]{1,0:T(8,128)(2,1)} custom-call(bf16[1200,128]{1,0:T(8,128)(2,1)S(1)} %copy-done.3, bf16[1200,128]{1,0:T(8,128)(2,1)S(1)} %copy-done.5, bf16[1200,128]{1,0:T(8,128)(2,1)S(1)} %copy-done.7, bf16[1200,128]{1,0:T(8,128)(2,1)S(1)} %copy-done.11, bf16[1200,128]{1,0:T(8,128)(2,1)S(1)} %copy-done.13, ...), custom_call_target="tpu_custom_call" | custom-call | flops 3145728000 | bytes 9000000 | tf_op jit(solution)/shard_map/pallas_call | solution.py:316
  166.0 5.0 %all-to-all-done.3 = bf16[32,4,1280]{2,1,0:T(4,128)(2,1)S(1)} async-done(((bf16[32,4,1280]{2,1,0:T(4,128)(2,1)}), bf16[32,4,1280]{2,1,0:T(4,128)(2,1)S(1)}, u32[]{:S(2)}, u32[]{:S(2)}) %all-to-all-start.3) | async-done | bytes 327712 | tf_op jit(solution)/shard_map/all_to_all | solution.py:390
  (92 shorter events, 15.5 us)
Async XLA Ops:
  2.3 23.3 %all-to-all-start = ((bf16[32,4,1280]{2,1,0:T(4,128)(2,1)}), bf16[32,4,1280]{2,1,0:T(4,128)(2,1)S(1)}, u32[]{:S(2)}, u32[]{:S(2)}) async-start(bf16[32,4,1280]{2,1,0:T(4,128)(2,1)} %bitcast.1), calls=%async_computation | async-start | bytes 655360 | tf_op jit(solution)/shard_map/all_to_all | solution.py:39
  27.5 11.6 %collective-permute-start = (bf16[4,32,1280]{2,1,0:T(8,128)(2,1)S(1)}, bf16[4,32,1280]{2,1,0:T(8,128)(2,1)}, u32[]{:S(2)}, u32[]{:S(2)}) collective-permute-start(bf16[4,32,1280]{2,1,0:T(8,128)(2,1)S(1)} %fusion.5.refs_0_), channel_id=1, source_target_pairs={{0,2},{2,4},{4,6},{6,0},{1,3},{3,5},{5,7},{7,1},{8,10},{10,12},{12... | collective-permute-start | bytes 983048 | tf_op jit(solution)/shard_map/ppermute | solution.py:42
  29.1 15.3 %collective-permute-start.1 = (bf16[4,32,1280]{2,1,0:T(8,128)(2,1)S(1)}, bf16[4,32,1280]{2,1,0:T(8,128)(2,1)}, u32[]{:S(2)}, u32[]{:S(2)}) collective-permute-start(bf16[4,32,1280]{2,1,0:T(8,128)(2,1)S(1)} %fusion.5.refs_0_), channel_id=1, source_target_pairs={{0,4},{2,6},{4,0},{6,2},{1,5},{3,7},{5,1},{7,3},{8,12},{10,14},{12... | collective-permute-start | bytes 983048 | tf_op jit(solution)/shard_map/ppermute | solution.py:42
  32.0 12.5 %collective-permute-start.2 = (bf16[4,32,1280]{2,1,0:T(8,128)(2,1)S(1)}, bf16[4,32,1280]{2,1,0:T(8,128)(2,1)}, u32[]{:S(2)}, u32[]{:S(2)}) collective-permute-start(bf16[4,32,1280]{2,1,0:T(8,128)(2,1)S(1)} %fusion.5.refs_0_), channel_id=1, source_target_pairs={{0,6},{2,0},{4,2},{6,4},{1,7},{3,1},{5,3},{7,5},{8,14},{10,8},{12,... | collective-permute-start | bytes 983048 | tf_op jit(solution)/shard_map/ppermute | solution.py:42
  33.4 32.2 %all-to-all-start.1 = ((bf16[64,4,1200]{2,1,0:T(4,128)(2,1)}), bf16[64,4,1200]{2,1,0:T(4,128)(2,1)}, u32[]{:S(2)}, u32[]{:S(2)}) async-start(bf16[64,4,1200]{2,1,0:T(4,128)(2,1)} %maximum_bitcast_fusion), calls=%async_computation.1 | async-start | bytes 1310720 | tf_op jit(solution)/shard_map/all_to_all | solution.py:70
  38.8 6.1 %collective-permute-start.3 = (bf16[4,32,1280]{2,1,0:T(8,128)(2,1)S(1)}, bf16[4,32,1280]{2,1,0:T(8,128)(2,1)}, u32[]{:S(2)}, u32[]{:S(2)}) collective-permute-start(bf16[4,32,1280]{2,1,0:T(8,128)(2,1)S(1)} %fusion.5.refs_0_), channel_id=1, source_target_pairs={{0,1},{1,0},{2,3},{3,2},{4,5},{5,4},{6,7},{7,6},{8,9},{9,8},{10,11... | collective-permute-start | bytes 983048 | tf_op jit(solution)/shard_map/ppermute | solution.py:43
  39.0 5.9 %collective-permute-start.4 = (bf16[4,32,1280]{2,1,0:T(8,128)(2,1)}, bf16[4,32,1280]{2,1,0:T(8,128)(2,1)}, u32[]{:S(2)}, u32[]{:S(2)}) collective-permute-start(bf16[4,32,1280]{2,1,0:T(8,128)(2,1)} %collective-permute-done.refs_1_), channel_id=1, source_target_pairs={{0,1},{1,0},{2,3},{3,2},{4,5},{5,4},{6,7},{7,6},{8,9},{9,8},{10,11... | collective-permute-start | bytes 983048 | tf_op jit(solution)/shard_map/ppermute | solution.py:43
  44.5 2.0 %collective-permute-start.5 = (bf16[4,32,1280]{2,1,0:T(8,128)(2,1)}, bf16[4,32,1280]{2,1,0:T(8,128)(2,1)}, u32[]{:S(2)}, u32[]{:S(2)}) collective-permute-start(bf16[4,32,1280]{2,1,0:T(8,128)(2,1)} %collective-permute-done.1.refs_2_), channel_id=1, source_target_pairs={{0,1},{1,0},{2,3},{3,2},{4,5},{5,4},{6,7},{7,6},{8,9},{9,8},{10,11... | collective-permute-start | bytes 983048 | tf_op jit(solution)/shard_map/ppermute | solution.py:43
  44.5 2.4 %collective-permute-start.6 = (bf16[4,32,1280]{2,1,0:T(8,128)(2,1)}, bf16[4,32,1280]{2,1,0:T(8,128)(2,1)}, u32[]{:S(2)}, u32[]{:S(2)}) collective-permute-start(bf16[4,32,1280]{2,1,0:T(8,128)(2,1)} %collective-permute-done.2.refs_3_), channel_id=1, source_target_pairs={{0,1},{1,0},{2,3},{3,2},{4,5},{5,4},{6,7},{7,6},{8,9},{9,8},{10,11... | collective-permute-start | bytes 983048 | tf_op jit(solution)/shard_map/ppermute | solution.py:43
  49.5 11.3 %collective-permute-start.8 = (bf16[1200,128]{1,0:T(8,128)(2,1)S(1)}, bf16[1200,128]{1,0:T(8,128)(2,1)S(1)}, u32[]{:S(2)}, u32[]{:S(2)}) collective-permute-start(bf16[1200,128]{1,0:T(8,128)(2,1)S(1)} %get-tuple-element.36), channel_id=1, source_target_pairs={{0,64},{64,128},{128,192},{192,0},{1,65},{65,129},{129,193},{193,1... | collective-permute-start | bytes 921608 | tf_op jit(solution)/shard_map/ppermute | solution.py:339
  50.4 10.4 %collective-permute-start.9 = (bf16[1200,128]{1,0:T(8,128)(2,1)S(1)}, bf16[1200,128]{1,0:T(8,128)(2,1)S(1)}, u32[]{:S(2)}, u32[]{:S(2)}) collective-permute-start(bf16[1200,128]{1,0:T(8,128)(2,1)S(1)} %get-tuple-element.37), channel_id=1, source_target_pairs={{0,192},{64,0},{128,64},{192,128},{1,193},{65,1},{129,65},{193,129... | collective-permute-start | bytes 921608 | tf_op jit(solution)/shard_map/ppermute | solution.py:339
  57.2 1.5 copy-start.16
  58.7 6.8 %copy-start = (f32[1200,256]{1,0:T(8,128)}, f32[1200,256]{1,0:T(8,128)S(1)}, u32[]{:S(2)}) copy-start(f32[1200,256]{1,0:T(8,128)S(1)} %get-tuple-element.32.own_ref) | copy-start | bytes 3686404
  58.7 10.5 %collective-permute-start.11 = (bf16[1200,128]{1,0:T(8,128)(2,1)}, bf16[1200,128]{1,0:T(8,128)(2,1)}, u32[]{:S(2)}, u32[]{:S(2)}) collective-permute-start(bf16[1200,128]{1,0:T(8,128)(2,1)} %get-tuple-element.39), channel_id=1, source_target_pairs={{0,64},{64,128},{128,192},{192,0},{1,65},{65,129},{129,193},{193,1... | collective-permute-start | bytes 921608 | tf_op jit(solution)/shard_map/ppermute | solution.py:339
  60.7 11.7 %collective-permute-start.7 = (bf16[1200,128]{1,0:T(8,128)(2,1)}, bf16[1200,128]{1,0:T(8,128)(2,1)}, u32[]{:S(2)}, u32[]{:S(2)}) collective-permute-start(bf16[1200,128]{1,0:T(8,128)(2,1)} %get-tuple-element.33), channel_id=1, source_target_pairs={{0,192},{64,0},{128,64},{192,128},{1,193},{65,1},{129,65},{193,129... | collective-permute-start | bytes 921608 | tf_op jit(solution)/shard_map/ppermute | solution.py:339
  62.3 12.1 %collective-permute-start.10 = (bf16[1200,128]{1,0:T(8,128)(2,1)}, bf16[1200,128]{1,0:T(8,128)(2,1)}, u32[]{:S(2)}, u32[]{:S(2)}) collective-permute-start(bf16[1200,128]{1,0:T(8,128)(2,1)} %get-tuple-element.38), channel_id=1, source_target_pairs={{0,64},{64,128},{128,192},{192,0},{1,65},{65,129},{129,193},{193,1... | collective-permute-start | bytes 921608 | tf_op jit(solution)/shard_map/ppermute | solution.py:339
  65.5 11.8 %collective-permute-start.12 = (bf16[1200,128]{1,0:T(8,128)(2,1)}, bf16[1200,128]{1,0:T(8,128)(2,1)}, u32[]{:S(2)}, u32[]{:S(2)}) collective-permute-start(bf16[1200,128]{1,0:T(8,128)(2,1)} %get-tuple-element.40), channel_id=1, source_target_pairs={{0,192},{64,0},{128,64},{192,128},{1,193},{65,1},{129,65},{193,129... | collective-permute-start | bytes 921608 | tf_op jit(solution)/shard_map/ppermute | solution.py:339
  77.3 1.3 copy-start.1
  107.5 5.7 %copy-start.2 = (bf16[1200,128]{1,0:T(8,128)(2,1)}, bf16[1200,128]{1,0:T(8,128)(2,1)S(1)}, u32[]{:S(2)}) copy-start(bf16[1200,128]{1,0:T(8,128)(2,1)S(1)} %get-tuple-element.44.refs_0_) | copy-start | bytes 921604
  107.5 5.7 %copy-start.4 = (bf16[1200,128]{1,0:T(8,128)(2,1)}, bf16[1200,128]{1,0:T(8,128)(2,1)S(1)}, u32[]{:S(2)}) copy-start(bf16[1200,128]{1,0:T(8,128)(2,1)S(1)} %get-tuple-element.45.refs_1_) | copy-start | bytes 921604
  108.1 15.2 %collective-permute-start.13 = (bf16[1,4,32,1280]{3,2,1,0:T(8,128)(2,1)S(1)}, bf16[1,4,32,1280]{3,2,1,0:T(8,128)(2,1)S(1)}, u32[]{:S(2)}, u32[]{:S(2)}) collective-permute-start(bf16[1,4,32,1280]{3,2,1,0:T(8,128)(2,1)S(1)} %bitcast.78), channel_id=1, source_target_pairs={{0,1},{1,0},{2,3},{3,2},{4,5},{5,4},{6,7},{7,6},{8,9},{9,8},{10,11... | collective-permute-start | bytes 983048 | tf_op jit(solution)/shard_map/ppermute | solution.py:370
  108.5 12.2 %collective-permute-start.17 = (bf16[1200,128]{1,0:T(8,128)(2,1)S(1)}, bf16[1200,128]{1,0:T(8,128)(2,1)S(1)}, u32[]{:S(2)}, u32[]{:S(2)}) collective-permute-start(bf16[1200,128]{1,0:T(8,128)(2,1)S(1)} %get-tuple-element.45.refs_1_), channel_id=1, source_target_pairs={{0,64},{64,128},{128,192},{192,0},{1,65},{65,129},{129,193},{193,1... | collective-permute-start | bytes 921608 | tf_op jit(solution)/shard_map/ppermute | solution.py:353
  108.8 11.3 %collective-permute-start.14 = (bf16[1200,128]{1,0:T(8,128)(2,1)S(1)}, bf16[1200,128]{1,0:T(8,128)(2,1)S(1)}, u32[]{:S(2)}, u32[]{:S(2)}) collective-permute-start(bf16[1200,128]{1,0:T(8,128)(2,1)S(1)} %get-tuple-element.44.refs_0_), channel_id=1, source_target_pairs={{0,192},{64,0},{128,64},{192,128},{1,193},{65,1},{129,65},{193,129... | collective-permute-start | bytes 921608 | tf_op jit(solution)/shard_map/ppermute | solution.py:353
  110.5 14.9 %collective-permute-start.15 = (bf16[1200,128]{1,0:T(8,128)(2,1)S(1)}, bf16[1200,128]{1,0:T(8,128)(2,1)S(1)}, u32[]{:S(2)}, u32[]{:S(2)}) collective-permute-start(bf16[1200,128]{1,0:T(8,128)(2,1)S(1)} %get-tuple-element.44.refs_0_), channel_id=1, source_target_pairs={{0,64},{64,128},{128,192},{192,0},{1,65},{65,129},{129,193},{193,1... | collective-permute-start | bytes 921608 | tf_op jit(solution)/shard_map/ppermute | solution.py:353
  112.0 15.0 %collective-permute-start.16 = (bf16[1200,128]{1,0:T(8,128)(2,1)S(1)}, bf16[1200,128]{1,0:T(8,128)(2,1)S(1)}, u32[]{:S(2)}, u32[]{:S(2)}) collective-permute-start(bf16[1200,128]{1,0:T(8,128)(2,1)S(1)} %get-tuple-element.45.refs_1_), channel_id=1, source_target_pairs={{0,192},{64,0},{128,64},{192,128},{1,193},{65,1},{129,65},{193,129... | collective-permute-start | bytes 921608 | tf_op jit(solution)/shard_map/ppermute | solution.py:353
  120.1 13.5 %copy-start.6 = (bf16[1200,128]{1,0:T(8,128)(2,1)}, bf16[1200,128]{1,0:T(8,128)(2,1)S(1)}, u32[]{:S(2)}) copy-start(bf16[1200,128]{1,0:T(8,128)(2,1)S(1)} %collective-permute-done.14.refs_2_) | copy-start | bytes 921604
  120.1 12.6 %collective-permute-start.21 = (bf16[1200,128]{1,0:T(8,128)(2,1)S(1)}, bf16[1200,128]{1,0:T(8,128)(2,1)S(1)}, u32[]{:S(2)}, u32[]{:S(2)}) collective-permute-start(bf16[1200,128]{1,0:T(8,128)(2,1)S(1)} %collective-permute-done.14.refs_2_), channel_id=1, source_target_pairs={{0,192},{64,0},{128,64},{192,128},{1,193},{65,1},{129,65},{193,129... | collective-permute-start | bytes 921608 | tf_op jit(solution)/shard_map/ppermute | solution.py:353
  120.7 12.0 %collective-permute-start.22 = (bf16[1200,128]{1,0:T(8,128)(2,1)S(1)}, bf16[1200,128]{1,0:T(8,128)(2,1)S(1)}, u32[]{:S(2)}, u32[]{:S(2)}) collective-permute-start(bf16[1200,128]{1,0:T(8,128)(2,1)S(1)} %collective-permute-done.17.refs_7_), channel_id=1, source_target_pairs={{0,64},{64,128},{128,192},{192,0},{1,65},{65,129},{129,193},{193,1... | collective-permute-start | bytes 921608 | tf_op jit(solution)/shard_map/ppermute | solution.py:353
  123.5 5.6 %collective-permute-start.18 = (bf16[1,32,1280]{2,1,0:T(8,128)(2,1)S(1)}, bf16[1,32,1280]{2,1,0:T(8,128)(2,1)S(1)}, u32[]{:S(2)}, u32[]{:S(2)}) collective-permute-start(bf16[1,32,1280]{2,1,0:T(8,128)(2,1)S(1)} %get-tuple-element.67), channel_id=1, source_target_pairs={{0,6},{2,0},{4,2},{6,4},{1,7},{3,1},{5,3},{7,5},{8,14},{10,8},{12,... | collective-permute-start | bytes 245768 | tf_op jit(solution)/shard_map/ppermute | solution.py:375
  125.4 8.9 %copy-start.8 = (bf16[1200,128]{1,0:T(8,128)(2,1)}, bf16[1200,128]{1,0:T(8,128)(2,1)S(1)}, u32[]{:S(2)}) copy-start(bf16[1200,128]{1,0:T(8,128)(2,1)S(1)} %collective-permute-done.15.refs_6_) | copy-start | bytes 921604
  125.4 6.1 %collective-permute-start.19 = (bf16[1,32,1280]{2,1,0:T(8,128)(2,1)S(1)}, bf16[1,32,1280]{2,1,0:T(8,128)(2,1)S(1)}, u32[]{:S(2)}, u32[]{:S(2)}) collective-permute-start(bf16[1,32,1280]{2,1,0:T(8,128)(2,1)S(1)} %get-tuple-element.66), channel_id=1, source_target_pairs={{0,4},{2,6},{4,0},{6,2},{1,5},{3,7},{5,1},{7,3},{8,12},{10,14},{12... | collective-permute-start | bytes 245768 | tf_op jit(solution)/shard_map/ppermute | solution.py:375
  127.0 1.9 %copy-start.10 = (bf16[1200,128]{1,0:T(8,128)(2,1)}, bf16[1200,128]{1,0:T(8,128)(2,1)S(1)}, u32[]{:S(2)}) copy-start(bf16[1200,128]{1,0:T(8,128)(2,1)S(1)} %collective-permute-done.16.refs_3_) | copy-start | bytes 921604
  127.0 5.7 %collective-permute-start.20 = (bf16[1,32,1280]{2,1,0:T(8,128)(2,1)S(1)}, bf16[1,32,1280]{2,1,0:T(8,128)(2,1)S(1)}, u32[]{:S(2)}, u32[]{:S(2)}) collective-permute-start(bf16[1,32,1280]{2,1,0:T(8,128)(2,1)S(1)} %get-tuple-element.65), channel_id=1, source_target_pairs={{0,2},{2,4},{4,6},{6,0},{1,3},{3,5},{5,7},{7,1},{8,10},{10,12},{12... | collective-permute-start | bytes 245768 | tf_op jit(solution)/shard_map/ppermute | solution.py:375
  132.7 2.2 %copy-start.12 = (bf16[1200,128]{1,0:T(8,128)(2,1)}, bf16[1200,128]{1,0:T(8,128)(2,1)S(1)}, u32[]{:S(2)}) copy-start(bf16[1200,128]{1,0:T(8,128)(2,1)S(1)} %collective-permute-done.21.refs_4_) | copy-start | bytes 921604
  132.7 1.5 copy-start.14
  133.5 2.7 %collective-permute-start.23 = (bf16[3,4,32,1280]{3,2,1,0:T(8,128)(2,1)S(1)}, bf16[3,4,32,1280]{3,2,1,0:T(8,128)(2,1)S(1)}, u32[]{:S(2)}, u32[]{:S(2)}) collective-permute-start(bf16[3,4,32,1280]{3,2,1,0:T(8,128)(2,1)S(1)} %pad_maximum_fusion), channel_id=1, source_target_pairs={{0,1},{1,0},{2,3},{3,2},{4,5},{5,4},{6,7},{7,6},{8,9},{9,8},{10,11... | collective-permute-start | bytes 2949128 | tf_op jit(solution)/shard_map/ppermute | solution.py:370
  136.4 22.8 %copy-start.3 = (bf16[1200,128]{1,0:T(8,128)(2,1)S(1)}, bf16[1200,128]{1,0:T(8,128)(2,1)}, u32[]{:S(2)}) copy-start(bf16[1200,128]{1,0:T(8,128)(2,1)} %copy-done.2) | copy-start | bytes 921604
  136.4 22.8 %copy-start.5 = (bf16[1200,128]{1,0:T(8,128)(2,1)S(1)}, bf16[1200,128]{1,0:T(8,128)(2,1)}, u32[]{:S(2)}) copy-start(bf16[1200,128]{1,0:T(8,128)(2,1)} %copy-done.4) | copy-start | bytes 921604
  136.4 22.8 %copy-start.7 = (bf16[1200,128]{1,0:T(8,128)(2,1)S(1)}, bf16[1200,128]{1,0:T(8,128)(2,1)}, u32[]{:S(2)}) copy-start(bf16[1200,128]{1,0:T(8,128)(2,1)} %copy-done.6) | copy-start | bytes 921604
  136.4 22.8 %copy-start.9 = (bf16[1200,128]{1,0:T(8,128)(2,1)S(1)}, bf16[1200,128]{1,0:T(8,128)(2,1)}, u32[]{:S(2)}) copy-start(bf16[1200,128]{1,0:T(8,128)(2,1)} %copy-done.8) | copy-start | bytes 921604
  136.5 22.8 %copy-start.11 = (bf16[1200,128]{1,0:T(8,128)(2,1)S(1)}, bf16[1200,128]{1,0:T(8,128)(2,1)}, u32[]{:S(2)}) copy-start(bf16[1200,128]{1,0:T(8,128)(2,1)} %copy-done.10) | copy-start | bytes 921604
  136.5 22.8 %copy-start.13 = (bf16[1200,128]{1,0:T(8,128)(2,1)S(1)}, bf16[1200,128]{1,0:T(8,128)(2,1)}, u32[]{:S(2)}) copy-start(bf16[1200,128]{1,0:T(8,128)(2,1)} %copy-done.12) | copy-start | bytes 921604
  136.5 22.8 %copy-start.15 = (bf16[1200,128]{1,0:T(8,128)(2,1)S(1)}, bf16[1200,128]{1,0:T(8,128)(2,1)}, u32[]{:S(2)}) copy-start(bf16[1200,128]{1,0:T(8,128)(2,1)} %copy-done.14) | copy-start | bytes 921604
  136.5 8.9 %collective-permute-start.24 = (bf16[3,32,1280]{2,1,0:T(8,128)(2,1)S(1)}, bf16[3,32,1280]{2,1,0:T(8,128)(2,1)S(1)}, u32[]{:S(2)}, u32[]{:S(2)}) collective-permute-start(bf16[3,32,1280]{2,1,0:T(8,128)(2,1)S(1)} %get-tuple-element.62), channel_id=1, source_target_pairs={{0,6},{2,0},{4,2},{6,4},{1,7},{3,1},{5,3},{7,5},{8,14},{10,8},{12,... | collective-permute-start | bytes 737288 | tf_op jit(solution)/shard_map/ppermute | solution.py:375
  138.0 10.4 %collective-permute-start.25 = (bf16[3,32,1280]{2,1,0:T(8,128)(2,1)S(1)}, bf16[3,32,1280]{2,1,0:T(8,128)(2,1)S(1)}, u32[]{:S(2)}, u32[]{:S(2)}) collective-permute-start(bf16[3,32,1280]{2,1,0:T(8,128)(2,1)S(1)} %get-tuple-element.64), channel_id=1, source_target_pairs={{0,4},{2,6},{4,0},{6,2},{1,5},{3,7},{5,1},{7,3},{8,12},{10,14},{12... | collective-permute-start | bytes 737288 | tf_op jit(solution)/shard_map/ppermute | solution.py:375
  139.1 13.4 %collective-permute-start.26 = (bf16[3,32,1280]{2,1,0:T(8,128)(2,1)S(1)}, bf16[3,32,1280]{2,1,0:T(8,128)(2,1)S(1)}, u32[]{:S(2)}, u32[]{:S(2)}) collective-permute-start(bf16[3,32,1280]{2,1,0:T(8,128)(2,1)S(1)} %get-tuple-element.63), channel_id=1, source_target_pairs={{0,2},{2,4},{4,6},{6,0},{1,3},{3,5},{5,7},{7,1},{8,10},{10,12},{12... | collective-permute-start | bytes 737288 | tf_op jit(solution)/shard_map/ppermute | solution.py:375
  153.6 17.4 %all-to-all-start.3 = ((bf16[32,4,1280]{2,1,0:T(4,128)(2,1)}), bf16[32,4,1280]{2,1,0:T(4,128)(2,1)S(1)}, u32[]{:S(2)}, u32[]{:S(2)}) async-start(bf16[32,4,1280]{2,1,0:T(4,128)(2,1)} %reshape.197), calls=%async_computation.3 | async-start | bytes 655360 | tf_op jit(solution)/shard_map/all_to_all | solution.py:390
  159.3 1.7 %copy-start.17 = (bf16[4,256,1280]{2,1,0:T(8,128)(2,1)S(1)}, bf16[4,256,1280]{2,1,0:T(8,128)(2,1)}, u32[]{:S(2)}) copy-start(bf16[4,256,1280]{2,1,0:T(8,128)(2,1)} %copy-done.16) | copy-start | bytes 7864324

commit v6 on v5

--- a/solution.py
+++ b/solution.py
@@ -222,38 +222,60 @@
     )
 
 
-def statistics(own, parts, teacher, chosen):
-    def kernel(own_ref, a0, a1, b0, b1, teacher_ref, chosen_ref, logits_ref, sums_ref):
-        def first(rows, i, tops):
-            arrived = jnp.concatenate(
-                [decode(a0[rows, :]) + decode(a1[rows, :]), decode(b0[rows, :]) + decode(b1[rows, :])],
-                axis=1,
-            )
-            student = jnp.where(valid(i), own_ref[rows, :] + arrived, far_below)
+def prepared(own, parts, teacher):
+    def kernel(own_ref, near_ref, far_ref, teacher_ref, base_ref, rows_ref):
+        def first(rows, i, top):
+            arrived = jnp.concatenate([decode(near_ref[rows, :]), decode(far_ref[rows, :])], axis=1)
+            base_ref[rows, :] = own_ref[rows, :] + arrived
             taught = jnp.where(valid(i), teacher_ref[rows, :], far_below)
+            return jnp.maximum(top, folded(taught, jnp.max))
+
+        top = chunks(CHUNK, first, jnp.full((8, SPAN), far_below, jnp.float32))
+        top = jnp.max(top, axis=0, keepdims=True)
+
+        def second(rows, i, total):
+            taught = jnp.where(valid(i), teacher_ref[rows, :] - top, far_below)
+            return total + folded(jnp.exp(taught), jnp.sum)
+
+        total = chunks(CHUNK, second, jnp.zeros((8, SPAN), jnp.float32))
+        whole_sum = top + jnp.log(jnp.sum(total, axis=0, keepdims=True))
+        rows_ref[...] = jnp.concatenate([top] * 4 + [whole_sum] * 4, axis=0)
+
+    return streamed(
+        kernel,
+        [((PADDED, SPAN), jnp.float32), ((8, SPAN), jnp.float32)],
+        40 * PADDED * SPAN,
+        own,
+        *parts,
+        teacher,
+    )
+
+
+def statistics(base, parts, teacher, taught_rows, chosen):
+    def kernel(base_ref, near_ref, far_ref, teacher_ref, taught_ref, chosen_ref, logits_ref, sums_ref):
+        def first(rows, i, top):
+            arrived = jnp.concatenate([decode(near_ref[rows, :]), decode(far_ref[rows, :])], axis=1)
+            student = jnp.where(valid(i), base_ref[rows, :] + arrived, far_below)
             logits_ref[rows, :] = student
-            return (
-                jnp.maximum(tops[0], folded(student, jnp.max)),
-                jnp.maximum(tops[1], folded(taught, jnp.max)),
-            )
-
-        lowest = jnp.full((8, SPAN), far_below, jnp.float32)
-        top_s, top_t = chunks(CHUNK, first, (lowest, lowest))
+            return jnp.maximum(top, folded(student, jnp.max))
+
+        top_s = chunks(CHUNK, first, jnp.full((8, SPAN), far_below, jnp.float32))
         top_s = jnp.max(top_s, axis=0, keepdims=True)
-        top_t = jnp.max(top_t, axis=0, keepdims=True)
+        top_t = taught_ref[0:1, :]
 
         def second(rows, i, sums):
             s = logits_ref[rows, :] - top_s
             t = jnp.where(valid(i), teacher_ref[rows, :] - top_t, far_below)
-            terms = (s, t, alpha_power * t + beta_power * s, joint_power * s)
+            terms = (s, alpha_power * t + beta_power * s, joint_power * s)
             return tuple(so_far + folded(jnp.exp(term), jnp.sum) for so_far, term in zip(sums, terms))
 
-        sums = chunks(CHUNK, second, (jnp.zeros((8, SPAN), jnp.float32),) * 4)
-        tops = (top_s, top_t, alpha_power * top_t + beta_power * top_s, joint_power * top_s)
+        sums = chunks(CHUNK, second, (jnp.zeros((8, SPAN), jnp.float32),) * 3)
+        tops = (top_s, alpha_power * top_t + beta_power * top_s, joint_power * top_s)
         rows = [
             top + jnp.log(jnp.maximum(jnp.sum(total, axis=0, keepdims=True), smallest))
             for top, total in zip(tops, sums)
         ]
+        rows = [rows[0], taught_ref[4:5, :], rows[1], rows[2]]
         rows = exact(jnp.concatenate(rows + rows, axis=0), chosen_ref[...], ((1,), (1,)))
         packed = jnp.concatenate([rows[:4, :HALF], rows[:4, HALF:]], axis=0)
         sums_ref[...] = jnp.broadcast_to(packed[None], sums_ref.shape)
@@ -262,9 +284,10 @@
         kernel,
         [((PADDED, SPAN), jnp.float32), ((NZ * NY * NC, 8, HALF), jnp.float32)],
         100 * PADDED * SPAN,
-        own,
+        base,
         *parts,
         teacher,
+        taught_rows,
         chosen,
     )
 
@@ -345,7 +368,8 @@
     summed = added((near1, far3), relay)
     summed = [sent(summed[0], 1), sent(summed[1], -1)]
     taught = gather_teacher(taught, chosen)
-    logits, sums = statistics(own, (direct[0], summed[0], direct[1], summed[1]), taught, chosen)
+    base, taught_rows = prepared(own, direct, taught)
+    logits, sums = statistics(base, summed, taught, taught_rows, chosen)
     every = lax.all_to_all(sums, VOCAB, 0, 0, tiled=True)
     near, far = gradients(every, logits, taught, chosen)
 

time: 174 us -> 173 us (level)
  waiting for transfers between devices: 47.1 us -> 42.5 us
  starting transfers between devices: 51.9 us -> 55.3 us
    ppermute x6, waiting for transfers between devices: 8.07 us -> 3.04 us  [sent(): return lax.ppermute(value, 'x', shift(NX, by))]
    ppermute x6, starting transfers between devices: 7.29 us -> 9.43 us  [passed(): return lax.ppermute(value, 'x', shift(NX, by))]
    pallas_call x2 -> x3, Pallas kernels: 4.96 us -> 6.13 us  [streamed(): pl.pallas_call(kernel, grid=(1,), in_specs=[whole(arg.shape) for arg in a...]
  transfers between devices with their start and end apart: 30 -> 30, of which waited for: 17 -> 16; matrix products, arithmetic and copies ran while one was open for 10% -> 10% of each run, Pallas kernels for 9% -> 10%
where the time goes in v6:
time: 173 us; the launch traced here: 171 us
  starting transfers between devices  55.3 us (32%)
  waiting for transfers between devices  42.5 us (25%)
  blocking collectives  22.8 us (13%)
  Pallas kernels  20.8 us (12%)
  local copies, waits for them, and re-layouts  15.8 us (9%)
  matrix products  6.54 us (4%)
  other arithmetic  5.78 us (3%)
    all_to_all x1, blocking collectives, body(): every = lax.all_to_all(sums, VOCAB, 0, 0, tiled=True)  22.8 us
    ppermute x6, waiting for transfers between devices, along(): lax.ppermute(part, 'y', shift(NY, -by))  16.4 us
    all_to_all x1, starting transfers between devices, gather_hidden(): got = lax.all_to_all(spread, ('x', 'z'), 0, 0, tiled=True)  11.6 us
    ppermute x6, starting transfers between devices, passed(): return lax.ppermute(value, 'x', shift(NX, by))  9.43 us
    ppermute x6, starting transfers between devices, sent(): return lax.ppermute(value, 'x', shift(NX, by))  8.58 us
    ppermute x6, waiting for transfers between devices, passed(): return lax.ppermute(value, 'x', shift(NX, by))  7.49 us
    ppermute x6, starting transfers between devices, along(): lax.ppermute(part, 'y', shift(NY, -by))  7.37 us
    pallas_call x3, Pallas kernels, streamed(): pl.pallas_call(kernel, grid=(1,), in_specs=[whole(arg.shape) for arg in a...  6.13 us
  transfers between devices with their start and end apart: 30, of which 16 were waited for; matrix products, arithmetic and copies ran while one was open for 10% of the time, Pallas kernels for 10%

profile of v6, /device:TPU:6, one launch (start us, length us, event | category | flops | bytes accessed | tf_op | source)
XLA Modules:
  0.0 170.6 jit_solution(2885260189293487104)
XLA Ops:
  0.6 0.8 reshape.192
  2.3 11.6 %all-to-all-start = ((bf16[32,4,1280]{2,1,0:T(4,128)(2,1)}), bf16[32,4,1280]{2,1,0:T(4,128)(2,1)S(1)}, u32[]{:S(2)}, u32[]{:S(2)}) async-start(bf16[32,4,1280]{2,1,0:T(4,128)(2,1)} %bitcast.1), calls=%async_computation | async-start | bytes 655360 | tf_op jit(solution)/shard_map/all_to_all | solution.py:39
  14.7 2.1 %reshape.195 = bf16[4,64,1187]{2,1,0:T(8,128)(2,1)S(1)} reshape(bf16[4,75968]{1,0:T(4,128)(2,1)} %param.5) | data formatting | bytes 1215488 | tf_op jit(solution)/shard_map/reshape | solution.py:63
  16.9 1.3 copy.19
  18.2 2.1 %pad.9.head_ref = bf16[1200,1280]{1,0:T(8,128)(2,1)S(1)} pad(bf16[1187,1280]{1,0:T(8,128)(2,1)} %bitcast.70, bf16[]{:T(256)} %constant.96.clone.1), padding=0_13x0_0 | pad | bytes 6110722 | tf_op jit(solution)/shard_map/jit(_pad)/pad | solution.py:354
  20.3 2.3 %maximum_bitcast_fusion = bf16[64,4,1200]{2,1,0:T(4,128)(2,1)} fusion(bf16[4,64,13]{2,0,1:T(4,128)(2,1)S(1)} %broadcast_in_dim.5, bf16[4,64,1187]{2,0,1:T(4,128)(2,1)} %copy.19), kind=kLoop, calls=%fused_computation.8 | loop fusion | flops 1228800 | bytes 1228800 | tf_op jit(solution)/shard_map/transpose | solution.py:66
  22.6 2.9 %all-to-all-done = bf16[32,4,1280]{2,1,0:T(4,128)(2,1)S(1)} async-done(((bf16[32,4,1280]{2,1,0:T(4,128)(2,1)}), bf16[32,4,1280]{2,1,0:T(4,128)(2,1)S(1)}, u32[]{:S(2)}, u32[]{:S(2)}) %all-to-all-start) | async-done | bytes 327712 | tf_op jit(solution)/shard_map/all_to_all | solution.py:39
  26.3 1.1 fusion.5.refs_0_
  27.5 1.7 collective-permute-start
  29.1 2.9 %collective-permute-start.1 = (bf16[4,32,1280]{2,1,0:T(8,128)(2,1)S(1)}, bf16[4,32,1280]{2,1,0:T(8,128)(2,1)}, u32[]{:S(2)}, u32[]{:S(2)}) collective-permute-start(bf16[4,32,1280]{2,1,0:T(8,128)(2,1)S(1)} %fusion.5.refs_0_), channel_id=1, source_target_pairs={{0,4},{2,6},{4,0},{6,2},{1,5},{3,7},{5,1},{7,3},{8,12},{10,14},{12... | collective-permute-start | bytes 983048 | tf_op jit(solution)/shard_map/ppermute | solution.py:42
  32.0 1.3 collective-permute-start.2
  33.4 5.5 %all-to-all-start.1 = ((bf16[64,4,1200]{2,1,0:T(4,128)(2,1)}), bf16[64,4,1200]{2,1,0:T(4,128)(2,1)}, u32[]{:S(2)}, u32[]{:S(2)}) async-start(bf16[64,4,1200]{2,1,0:T(4,128)(2,1)} %maximum_bitcast_fusion), calls=%async_computation.1 | async-start | bytes 1310720 | tf_op jit(solution)/shard_map/all_to_all | solution.py:70
  39.4 5.0 %collective-permute-done.1.refs_2_ = bf16[4,32,1280]{2,1,0:T(8,128)(2,1)} collective-permute-done((bf16[4,32,1280]{2,1,0:T(8,128)(2,1)S(1)}, bf16[4,32,1280]{2,1,0:T(8,128)(2,1)}, u32[]{:S(2)}, u32[]{:S(2)}) %collective-permute-start.1) | collective-permute-done | bytes 327712 | tf_op jit(solution)/shard_map/ppermute | solution.py:42
  45.0 1.5 collective-permute-done.5.refs_6_
  46.9 2.6 %shard_map.61 = (bf16[1200,128]{1,0:T(8,128)(2,1)S(1)}, bf16[1200,128]{1,0:T(8,128)(2,1)S(1)}) custom-call(bf16[1200,1280]{1,0:T(8,128)(2,1)S(1)} %pad.9.head_ref, bf16[4,32,1280]{2,1,0:T(8,128)(2,1)S(1)} %fusion.5.refs_0_, bf16[4,32,1280]{2,1,0:T(8,128)(2,1)} %collective-permute-done.refs_1_, bf16[4,32,1280]{2,1,0:T(8,128)(2,1)} %collective-permute-done.1.refs_2_, ...), custom_call_target="tpu_custom_call" | custom-call | flops 786432000 | bytes 1000000 | tf_op jit(solution)/shard_map/pallas_call | solution.py:100
  50.0 2.8 %collective-permute-start.9 = (bf16[1200,128]{1,0:T(8,128)(2,1)S(1)}, bf16[1200,128]{1,0:T(8,128)(2,1)S(1)}, u32[]{:S(2)}, u32[]{:S(2)}) collective-permute-start(bf16[1200,128]{1,0:T(8,128)(2,1)S(1)} %get-tuple-element.41), channel_id=1, source_target_pairs={{0,64},{64,128},{128,192},{192,0},{1,65},{65,129},{129,193},{193,1... | collective-permute-start | bytes 921608 | tf_op jit(solution)/shard_map/ppermute | solution.py:362
  52.8 5.6 %shard_map.59 = (bf16[4,256,1280]{2,1,0:T(8,128)(2,1)S(1)}, bf16[1200,128]{1,0:T(8,128)(2,1)}, bf16[1200,128]{1,0:T(8,128)(2,1)}, f32[1200,128]{1,0:T(8,128)S(1)...) custom-call(bf16[1200,1280]{1,0:T(8,128)(2,1)S(1)} %pad.9.head_ref, bf16[4,32,1280]{2,1,0:T(8,128)(2,1)S(1)} %fusion.5.refs_0_, ...), custom_call_target="tpu_custom_call" | custom-call | flops 2359296000 | bytes 4000000 | tf_op jit(solution)/shard_map/pallas_call | solution.py:186
  58.4 1.5 copy-done.16
  59.9 3.2 %collective-permute-start.8 = (bf16[1200,128]{1,0:T(8,128)(2,1)}, bf16[1200,128]{1,0:T(8,128)(2,1)}, u32[]{:S(2)}, u32[]{:S(2)}) collective-permute-start(bf16[1200,128]{1,0:T(8,128)(2,1)} %get-tuple-element.36), channel_id=1, source_target_pairs={{0,64},{64,128},{128,192},{192,0},{1,65},{65,129},{129,193},{193,1... | collective-permute-start | bytes 921608 | tf_op jit(solution)/shard_map/ppermute | solution.py:362
  63.2 1.5 shard_map.62
  64.7 2.0 %collective-permute-start.12 = (bf16[1200,128]{1,0:T(8,128)(2,1)}, bf16[1200,128]{1,0:T(8,128)(2,1)}, u32[]{:S(2)}, u32[]{:S(2)}) collective-permute-start(bf16[1200,128]{1,0:T(8,128)(2,1)} %get-tuple-element.44), channel_id=1, source_target_pairs={{0,192},{64,0},{128,64},{192,128},{1,193},{65,1},{129,65},{193,129... | collective-permute-start | bytes 921608 | tf_op jit(solution)/shard_map/ppermute | solution.py:362
  66.7 2.2 %reshape.196 = bf16[256,1200]{1,0:T(8,128)(2,1)} reshape(bf16[64,4,1200]{2,1,0:T(4,128)(2,1)} %all-to-all-done.1) | data formatting | bytes 1228800 | tf_op jit(solution)/shard_map/reshape | solution.py:70
  68.9 1.5 fusion.7.teacher_ref
  70.4 1.2 collective-permute-done.7.near_ref
  71.6 1.3 copy-done.1
  72.9 2.1 %shard_map.60 = (f32[1200,256]{1,0:T(8,128)S(1)}, f32[8,256]{1,0:T(8,128)S(1)}) custom-call(f32[1200,256]{1,0:T(8,128)S(1)} %copy-done.1, bf16[1200,128]{1,0:T(8,128)(2,1)} %collective-permute-done.7.near_ref, bf16[1200,128]{1,0:T(8,128)(2,1)} %collective-permute-done.8.far_ref, f32[1200,256]{1,0:T(8,128)S(1)} %fusion.7.teacher_ref), custom_call_target="tpu_custom_call" | custom-call | flops 12288000 | bytes 5000000 | tf_op jit(solution)/shard_map/pallas_call | solution.py:116
  75.0 1.1 collective-permute-done.11.near_ref
  76.8 2.9 %shard_map.63 = (f32[1200,256]{1,0:T(8,128)S(1)}, f32[64,8,128]{2,1,0:T(8,128)S(1)}) custom-call(f32[1200,256]{1,0:T(8,128)S(1)} %get-tuple-element.38.base_ref, bf16[1200,128]{1,0:T(8,128)(2,1)} %collective-permute-done.11.near_ref, bf16[1200,128]{1,0:T(8,128)(2,1)} %collective-permute-done.12.far_ref, f32[1200,256]{1,0:T(8,128)S(1)} %fusion.7.teacher_ref, ...), custom_call_target="tpu_custom_call" | custom-call | flops 30720000 | bytes 5000000 | tf_op jit(solution)/shard_map/pallas_call | solution.py:116
  79.7 22.8 %all_to_all.20.every_ref = f32[64,8,128]{2,1,0:T(8,128)S(1)} all-to-all(f32[64,8,128]{2,1,0:T(8,128)S(1)} %get-tuple-element.46), channel_id=1, replica_groups=mesh['x'=4,'z'=8,'y'=4,'c'=2] {'z','y','c'}, dimensions={0} | all-to-all | bytes 524288 | tf_op jit(solution)/shard_map/all_to_all | solution.py:373
  102.5 1.1 shard_map.64
  104.7 3.0 %collective-permute-start.17 = (bf16[1200,128]{1,0:T(8,128)(2,1)S(1)}, bf16[1200,128]{1,0:T(8,128)(2,1)S(1)}, u32[]{:S(2)}, u32[]{:S(2)}) collective-permute-start(bf16[1200,128]{1,0:T(8,128)(2,1)S(1)} %get-tuple-element.49.refs_1_), channel_id=1, source_target_pairs={{0,64},{64,128},{128,192},{192,0},{1,65},{65,129},{129,193},{193,1... | collective-permute-start | bytes 921608 | tf_op jit(solution)/shard_map/ppermute | solution.py:377
  107.6 3.2 %collective-permute-start.15 = (bf16[1200,128]{1,0:T(8,128)(2,1)S(1)}, bf16[1200,128]{1,0:T(8,128)(2,1)S(1)}, u32[]{:S(2)}, u32[]{:S(2)}) collective-permute-start(bf16[1200,128]{1,0:T(8,128)(2,1)S(1)} %get-tuple-element.48.refs_0_), channel_id=1, source_target_pairs={{0,64},{64,128},{128,192},{192,0},{1,65},{65,129},{129,193},{193,1... | collective-permute-start | bytes 921608 | tf_op jit(solution)/shard_map/ppermute | solution.py:377
  111.5 7.4 %collective-permute-done.14.refs_2_ = bf16[1200,128]{1,0:T(8,128)(2,1)S(1)} collective-permute-done((bf16[1200,128]{1,0:T(8,128)(2,1)S(1)}, bf16[1200,128]{1,0:T(8,128)(2,1)S(1)}, u32[]{:S(2)}, u32[]{:S(2)}) %collective-permute-start.14) | collective-permute-done | bytes 307232 | tf_op jit(solution)/shard_map/ppermute | solution.py:377
  119.0 3.2 %collective-permute-start.22 = (bf16[1200,128]{1,0:T(8,128)(2,1)S(1)}, bf16[1200,128]{1,0:T(8,128)(2,1)S(1)}, u32[]{:S(2)}, u32[]{:S(2)}) collective-permute-start(bf16[1200,128]{1,0:T(8,128)(2,1)S(1)} %collective-permute-done.17.refs_7_), channel_id=1, source_target_pairs={{0,64},{64,128},{128,192},{192,0},{1,65},{65,129},{129,193},{193,1... | collective-permute-start | bytes 921608 | tf_op jit(solution)/shard_map/ppermute | solution.py:377
  122.3 1.9 %collective-permute-start.18 = (bf16[1,32,1280]{2,1,0:T(8,128)(2,1)S(1)}, bf16[1,32,1280]{2,1,0:T(8,128)(2,1)S(1)}, u32[]{:S(2)}, u32[]{:S(2)}) collective-permute-start(bf16[1,32,1280]{2,1,0:T(8,128)(2,1)S(1)} %get-tuple-element.71), channel_id=1, source_target_pairs={{0,6},{2,0},{4,2},{6,4},{1,7},{3,1},{5,3},{7,5},{8,14},{10,8},{12,... | collective-permute-start | bytes 245768 | tf_op jit(solution)/shard_map/ppermute | solution.py:399
  124.3 1.3 collective-permute-start.19
  127.6 2.7 %collective-permute-done.19 = bf16[1,32,1280]{2,1,0:T(8,128)(2,1)S(1)} collective-permute-done((bf16[1,32,1280]{2,1,0:T(8,128)(2,1)S(1)}, bf16[1,32,1280]{2,1,0:T(8,128)(2,1)S(1)}, u32[]{:S(2)}, u32[]{:S(2)}) %collective-permute-start.19) | collective-permute-done | bytes 81952 | tf_op jit(solution)/shard_map/ppermute | solution.py:399
  130.3 0.9 collective-permute-done.20
  135.1 1.8 %collective-permute-start.24 = (bf16[3,32,1280]{2,1,0:T(8,128)(2,1)S(1)}, bf16[3,32,1280]{2,1,0:T(8,128)(2,1)S(1)}, u32[]{:S(2)}, u32[]{:S(2)}) collective-permute-start(bf16[3,32,1280]{2,1,0:T(8,128)(2,1)S(1)} %get-tuple-element.66), channel_id=1, source_target_pairs={{0,6},{2,0},{4,2},{6,4},{1,7},{3,1},{5,3},{7,5},{8,14},{10,8},{12,... | collective-permute-start | bytes 737288 | tf_op jit(solution)/shard_map/ppermute | solution.py:399
  136.9 1.1 collective-permute-start.25
  138.6 5.3 %collective-permute-done.24 = bf16[3,32,1280]{2,1,0:T(8,128)(2,1)S(1)} collective-permute-done((bf16[3,32,1280]{2,1,0:T(8,128)(2,1)S(1)}, bf16[3,32,1280]{2,1,0:T(8,128)(2,1)S(1)}, u32[]{:S(2)}, u32[]{:S(2)}) %collective-permute-start.24) | collective-permute-done | bytes 245792 | tf_op jit(solution)/shard_map/ppermute | solution.py:399
  143.9 3.3 %collective-permute-done.25 = bf16[3,32,1280]{2,1,0:T(8,128)(2,1)S(1)} collective-permute-done((bf16[3,32,1280]{2,1,0:T(8,128)(2,1)S(1)}, bf16[3,32,1280]{2,1,0:T(8,128)(2,1)S(1)}, u32[]{:S(2)}, u32[]{:S(2)}) %collective-permute-start.25) | collective-permute-done | bytes 245792 | tf_op jit(solution)/shard_map/ppermute | solution.py:399
  147.3 4.1 %collective-permute-done.26 = bf16[3,32,1280]{2,1,0:T(8,128)(2,1)S(1)} collective-permute-done((bf16[3,32,1280]{2,1,0:T(8,128)(2,1)S(1)}, bf16[3,32,1280]{2,1,0:T(8,128)(2,1)S(1)}, u32[]{:S(2)}, u32[]{:S(2)}) %collective-permute-start.26) | collective-permute-done | bytes 245792 | tf_op jit(solution)/shard_map/ppermute | solution.py:399
  151.7 0.8 reshape.197
  152.5 5.6 %all-to-all-start.3 = ((bf16[32,4,1280]{2,1,0:T(4,128)(2,1)}), bf16[32,4,1280]{2,1,0:T(4,128)(2,1)S(1)}, u32[]{:S(2)}, u32[]{:S(2)}) async-start(bf16[32,4,1280]{2,1,0:T(4,128)(2,1)} %reshape.197), calls=%async_computation.3 | async-start | bytes 655360 | tf_op jit(solution)/shard_map/all_to_all | solution.py:414
  158.2 1.7 %copy-done.17 = bf16[4,256,1280]{2,1,0:T(8,128)(2,1)S(1)} copy-done((bf16[4,256,1280]{2,1,0:T(8,128)(2,1)S(1)}, bf16[4,256,1280]{2,1,0:T(8,128)(2,1)}, u32[]{:S(2)}) %copy-start.17) | copy-done | bytes 2621464
  159.9 5.0 %shard_map.65 = bf16[1187,1280]{1,0:T(8,128)(2,1)} custom-call(bf16[1200,128]{1,0:T(8,128)(2,1)S(1)} %copy-done.3, bf16[1200,128]{1,0:T(8,128)(2,1)S(1)} %copy-done.5, bf16[1200,128]{1,0:T(8,128)(2,1)S(1)} %copy-done.7, bf16[1200,128]{1,0:T(8,128)(2,1)S(1)} %copy-done.11, bf16[1200,128]{1,0:T(8,128)(2,1)S(1)} %copy-done.13, ...), custom_call_target="tpu_custom_call" | custom-call | flops 3145728000 | bytes 9000000 | tf_op jit(solution)/shard_map/pallas_call | solution.py:339
  164.9 5.0 %all-to-all-done.3 = bf16[32,4,1280]{2,1,0:T(4,128)(2,1)S(1)} async-done(((bf16[32,4,1280]{2,1,0:T(4,128)(2,1)}), bf16[32,4,1280]{2,1,0:T(4,128)(2,1)S(1)}, u32[]{:S(2)}, u32[]{:S(2)}) %all-to-all-start.3) | async-done | bytes 327712 | tf_op jit(solution)/shard_map/all_to_all | solution.py:414
  (93 shorter events, 14.6 us)
Async XLA Ops:
  2.3 23.3 %all-to-all-start = ((bf16[32,4,1280]{2,1,0:T(4,128)(2,1)}), bf16[32,4,1280]{2,1,0:T(4,128)(2,1)S(1)}, u32[]{:S(2)}, u32[]{:S(2)}) async-start(bf16[32,4,1280]{2,1,0:T(4,128)(2,1)} %bitcast.1), calls=%async_computation | async-start | bytes 655360 | tf_op jit(solution)/shard_map/all_to_all | solution.py:39
  27.5 11.6 %collective-permute-start = (bf16[4,32,1280]{2,1,0:T(8,128)(2,1)S(1)}, bf16[4,32,1280]{2,1,0:T(8,128)(2,1)}, u32[]{:S(2)}, u32[]{:S(2)}) collective-permute-start(bf16[4,32,1280]{2,1,0:T(8,128)(2,1)S(1)} %fusion.5.refs_0_), channel_id=1, source_target_pairs={{0,2},{2,4},{4,6},{6,0},{1,3},{3,5},{5,7},{7,1},{8,10},{10,12},{12... | collective-permute-start | bytes 983048 | tf_op jit(solution)/shard_map/ppermute | solution.py:42
  29.1 15.3 %collective-permute-start.1 = (bf16[4,32,1280]{2,1,0:T(8,128)(2,1)S(1)}, bf16[4,32,1280]{2,1,0:T(8,128)(2,1)}, u32[]{:S(2)}, u32[]{:S(2)}) collective-permute-start(bf16[4,32,1280]{2,1,0:T(8,128)(2,1)S(1)} %fusion.5.refs_0_), channel_id=1, source_target_pairs={{0,4},{2,6},{4,0},{6,2},{1,5},{3,7},{5,1},{7,3},{8,12},{10,14},{12... | collective-permute-start | bytes 983048 | tf_op jit(solution)/shard_map/ppermute | solution.py:42
  32.0 12.5 %collective-permute-start.2 = (bf16[4,32,1280]{2,1,0:T(8,128)(2,1)S(1)}, bf16[4,32,1280]{2,1,0:T(8,128)(2,1)}, u32[]{:S(2)}, u32[]{:S(2)}) collective-permute-start(bf16[4,32,1280]{2,1,0:T(8,128)(2,1)S(1)} %fusion.5.refs_0_), channel_id=1, source_target_pairs={{0,6},{2,0},{4,2},{6,4},{1,7},{3,1},{5,3},{7,5},{8,14},{10,8},{12,... | collective-permute-start | bytes 983048 | tf_op jit(solution)/shard_map/ppermute | solution.py:42
  33.4 33.3 %all-to-all-start.1 = ((bf16[64,4,1200]{2,1,0:T(4,128)(2,1)}), bf16[64,4,1200]{2,1,0:T(4,128)(2,1)}, u32[]{:S(2)}, u32[]{:S(2)}) async-start(bf16[64,4,1200]{2,1,0:T(4,128)(2,1)} %maximum_bitcast_fusion), calls=%async_computation.1 | async-start | bytes 1310720 | tf_op jit(solution)/shard_map/all_to_all | solution.py:70
  38.8 6.1 %collective-permute-start.3 = (bf16[4,32,1280]{2,1,0:T(8,128)(2,1)S(1)}, bf16[4,32,1280]{2,1,0:T(8,128)(2,1)}, u32[]{:S(2)}, u32[]{:S(2)}) collective-permute-start(bf16[4,32,1280]{2,1,0:T(8,128)(2,1)S(1)} %fusion.5.refs_0_), channel_id=1, source_target_pairs={{0,1},{1,0},{2,3},{3,2},{4,5},{5,4},{6,7},{7,6},{8,9},{9,8},{10,11... | collective-permute-start | bytes 983048 | tf_op jit(solution)/shard_map/ppermute | solution.py:43
  39.0 5.9 %collective-permute-start.4 = (bf16[4,32,1280]{2,1,0:T(8,128)(2,1)}, bf16[4,32,1280]{2,1,0:T(8,128)(2,1)}, u32[]{:S(2)}, u32[]{:S(2)}) collective-permute-start(bf16[4,32,1280]{2,1,0:T(8,128)(2,1)} %collective-permute-done.refs_1_), channel_id=1, source_target_pairs={{0,1},{1,0},{2,3},{3,2},{4,5},{5,4},{6,7},{7,6},{8,9},{9,8},{10,11... | collective-permute-start | bytes 983048 | tf_op jit(solution)/shard_map/ppermute | solution.py:43
  44.5 2.0 %collective-permute-start.5 = (bf16[4,32,1280]{2,1,0:T(8,128)(2,1)}, bf16[4,32,1280]{2,1,0:T(8,128)(2,1)}, u32[]{:S(2)}, u32[]{:S(2)}) collective-permute-start(bf16[4,32,1280]{2,1,0:T(8,128)(2,1)} %collective-permute-done.1.refs_2_), channel_id=1, source_target_pairs={{0,1},{1,0},{2,3},{3,2},{4,5},{5,4},{6,7},{7,6},{8,9},{9,8},{10,11... | collective-permute-start | bytes 983048 | tf_op jit(solution)/shard_map/ppermute | solution.py:43
  44.5 2.4 %collective-permute-start.6 = (bf16[4,32,1280]{2,1,0:T(8,128)(2,1)}, bf16[4,32,1280]{2,1,0:T(8,128)(2,1)}, u32[]{:S(2)}, u32[]{:S(2)}) collective-permute-start(bf16[4,32,1280]{2,1,0:T(8,128)(2,1)} %collective-permute-done.2.refs_3_), channel_id=1, source_target_pairs={{0,1},{1,0},{2,3},{3,2},{4,5},{5,4},{6,7},{7,6},{8,9},{9,8},{10,11... | collective-permute-start | bytes 983048 | tf_op jit(solution)/shard_map/ppermute | solution.py:43
  49.5 13.7 %collective-permute-start.10 = (bf16[1200,128]{1,0:T(8,128)(2,1)S(1)}, bf16[1200,128]{1,0:T(8,128)(2,1)S(1)}, u32[]{:S(2)}, u32[]{:S(2)}) collective-permute-start(bf16[1200,128]{1,0:T(8,128)(2,1)S(1)} %get-tuple-element.42), channel_id=1, source_target_pairs={{0,192},{64,0},{128,64},{192,128},{1,193},{65,1},{129,65},{193,129... | collective-permute-start | bytes 921608 | tf_op jit(solution)/shard_map/ppermute | solution.py:362
  50.0 13.1 %collective-permute-start.9 = (bf16[1200,128]{1,0:T(8,128)(2,1)S(1)}, bf16[1200,128]{1,0:T(8,128)(2,1)S(1)}, u32[]{:S(2)}, u32[]{:S(2)}) collective-permute-start(bf16[1200,128]{1,0:T(8,128)(2,1)S(1)} %get-tuple-element.41), channel_id=1, source_target_pairs={{0,64},{64,128},{128,192},{192,0},{1,65},{65,129},{129,193},{193,1... | collective-permute-start | bytes 921608 | tf_op jit(solution)/shard_map/ppermute | solution.py:362
  58.4 1.5 copy-start.16
  59.9 4.7 %copy-start = (f32[1200,256]{1,0:T(8,128)}, f32[1200,256]{1,0:T(8,128)S(1)}, u32[]{:S(2)}) copy-start(f32[1200,256]{1,0:T(8,128)S(1)} %get-tuple-element.34.own_ref) | copy-start | bytes 3686404
  59.9 11.7 %collective-permute-start.7 = (bf16[1200,128]{1,0:T(8,128)(2,1)}, bf16[1200,128]{1,0:T(8,128)(2,1)}, u32[]{:S(2)}, u32[]{:S(2)}) collective-permute-start(bf16[1200,128]{1,0:T(8,128)(2,1)} %get-tuple-element.35), channel_id=1, source_target_pairs={{0,192},{64,0},{128,64},{192,128},{1,193},{65,1},{129,65},{193,129... | collective-permute-start | bytes 921608 | tf_op jit(solution)/shard_map/ppermute | solution.py:362
  59.9 11.7 %collective-permute-start.8 = (bf16[1200,128]{1,0:T(8,128)(2,1)}, bf16[1200,128]{1,0:T(8,128)(2,1)}, u32[]{:S(2)}, u32[]{:S(2)}) collective-permute-start(bf16[1200,128]{1,0:T(8,128)(2,1)} %get-tuple-element.36), channel_id=1, source_target_pairs={{0,64},{64,128},{128,192},{192,0},{1,65},{65,129},{129,193},{193,1... | collective-permute-start | bytes 921608 | tf_op jit(solution)/shard_map/ppermute | solution.py:362
  64.6 11.4 %collective-permute-start.11 = (bf16[1200,128]{1,0:T(8,128)(2,1)}, bf16[1200,128]{1,0:T(8,128)(2,1)}, u32[]{:S(2)}, u32[]{:S(2)}) collective-permute-start(bf16[1200,128]{1,0:T(8,128)(2,1)} %get-tuple-element.43), channel_id=1, source_target_pairs={{0,64},{64,128},{128,192},{192,0},{1,65},{65,129},{129,193},{193,1... | collective-permute-start | bytes 921608 | tf_op jit(solution)/shard_map/ppermute | solution.py:362
  64.7 12.1 %collective-permute-start.12 = (bf16[1200,128]{1,0:T(8,128)(2,1)}, bf16[1200,128]{1,0:T(8,128)(2,1)}, u32[]{:S(2)}, u32[]{:S(2)}) collective-permute-start(bf16[1200,128]{1,0:T(8,128)(2,1)} %get-tuple-element.44), channel_id=1, source_target_pairs={{0,192},{64,0},{128,64},{192,128},{1,193},{65,1},{129,65},{193,129... | collective-permute-start | bytes 921608 | tf_op jit(solution)/shard_map/ppermute | solution.py:362
  71.6 1.3 copy-start.1
  103.7 7.9 %copy-start.2 = (bf16[1200,128]{1,0:T(8,128)(2,1)}, bf16[1200,128]{1,0:T(8,128)(2,1)S(1)}, u32[]{:S(2)}) copy-start(bf16[1200,128]{1,0:T(8,128)(2,1)S(1)} %get-tuple-element.48.refs_0_) | copy-start | bytes 921604
  103.7 7.9 %copy-start.4 = (bf16[1200,128]{1,0:T(8,128)(2,1)}, bf16[1200,128]{1,0:T(8,128)(2,1)S(1)}, u32[]{:S(2)}) copy-start(bf16[1200,128]{1,0:T(8,128)(2,1)S(1)} %get-tuple-element.49.refs_1_) | copy-start | bytes 921604
  104.3 17.9 %collective-permute-start.13 = (bf16[1,4,32,1280]{3,2,1,0:T(8,128)(2,1)S(1)}, bf16[1,4,32,1280]{3,2,1,0:T(8,128)(2,1)S(1)}, u32[]{:S(2)}, u32[]{:S(2)}) collective-permute-start(bf16[1,4,32,1280]{3,2,1,0:T(8,128)(2,1)S(1)} %bitcast.78), channel_id=1, source_target_pairs={{0,1},{1,0},{2,3},{3,2},{4,5},{5,4},{6,7},{7,6},{8,9},{9,8},{10,11... | collective-permute-start | bytes 983048 | tf_op jit(solution)/shard_map/ppermute | solution.py:394
  104.7 14.3 %collective-permute-start.17 = (bf16[1200,128]{1,0:T(8,128)(2,1)S(1)}, bf16[1200,128]{1,0:T(8,128)(2,1)S(1)}, u32[]{:S(2)}, u32[]{:S(2)}) collective-permute-start(bf16[1200,128]{1,0:T(8,128)(2,1)S(1)} %get-tuple-element.49.refs_1_), channel_id=1, source_target_pairs={{0,64},{64,128},{128,192},{192,0},{1,65},{65,129},{129,193},{193,1... | collective-permute-start | bytes 921608 | tf_op jit(solution)/shard_map/ppermute | solution.py:377
  107.6 11.3 %collective-permute-start.14 = (bf16[1200,128]{1,0:T(8,128)(2,1)S(1)}, bf16[1200,128]{1,0:T(8,128)(2,1)S(1)}, u32[]{:S(2)}, u32[]{:S(2)}) collective-permute-start(bf16[1200,128]{1,0:T(8,128)(2,1)S(1)} %get-tuple-element.48.refs_0_), channel_id=1, source_target_pairs={{0,192},{64,0},{128,64},{192,128},{1,193},{65,1},{129,65},{193,129... | collective-permute-start | bytes 921608 | tf_op jit(solution)/shard_map/ppermute | solution.py:377
  107.6 16.6 %collective-permute-start.15 = (bf16[1200,128]{1,0:T(8,128)(2,1)S(1)}, bf16[1200,128]{1,0:T(8,128)(2,1)S(1)}, u32[]{:S(2)}, u32[]{:S(2)}) collective-permute-start(bf16[1200,128]{1,0:T(8,128)(2,1)S(1)} %get-tuple-element.48.refs_0_), channel_id=1, source_target_pairs={{0,64},{64,128},{128,192},{192,0},{1,65},{65,129},{129,193},{193,1... | collective-permute-start | bytes 921608 | tf_op jit(solution)/shard_map/ppermute | solution.py:377
  110.9 14.7 %collective-permute-start.16 = (bf16[1200,128]{1,0:T(8,128)(2,1)S(1)}, bf16[1200,128]{1,0:T(8,128)(2,1)S(1)}, u32[]{:S(2)}, u32[]{:S(2)}) collective-permute-start(bf16[1200,128]{1,0:T(8,128)(2,1)S(1)} %get-tuple-element.49.refs_1_), channel_id=1, source_target_pairs={{0,192},{64,0},{128,64},{192,128},{1,193},{65,1},{129,65},{193,129... | collective-permute-start | bytes 921608 | tf_op jit(solution)/shard_map/ppermute | solution.py:377
  119.0 13.1 %copy-start.6 = (bf16[1200,128]{1,0:T(8,128)(2,1)}, bf16[1200,128]{1,0:T(8,128)(2,1)S(1)}, u32[]{:S(2)}) copy-start(bf16[1200,128]{1,0:T(8,128)(2,1)S(1)} %collective-permute-done.14.refs_2_) | copy-start | bytes 921604
  119.0 12.2 %collective-permute-start.21 = (bf16[1200,128]{1,0:T(8,128)(2,1)S(1)}, bf16[1200,128]{1,0:T(8,128)(2,1)S(1)}, u32[]{:S(2)}, u32[]{:S(2)}) collective-permute-start(bf16[1200,128]{1,0:T(8,128)(2,1)S(1)} %collective-permute-done.14.refs_2_), channel_id=1, source_target_pairs={{0,192},{64,0},{128,64},{192,128},{1,193},{65,1},{129,65},{193,129... | collective-permute-start | bytes 921608 | tf_op jit(solution)/shard_map/ppermute | solution.py:377
  119.0 12.2 %collective-permute-start.22 = (bf16[1200,128]{1,0:T(8,128)(2,1)S(1)}, bf16[1200,128]{1,0:T(8,128)(2,1)S(1)}, u32[]{:S(2)}, u32[]{:S(2)}) collective-permute-start(bf16[1200,128]{1,0:T(8,128)(2,1)S(1)} %collective-permute-done.17.refs_7_), channel_id=1, source_target_pairs={{0,64},{64,128},{128,192},{192,0},{1,65},{65,129},{129,193},{193,1... | collective-permute-start | bytes 921608 | tf_op jit(solution)/shard_map/ppermute | solution.py:377
  122.3 5.2 %collective-permute-start.18 = (bf16[1,32,1280]{2,1,0:T(8,128)(2,1)S(1)}, bf16[1,32,1280]{2,1,0:T(8,128)(2,1)S(1)}, u32[]{:S(2)}, u32[]{:S(2)}) collective-permute-start(bf16[1,32,1280]{2,1,0:T(8,128)(2,1)S(1)} %get-tuple-element.71), channel_id=1, source_target_pairs={{0,6},{2,0},{4,2},{6,4},{1,7},{3,1},{5,3},{7,5},{8,14},{10,8},{12,... | collective-permute-start | bytes 245768 | tf_op jit(solution)/shard_map/ppermute | solution.py:399
  124.3 8.5 %copy-start.8 = (bf16[1200,128]{1,0:T(8,128)(2,1)}, bf16[1200,128]{1,0:T(8,128)(2,1)S(1)}, u32[]{:S(2)}) copy-start(bf16[1200,128]{1,0:T(8,128)(2,1)S(1)} %collective-permute-done.15.refs_6_) | copy-start | bytes 921604
  124.3 6.0 %collective-permute-start.19 = (bf16[1,32,1280]{2,1,0:T(8,128)(2,1)S(1)}, bf16[1,32,1280]{2,1,0:T(8,128)(2,1)S(1)}, u32[]{:S(2)}, u32[]{:S(2)}) collective-permute-start(bf16[1,32,1280]{2,1,0:T(8,128)(2,1)S(1)} %get-tuple-element.70), channel_id=1, source_target_pairs={{0,4},{2,6},{4,0},{6,2},{1,5},{3,7},{5,1},{7,3},{8,12},{10,14},{12... | collective-permute-start | bytes 245768 | tf_op jit(solution)/shard_map/ppermute | solution.py:399
  125.6 2.0 %copy-start.10 = (bf16[1200,128]{1,0:T(8,128)(2,1)}, bf16[1200,128]{1,0:T(8,128)(2,1)S(1)}, u32[]{:S(2)}) copy-start(bf16[1200,128]{1,0:T(8,128)(2,1)S(1)} %collective-permute-done.16.refs_3_) | copy-start | bytes 921604
  125.6 5.7 %collective-permute-start.20 = (bf16[1,32,1280]{2,1,0:T(8,128)(2,1)S(1)}, bf16[1,32,1280]{2,1,0:T(8,128)(2,1)S(1)}, u32[]{:S(2)}, u32[]{:S(2)}) collective-permute-start(bf16[1,32,1280]{2,1,0:T(8,128)(2,1)S(1)} %get-tuple-element.69), channel_id=1, source_target_pairs={{0,2},{2,4},{4,6},{6,0},{1,3},{3,5},{5,7},{7,1},{8,10},{10,12},{12... | collective-permute-start | bytes 245768 | tf_op jit(solution)/shard_map/ppermute | solution.py:399
  131.2 2.2 %copy-start.12 = (bf16[1200,128]{1,0:T(8,128)(2,1)}, bf16[1200,128]{1,0:T(8,128)(2,1)S(1)}, u32[]{:S(2)}) copy-start(bf16[1200,128]{1,0:T(8,128)(2,1)S(1)} %collective-permute-done.21.refs_4_) | copy-start | bytes 921604
  131.2 1.5 copy-start.14
  132.0 2.7 %collective-permute-start.23 = (bf16[3,4,32,1280]{3,2,1,0:T(8,128)(2,1)S(1)}, bf16[3,4,32,1280]{3,2,1,0:T(8,128)(2,1)S(1)}, u32[]{:S(2)}, u32[]{:S(2)}) collective-permute-start(bf16[3,4,32,1280]{3,2,1,0:T(8,128)(2,1)S(1)} %pad_maximum_fusion), channel_id=1, source_target_pairs={{0,1},{1,0},{2,3},{3,2},{4,5},{5,4},{6,7},{7,6},{8,9},{9,8},{10,11... | collective-permute-start | bytes 2949128 | tf_op jit(solution)/shard_map/ppermute | solution.py:394
  134.9 23.1 %copy-start.3 = (bf16[1200,128]{1,0:T(8,128)(2,1)S(1)}, bf16[1200,128]{1,0:T(8,128)(2,1)}, u32[]{:S(2)}) copy-start(bf16[1200,128]{1,0:T(8,128)(2,1)} %copy-done.2) | copy-start | bytes 921604
  135.0 23.1 %copy-start.5 = (bf16[1200,128]{1,0:T(8,128)(2,1)S(1)}, bf16[1200,128]{1,0:T(8,128)(2,1)}, u32[]{:S(2)}) copy-start(bf16[1200,128]{1,0:T(8,128)(2,1)} %copy-done.4) | copy-start | bytes 921604
  135.0 23.1 %copy-start.7 = (bf16[1200,128]{1,0:T(8,128)(2,1)S(1)}, bf16[1200,128]{1,0:T(8,128)(2,1)}, u32[]{:S(2)}) copy-start(bf16[1200,128]{1,0:T(8,128)(2,1)} %copy-done.6) | copy-start | bytes 921604
  135.0 23.1 %copy-start.9 = (bf16[1200,128]{1,0:T(8,128)(2,1)S(1)}, bf16[1200,128]{1,0:T(8,128)(2,1)}, u32[]{:S(2)}) copy-start(bf16[1200,128]{1,0:T(8,128)(2,1)} %copy-done.8) | copy-start | bytes 921604
  135.0 23.1 %copy-start.11 = (bf16[1200,128]{1,0:T(8,128)(2,1)S(1)}, bf16[1200,128]{1,0:T(8,128)(2,1)}, u32[]{:S(2)}) copy-start(bf16[1200,128]{1,0:T(8,128)(2,1)} %copy-done.10) | copy-start | bytes 921604
  135.0 23.1 %copy-start.13 = (bf16[1200,128]{1,0:T(8,128)(2,1)S(1)}, bf16[1200,128]{1,0:T(8,128)(2,1)}, u32[]{:S(2)}) copy-start(bf16[1200,128]{1,0:T(8,128)(2,1)} %copy-done.12) | copy-start | bytes 921604
  135.0 23.1 %copy-start.15 = (bf16[1200,128]{1,0:T(8,128)(2,1)S(1)}, bf16[1200,128]{1,0:T(8,128)(2,1)}, u32[]{:S(2)}) copy-start(bf16[1200,128]{1,0:T(8,128)(2,1)} %copy-done.14) | copy-start | bytes 921604
  135.1 8.9 %collective-permute-start.24 = (bf16[3,32,1280]{2,1,0:T(8,128)(2,1)S(1)}, bf16[3,32,1280]{2,1,0:T(8,128)(2,1)S(1)}, u32[]{:S(2)}, u32[]{:S(2)}) collective-permute-start(bf16[3,32,1280]{2,1,0:T(8,128)(2,1)S(1)} %get-tuple-element.66), channel_id=1, source_target_pairs={{0,6},{2,0},{4,2},{6,4},{1,7},{3,1},{5,3},{7,5},{8,14},{10,8},{12,... | collective-permute-start | bytes 737288 | tf_op jit(solution)/shard_map/ppermute | solution.py:399
  136.9 10.4 %collective-permute-start.25 = (bf16[3,32,1280]{2,1,0:T(8,128)(2,1)S(1)}, bf16[3,32,1280]{2,1,0:T(8,128)(2,1)S(1)}, u32[]{:S(2)}, u32[]{:S(2)}) collective-permute-start(bf16[3,32,1280]{2,1,0:T(8,128)(2,1)S(1)} %get-tuple-element.68), channel_id=1, source_target_pairs={{0,4},{2,6},{4,0},{6,2},{1,5},{3,7},{5,1},{7,3},{8,12},{10,14},{12... | collective-permute-start | bytes 737288 | tf_op jit(solution)/shard_map/ppermute | solution.py:399
  138.0 13.4 %collective-permute-start.26 = (bf16[3,32,1280]{2,1,0:T(8,128)(2,1)S(1)}, bf16[3,32,1280]{2,1,0:T(8,128)(2,1)S(1)}, u32[]{:S(2)}, u32[]{:S(2)}) collective-permute-start(bf16[3,32,1280]{2,1,0:T(8,128)(2,1)S(1)} %get-tuple-element.67), channel_id=1, source_target_pairs={{0,2},{2,4},{4,6},{6,0},{1,3},{3,5},{5,7},{7,1},{8,10},{10,12},{12... | collective-permute-start | bytes 737288 | tf_op jit(solution)/shard_map/ppermute | solution.py:399
  152.5 17.4 %all-to-all-start.3 = ((bf16[32,4,1280]{2,1,0:T(4,128)(2,1)}), bf16[32,4,1280]{2,1,0:T(4,128)(2,1)S(1)}, u32[]{:S(2)}, u32[]{:S(2)}) async-start(bf16[32,4,1280]{2,1,0:T(4,128)(2,1)} %reshape.197), calls=%async_computation.3 | async-start | bytes 655360 | tf_op jit(solution)/shard_map/all_to_all | solution.py:414
  158.1 1.7 %copy-start.17 = (bf16[4,256,1280]{2,1,0:T(8,128)(2,1)S(1)}, bf16[4,256,1280]{2,1,0:T(8,128)(2,1)}, u32[]{:S(2)}) copy-start(bf16[4,256,1280]{2,1,0:T(8,128)(2,1)} %copy-done.16) | copy-start | bytes 7864324

commit v7 on v6

--- a/solution.py
+++ b/solution.py
@@ -33,7 +33,7 @@
     return lax.dynamic_slice_in_dim(jnp.concatenate([value, value], axis=0), by, count, axis=0)
 
 
-def gather_hidden(hidden, x, *ready):
+def gather_hidden(hidden, x, head, *ready):
     pieces = hidden.reshape(OWN, NX, COLS).transpose(1, 0, 2)
     spread = jnp.broadcast_to(pieces[:, None], (NX, NZ, OWN, COLS)).reshape(NX * NZ, OWN, COLS)
     got = lax.all_to_all(spread, ("x", "z"), 0, 0, tiled=True)
@@ -41,7 +41,8 @@
     mine, *ready = lax.optimization_barrier((mine, *ready))
     near = [mine] + [lax.ppermute(mine, "y", shift(NY, by)) for by in range(1, NY)]
     far = [lax.ppermute(block, "c", shift(NC, 1)) for block in near]
-    return near + far, *ready
+    far[0], head = lax.optimization_barrier((far[0], head))
+    return near + far, head, *ready
 
 
 def order(y, c):
@@ -354,8 +355,8 @@
     head = jnp.pad(head_weight.T, ((0, PADDED - SLICE), (0, 0)))
     chosen = order(y, c).astype(jnp.float32)
     back = lax.rem(NX - x, NX).astype(jnp.uint32)
-    blocks, taught, head, back = gather_hidden(
-        hidden, x, teacher_rows(teacher, loss_weight), head, back
+    blocks, head, taught, back = gather_hidden(
+        hidden, x, head, teacher_rows(teacher, loss_weight), back
     )
 
     def sent(value, by):

time: 173 us -> 172 us (level)
  other arithmetic: 5.78 us -> 3.73 us
  waiting for transfers between devices: 42.5 us -> 44.4 us
    all_to_all x1, waiting for transfers between devices: 2.94 us -> 6.92 us  [gather_hidden(): got = lax.all_to_all(spread, ('x', 'z'), 0, 0, tiled=True)]
    ppermute x4, waiting for transfers between devices: 1.92 us -> 0.01 us  [gather_hidden(): far = [lax.ppermute(block, 'c', shift(NC, 1)) for block in near]]
  transfers between devices with their start and end apart: 30 -> 30, of which waited for: 16 -> 14; matrix products, arithmetic and copies ran while one was open for 10% -> 9% of each run, Pallas kernels for 10% -> 10%
where the time goes in v7:
time: 172 us; the launch traced here: 169 us
  starting transfers between devices  55.3 us (32%)
  waiting for transfers between devices  44.4 us (26%)
  blocking collectives  23.2 us (13%)
  Pallas kernels  20.8 us (12%)
  local copies, waits for them, and re-layouts  14.2 us (8%)
  matrix products  6.55 us (4%)
  other arithmetic  3.73 us (2%)
    all_to_all x1, blocking collectives, body(): every = lax.all_to_all(sums, VOCAB, 0, 0, tiled=True)  23.2 us
    ppermute x6, waiting for transfers between devices, along(): lax.ppermute(part, 'y', shift(NY, -by))  16.4 us
    all_to_all x1, starting transfers between devices, gather_hidden(): got = lax.all_to_all(spread, ('x', 'z'), 0, 0, tiled=True)  11.6 us
    ppermute x6, starting transfers between devices, passed(): return lax.ppermute(value, 'x', shift(NX, by))  9.43 us
    ppermute x6, starting transfers between devices, sent(): return lax.ppermute(value, 'x', shift(NX, by))  8.58 us
    ppermute x6, waiting for transfers between devices, passed(): return lax.ppermute(value, 'x', shift(NX, by))  7.48 us
    ppermute x6, starting transfers between devices, along(): lax.ppermute(part, 'y', shift(NY, -by))  7.37 us
    all_to_all x1, waiting for transfers between devices, gather_hidden(): got = lax.all_to_all(spread, ('x', 'z'), 0, 0, tiled=True)  6.92 us
  transfers between devices with their start and end apart: 30, of which 14 were waited for; matrix products, arithmetic and copies ran while one was open for 9% of the time, Pallas kernels for 10%

profile of v7, /device:TPU:6, one launch (start us, length us, event | category | flops | bytes accessed | tf_op | source)
XLA Modules:
  0.0 169.4 jit_solution(620888045081426413)
XLA Ops:
  0.6 0.8 reshape.192
  1.5 0.8 broadcast_in_dim.4
  2.3 11.6 %all-to-all-start = ((bf16[32,4,1280]{2,1,0:T(4,128)(2,1)}), bf16[32,4,1280]{2,1,0:T(4,128)(2,1)S(1)}, u32[]{:S(2)}, u32[]{:S(2)}) async-start(bf16[32,4,1280]{2,1,0:T(4,128)(2,1)} %bitcast.1), calls=%async_computation | async-start | bytes 655360 | tf_op jit(solution)/shard_map/all_to_all | solution.py:39
  13.9 0.7 convert_bitcast_fusion.2
  14.7 2.1 %reshape.195 = bf16[4,64,1187]{2,1,0:T(8,128)(2,1)S(1)} reshape(bf16[4,75968]{1,0:T(4,128)(2,1)} %param.5) | data formatting | bytes 1215488 | tf_op jit(solution)/shard_map/reshape | solution.py:64
  17.4 1.2 maximum_bitcast_fusion
  18.6 6.9 %all-to-all-done = bf16[32,4,1280]{2,1,0:T(4,128)(2,1)S(1)} async-done(((bf16[32,4,1280]{2,1,0:T(4,128)(2,1)}), bf16[32,4,1280]{2,1,0:T(4,128)(2,1)S(1)}, u32[]{:S(2)}, u32[]{:S(2)}) %all-to-all-start) | async-done | bytes 327712 | tf_op jit(solution)/shard_map/all_to_all | solution.py:39
  25.8 1.7 collective-permute-start.1
  27.4 2.9 %collective-permute-start.2 = (bf16[4,32,1280]{2,1,0:T(8,128)(2,1)S(1)}, bf16[4,32,1280]{2,1,0:T(8,128)(2,1)}, u32[]{:S(2)}, u32[]{:S(2)}) collective-permute-start(bf16[4,32,1280]{2,1,0:T(8,128)(2,1)S(1)} %fusion.5.refs_0_), channel_id=1, source_target_pairs={{0,4},{2,6},{4,0},{6,2},{1,5},{3,7},{5,1},{7,3},{8,12},{10,14},{12... | collective-permute-start | bytes 983048 | tf_op jit(solution)/shard_map/ppermute | solution.py:42
  30.3 1.3 collective-permute-start.3
  31.7 5.5 %all-to-all-start.1 = ((bf16[64,4,1200]{2,1,0:T(4,128)(2,1)}), bf16[64,4,1200]{2,1,0:T(4,128)(2,1)}, u32[]{:S(2)}, u32[]{:S(2)}) async-start(bf16[64,4,1200]{2,1,0:T(4,128)(2,1)} %maximum_bitcast_fusion), calls=%async_computation.1 | async-start | bytes 1310720 | tf_op jit(solution)/shard_map/all_to_all | solution.py:71
  37.8 5.0 %collective-permute-done.2.refs_2_ = bf16[4,32,1280]{2,1,0:T(8,128)(2,1)} collective-permute-done((bf16[4,32,1280]{2,1,0:T(8,128)(2,1)S(1)}, bf16[4,32,1280]{2,1,0:T(8,128)(2,1)}, u32[]{:S(2)}, u32[]{:S(2)}) %collective-permute-start.2) | collective-permute-done | bytes 327712 | tf_op jit(solution)/shard_map/ppermute | solution.py:42
  43.3 2.1 %pad.9.head_ref = bf16[1200,1280]{1,0:T(8,128)(2,1)S(1)} pad(bf16[1187,1280]{1,0:T(8,128)(2,1)} %bitcast.70, bf16[]{:T(256)} %constant.96.clone.1), padding=0_13x0_0 | pad | bytes 6110722 | tf_op jit(solution)/shard_map/jit(_pad)/pad | solution.py:355
  45.4 2.6 %shard_map.61 = (bf16[1200,128]{1,0:T(8,128)(2,1)S(1)}, bf16[1200,128]{1,0:T(8,128)(2,1)S(1)}) custom-call(bf16[1200,1280]{1,0:T(8,128)(2,1)S(1)} %pad.9.head_ref, bf16[4,32,1280]{2,1,0:T(8,128)(2,1)S(1)} %fusion.5.refs_0_, bf16[4,32,1280]{2,1,0:T(8,128)(2,1)} %collective-permute-done.1.refs_1_, bf16[4,32,1280]{2,1,0:T(8,128)(2,1)} %collective-permute-done.2.refs_2_, ...), custom_call_target="tpu_custom_call" | custom-call | flops 786432000 | bytes 1000000 | tf_op jit(solution)/shard_map/pallas_call | solution.py:101
  48.5 2.8 %collective-permute-start.9 = (bf16[1200,128]{1,0:T(8,128)(2,1)S(1)}, bf16[1200,128]{1,0:T(8,128)(2,1)S(1)}, u32[]{:S(2)}, u32[]{:S(2)}) collective-permute-start(bf16[1200,128]{1,0:T(8,128)(2,1)S(1)} %get-tuple-element.43), channel_id=1, source_target_pairs={{0,64},{64,128},{128,192},{192,0},{1,65},{65,129},{129,193},{193,1... | collective-permute-start | bytes 921608 | tf_op jit(solution)/shard_map/ppermute | solution.py:363
  51.3 5.6 %shard_map.59 = (bf16[4,256,1280]{2,1,0:T(8,128)(2,1)S(1)}, bf16[1200,128]{1,0:T(8,128)(2,1)}, bf16[1200,128]{1,0:T(8,128)(2,1)}, f32[1200,128]{1,0:T(8,128)S(1)...) custom-call(bf16[1200,1280]{1,0:T(8,128)(2,1)S(1)} %pad.9.head_ref, bf16[4,32,1280]{2,1,0:T(8,128)(2,1)S(1)} %fusion.5.refs_0_, ...), custom_call_target="tpu_custom_call" | custom-call | flops 2359296000 | bytes 4000000 | tf_op jit(solution)/shard_map/pallas_call | solution.py:187
  57.0 1.5 copy-done.16
  58.4 3.2 %collective-permute-start.8 = (bf16[1200,128]{1,0:T(8,128)(2,1)}, bf16[1200,128]{1,0:T(8,128)(2,1)}, u32[]{:S(2)}, u32[]{:S(2)}) collective-permute-start(bf16[1200,128]{1,0:T(8,128)(2,1)} %get-tuple-element.38), channel_id=1, source_target_pairs={{0,64},{64,128},{128,192},{192,0},{1,65},{65,129},{129,193},{193,1... | collective-permute-start | bytes 921608 | tf_op jit(solution)/shard_map/ppermute | solution.py:363
  61.7 1.5 shard_map.62
  63.2 2.0 %collective-permute-start.12 = (bf16[1200,128]{1,0:T(8,128)(2,1)}, bf16[1200,128]{1,0:T(8,128)(2,1)}, u32[]{:S(2)}, u32[]{:S(2)}) collective-permute-start(bf16[1200,128]{1,0:T(8,128)(2,1)} %get-tuple-element.46), channel_id=1, source_target_pairs={{0,192},{64,0},{128,64},{192,128},{1,193},{65,1},{129,65},{193,129... | collective-permute-start | bytes 921608 | tf_op jit(solution)/shard_map/ppermute | solution.py:363
  65.2 2.2 %reshape.196 = bf16[256,1200]{1,0:T(8,128)(2,1)} reshape(bf16[64,4,1200]{2,1,0:T(4,128)(2,1)} %all-to-all-done.1) | data formatting | bytes 1228800 | tf_op jit(solution)/shard_map/reshape | solution.py:71
  67.5 1.5 fusion.7.teacher_ref
  68.9 1.3 collective-permute-done.7.near_ref
  70.2 1.3 copy-done.1
  71.5 2.1 %shard_map.60 = (f32[1200,256]{1,0:T(8,128)S(1)}, f32[8,256]{1,0:T(8,128)S(1)}) custom-call(f32[1200,256]{1,0:T(8,128)S(1)} %copy-done.1, bf16[1200,128]{1,0:T(8,128)(2,1)} %collective-permute-done.7.near_ref, bf16[1200,128]{1,0:T(8,128)(2,1)} %collective-permute-done.8.far_ref, f32[1200,256]{1,0:T(8,128)S(1)} %fusion.7.teacher_ref), custom_call_target="tpu_custom_call" | custom-call | flops 12288000 | bytes 5000000 | tf_op jit(solution)/shard_map/pallas_call | solution.py:117
  73.5 0.9 collective-permute-done.11.near_ref
  75.2 2.9 %shard_map.63 = (f32[1200,256]{1,0:T(8,128)S(1)}, f32[64,8,128]{2,1,0:T(8,128)S(1)}) custom-call(f32[1200,256]{1,0:T(8,128)S(1)} %get-tuple-element.40.base_ref, bf16[1200,128]{1,0:T(8,128)(2,1)} %collective-permute-done.11.near_ref, bf16[1200,128]{1,0:T(8,128)(2,1)} %collective-permute-done.12.far_ref, f32[1200,256]{1,0:T(8,128)S(1)} %fusion.7.teacher_ref, ...), custom_call_target="tpu_custom_call" | custom-call | flops 30720000 | bytes 5000000 | tf_op jit(solution)/shard_map/pallas_call | solution.py:117
  78.1 23.2 %all_to_all.20.every_ref = f32[64,8,128]{2,1,0:T(8,128)S(1)} all-to-all(f32[64,8,128]{2,1,0:T(8,128)S(1)} %get-tuple-element.48), channel_id=1, replica_groups=mesh['x'=4,'z'=8,'y'=4,'c'=2] {'z','y','c'}, dimensions={0} | all-to-all | bytes 524288 | tf_op jit(solution)/shard_map/all_to_all | solution.py:374
  101.3 1.1 shard_map.64
  103.4 3.0 %collective-permute-start.17 = (bf16[1200,128]{1,0:T(8,128)(2,1)S(1)}, bf16[1200,128]{1,0:T(8,128)(2,1)S(1)}, u32[]{:S(2)}, u32[]{:S(2)}) collective-permute-start(bf16[1200,128]{1,0:T(8,128)(2,1)S(1)} %get-tuple-element.51.refs_1_), channel_id=1, source_target_pairs={{0,64},{64,128},{128,192},{192,0},{1,65},{65,129},{129,193},{193,1... | collective-permute-start | bytes 921608 | tf_op jit(solution)/shard_map/ppermute | solution.py:378
  106.4 3.2 %collective-permute-start.15 = (bf16[1200,128]{1,0:T(8,128)(2,1)S(1)}, bf16[1200,128]{1,0:T(8,128)(2,1)S(1)}, u32[]{:S(2)}, u32[]{:S(2)}) collective-permute-start(bf16[1200,128]{1,0:T(8,128)(2,1)S(1)} %get-tuple-element.50.refs_0_), channel_id=1, source_target_pairs={{0,64},{64,128},{128,192},{192,0},{1,65},{65,129},{129,193},{193,1... | collective-permute-start | bytes 921608 | tf_op jit(solution)/shard_map/ppermute | solution.py:378
  110.3 7.4 %collective-permute-done.14.refs_2_ = bf16[1200,128]{1,0:T(8,128)(2,1)S(1)} collective-permute-done((bf16[1200,128]{1,0:T(8,128)(2,1)S(1)}, bf16[1200,128]{1,0:T(8,128)(2,1)S(1)}, u32[]{:S(2)}, u32[]{:S(2)}) %collective-permute-start.14) | collective-permute-done | bytes 307232 | tf_op jit(solution)/shard_map/ppermute | solution.py:378
  117.7 3.2 %collective-permute-start.22 = (bf16[1200,128]{1,0:T(8,128)(2,1)S(1)}, bf16[1200,128]{1,0:T(8,128)(2,1)S(1)}, u32[]{:S(2)}, u32[]{:S(2)}) collective-permute-start(bf16[1200,128]{1,0:T(8,128)(2,1)S(1)} %collective-permute-done.17.refs_7_), channel_id=1, source_target_pairs={{0,64},{64,128},{128,192},{192,0},{1,65},{65,129},{129,193},{193,1... | collective-permute-start | bytes 921608 | tf_op jit(solution)/shard_map/ppermute | solution.py:378
  121.1 1.9 %collective-permute-start.18 = (bf16[1,32,1280]{2,1,0:T(8,128)(2,1)S(1)}, bf16[1,32,1280]{2,1,0:T(8,128)(2,1)S(1)}, u32[]{:S(2)}, u32[]{:S(2)}) collective-permute-start(bf16[1,32,1280]{2,1,0:T(8,128)(2,1)S(1)} %get-tuple-element.73), channel_id=1, source_target_pairs={{0,6},{2,0},{4,2},{6,4},{1,7},{3,1},{5,3},{7,5},{8,14},{10,8},{12,... | collective-permute-start | bytes 245768 | tf_op jit(solution)/shard_map/ppermute | solution.py:400
  123.0 1.3 collective-permute-start.19
  126.3 2.7 %collective-permute-done.19 = bf16[1,32,1280]{2,1,0:T(8,128)(2,1)S(1)} collective-permute-done((bf16[1,32,1280]{2,1,0:T(8,128)(2,1)S(1)}, bf16[1,32,1280]{2,1,0:T(8,128)(2,1)S(1)}, u32[]{:S(2)}, u32[]{:S(2)}) %collective-permute-start.19) | collective-permute-done | bytes 81952 | tf_op jit(solution)/shard_map/ppermute | solution.py:400
  129.0 0.9 collective-permute-done.20
  133.8 1.8 %collective-permute-start.24 = (bf16[3,32,1280]{2,1,0:T(8,128)(2,1)S(1)}, bf16[3,32,1280]{2,1,0:T(8,128)(2,1)S(1)}, u32[]{:S(2)}, u32[]{:S(2)}) collective-permute-start(bf16[3,32,1280]{2,1,0:T(8,128)(2,1)S(1)} %get-tuple-element.68), channel_id=1, source_target_pairs={{0,6},{2,0},{4,2},{6,4},{1,7},{3,1},{5,3},{7,5},{8,14},{10,8},{12,... | collective-permute-start | bytes 737288 | tf_op jit(solution)/shard_map/ppermute | solution.py:400
  135.6 1.1 collective-permute-start.25
  137.4 5.3 %collective-permute-done.24 = bf16[3,32,1280]{2,1,0:T(8,128)(2,1)S(1)} collective-permute-done((bf16[3,32,1280]{2,1,0:T(8,128)(2,1)S(1)}, bf16[3,32,1280]{2,1,0:T(8,128)(2,1)S(1)}, u32[]{:S(2)}, u32[]{:S(2)}) %collective-permute-start.24) | collective-permute-done | bytes 245792 | tf_op jit(solution)/shard_map/ppermute | solution.py:400
  142.7 3.3 %collective-permute-done.25 = bf16[3,32,1280]{2,1,0:T(8,128)(2,1)S(1)} collective-permute-done((bf16[3,32,1280]{2,1,0:T(8,128)(2,1)S(1)}, bf16[3,32,1280]{2,1,0:T(8,128)(2,1)S(1)}, u32[]{:S(2)}, u32[]{:S(2)}) %collective-permute-start.25) | collective-permute-done | bytes 245792 | tf_op jit(solution)/shard_map/ppermute | solution.py:400
  146.0 4.1 %collective-permute-done.26 = bf16[3,32,1280]{2,1,0:T(8,128)(2,1)S(1)} collective-permute-done((bf16[3,32,1280]{2,1,0:T(8,128)(2,1)S(1)}, bf16[3,32,1280]{2,1,0:T(8,128)(2,1)S(1)}, u32[]{:S(2)}, u32[]{:S(2)}) %collective-permute-start.26) | collective-permute-done | bytes 245792 | tf_op jit(solution)/shard_map/ppermute | solution.py:400
  150.4 0.8 reshape.197
  151.3 5.6 %all-to-all-start.3 = ((bf16[32,4,1280]{2,1,0:T(4,128)(2,1)}), bf16[32,4,1280]{2,1,0:T(4,128)(2,1)S(1)}, u32[]{:S(2)}, u32[]{:S(2)}) async-start(bf16[32,4,1280]{2,1,0:T(4,128)(2,1)} %reshape.197), calls=%async_computation.3 | async-start | bytes 655360 | tf_op jit(solution)/shard_map/all_to_all | solution.py:415
  156.9 1.7 %copy-done.17 = bf16[4,256,1280]{2,1,0:T(8,128)(2,1)S(1)} copy-done((bf16[4,256,1280]{2,1,0:T(8,128)(2,1)S(1)}, bf16[4,256,1280]{2,1,0:T(8,128)(2,1)}, u32[]{:S(2)}) %copy-start.17) | copy-done | bytes 2621464
  158.6 5.0 %shard_map.65 = bf16[1187,1280]{1,0:T(8,128)(2,1)} custom-call(bf16[1200,128]{1,0:T(8,128)(2,1)S(1)} %copy-done.3, bf16[1200,128]{1,0:T(8,128)(2,1)S(1)} %copy-done.5, bf16[1200,128]{1,0:T(8,128)(2,1)S(1)} %copy-done.7, bf16[1200,128]{1,0:T(8,128)(2,1)S(1)} %copy-done.11, bf16[1200,128]{1,0:T(8,128)(2,1)S(1)} %copy-done.13, ...), custom_call_target="tpu_custom_call" | custom-call | flops 3145728000 | bytes 9000000 | tf_op jit(solution)/shard_map/pallas_call | solution.py:340
  163.7 5.0 %all-to-all-done.3 = bf16[32,4,1280]{2,1,0:T(4,128)(2,1)S(1)} async-done(((bf16[32,4,1280]{2,1,0:T(4,128)(2,1)}), bf16[32,4,1280]{2,1,0:T(4,128)(2,1)S(1)}, u32[]{:S(2)}, u32[]{:S(2)}) %all-to-all-start.3) | async-done | bytes 327712 | tf_op jit(solution)/shard_map/all_to_all | solution.py:415
  168.6 0.8 bitcast_reduce_fusion
  (93 shorter events, 11.8 us)
Async XLA Ops:
  2.3 23.3 %all-to-all-start = ((bf16[32,4,1280]{2,1,0:T(4,128)(2,1)}), bf16[32,4,1280]{2,1,0:T(4,128)(2,1)S(1)}, u32[]{:S(2)}, u32[]{:S(2)}) async-start(bf16[32,4,1280]{2,1,0:T(4,128)(2,1)} %bitcast.1), calls=%async_computation | async-start | bytes 655360 | tf_op jit(solution)/shard_map/all_to_all | solution.py:39
  25.8 11.6 %collective-permute-start.1 = (bf16[4,32,1280]{2,1,0:T(8,128)(2,1)S(1)}, bf16[4,32,1280]{2,1,0:T(8,128)(2,1)}, u32[]{:S(2)}, u32[]{:S(2)}) collective-permute-start(bf16[4,32,1280]{2,1,0:T(8,128)(2,1)S(1)} %fusion.5.refs_0_), channel_id=1, source_target_pairs={{0,2},{2,4},{4,6},{6,0},{1,3},{3,5},{5,7},{7,1},{8,10},{10,12},{12... | collective-permute-start | bytes 983048 | tf_op jit(solution)/shard_map/ppermute | solution.py:42
  27.4 15.3 %collective-permute-start.2 = (bf16[4,32,1280]{2,1,0:T(8,128)(2,1)S(1)}, bf16[4,32,1280]{2,1,0:T(8,128)(2,1)}, u32[]{:S(2)}, u32[]{:S(2)}) collective-permute-start(bf16[4,32,1280]{2,1,0:T(8,128)(2,1)S(1)} %fusion.5.refs_0_), channel_id=1, source_target_pairs={{0,4},{2,6},{4,0},{6,2},{1,5},{3,7},{5,1},{7,3},{8,12},{10,14},{12... | collective-permute-start | bytes 983048 | tf_op jit(solution)/shard_map/ppermute | solution.py:42
  30.3 12.5 %collective-permute-start.3 = (bf16[4,32,1280]{2,1,0:T(8,128)(2,1)S(1)}, bf16[4,32,1280]{2,1,0:T(8,128)(2,1)}, u32[]{:S(2)}, u32[]{:S(2)}) collective-permute-start(bf16[4,32,1280]{2,1,0:T(8,128)(2,1)S(1)} %fusion.5.refs_0_), channel_id=1, source_target_pairs={{0,6},{2,0},{4,2},{6,4},{1,7},{3,1},{5,3},{7,5},{8,14},{10,8},{12,... | collective-permute-start | bytes 983048 | tf_op jit(solution)/shard_map/ppermute | solution.py:42
  31.7 33.5 %all-to-all-start.1 = ((bf16[64,4,1200]{2,1,0:T(4,128)(2,1)}), bf16[64,4,1200]{2,1,0:T(4,128)(2,1)}, u32[]{:S(2)}, u32[]{:S(2)}) async-start(bf16[64,4,1200]{2,1,0:T(4,128)(2,1)} %maximum_bitcast_fusion), calls=%async_computation.1 | async-start | bytes 1310720 | tf_op jit(solution)/shard_map/all_to_all | solution.py:71
  37.2 8.2 %collective-permute-start = (bf16[4,32,1280]{2,1,0:T(8,128)(2,1)S(1)}, bf16[4,32,1280]{2,1,0:T(8,128)(2,1)}, u32[]{:S(2)}, u32[]{:S(2)}) collective-permute-start(bf16[4,32,1280]{2,1,0:T(8,128)(2,1)S(1)} %fusion.5.refs_0_), channel_id=1, source_target_pairs={{0,1},{1,0},{2,3},{3,2},{4,5},{5,4},{6,7},{7,6},{8,9},{9,8},{10,11... | collective-permute-start | bytes 983048 | tf_op jit(solution)/shard_map/ppermute | solution.py:43
  37.4 8.0 %collective-permute-start.4 = (bf16[4,32,1280]{2,1,0:T(8,128)(2,1)}, bf16[4,32,1280]{2,1,0:T(8,128)(2,1)}, u32[]{:S(2)}, u32[]{:S(2)}) collective-permute-start(bf16[4,32,1280]{2,1,0:T(8,128)(2,1)} %collective-permute-done.1.refs_1_), channel_id=1, source_target_pairs={{0,1},{1,0},{2,3},{3,2},{4,5},{5,4},{6,7},{7,6},{8,9},{9,8},{10,11... | collective-permute-start | bytes 983048 | tf_op jit(solution)/shard_map/ppermute | solution.py:43
  42.8 2.6 %collective-permute-start.5 = (bf16[4,32,1280]{2,1,0:T(8,128)(2,1)}, bf16[4,32,1280]{2,1,0:T(8,128)(2,1)}, u32[]{:S(2)}, u32[]{:S(2)}) collective-permute-start(bf16[4,32,1280]{2,1,0:T(8,128)(2,1)} %collective-permute-done.2.refs_2_), channel_id=1, source_target_pairs={{0,1},{1,0},{2,3},{3,2},{4,5},{5,4},{6,7},{7,6},{8,9},{9,8},{10,11... | collective-permute-start | bytes 983048 | tf_op jit(solution)/shard_map/ppermute | solution.py:43
  42.8 2.6 %collective-permute-start.6 = (bf16[4,32,1280]{2,1,0:T(8,128)(2,1)}, bf16[4,32,1280]{2,1,0:T(8,128)(2,1)}, u32[]{:S(2)}, u32[]{:S(2)}) collective-permute-start(bf16[4,32,1280]{2,1,0:T(8,128)(2,1)} %collective-permute-done.3.refs_3_), channel_id=1, source_target_pairs={{0,1},{1,0},{2,3},{3,2},{4,5},{5,4},{6,7},{7,6},{8,9},{9,8},{10,11... | collective-permute-start | bytes 983048 | tf_op jit(solution)/shard_map/ppermute | solution.py:43
  48.0 13.7 %collective-permute-start.10 = (bf16[1200,128]{1,0:T(8,128)(2,1)S(1)}, bf16[1200,128]{1,0:T(8,128)(2,1)S(1)}, u32[]{:S(2)}, u32[]{:S(2)}) collective-permute-start(bf16[1200,128]{1,0:T(8,128)(2,1)S(1)} %get-tuple-element.44), channel_id=1, source_target_pairs={{0,192},{64,0},{128,64},{192,128},{1,193},{65,1},{129,65},{193,129... | collective-permute-start | bytes 921608 | tf_op jit(solution)/shard_map/ppermute | solution.py:363
  48.5 13.2 %collective-permute-start.9 = (bf16[1200,128]{1,0:T(8,128)(2,1)S(1)}, bf16[1200,128]{1,0:T(8,128)(2,1)S(1)}, u32[]{:S(2)}, u32[]{:S(2)}) collective-permute-start(bf16[1200,128]{1,0:T(8,128)(2,1)S(1)} %get-tuple-element.43), channel_id=1, source_target_pairs={{0,64},{64,128},{128,192},{192,0},{1,65},{65,129},{129,193},{193,1... | collective-permute-start | bytes 921608 | tf_op jit(solution)/shard_map/ppermute | solution.py:363
  56.9 1.5 copy-start.16
  58.4 4.7 %copy-start = (f32[1200,256]{1,0:T(8,128)}, f32[1200,256]{1,0:T(8,128)S(1)}, u32[]{:S(2)}) copy-start(f32[1200,256]{1,0:T(8,128)S(1)} %get-tuple-element.36.own_ref) | copy-start | bytes 3686404
  58.4 11.7 %collective-permute-start.7 = (bf16[1200,128]{1,0:T(8,128)(2,1)}, bf16[1200,128]{1,0:T(8,128)(2,1)}, u32[]{:S(2)}, u32[]{:S(2)}) collective-permute-start(bf16[1200,128]{1,0:T(8,128)(2,1)} %get-tuple-element.37), channel_id=1, source_target_pairs={{0,192},{64,0},{128,64},{192,128},{1,193},{65,1},{129,65},{193,129... | collective-permute-start | bytes 921608 | tf_op jit(solution)/shard_map/ppermute | solution.py:363
  58.4 11.7 %collective-permute-start.8 = (bf16[1200,128]{1,0:T(8,128)(2,1)}, bf16[1200,128]{1,0:T(8,128)(2,1)}, u32[]{:S(2)}, u32[]{:S(2)}) collective-permute-start(bf16[1200,128]{1,0:T(8,128)(2,1)} %get-tuple-element.38), channel_id=1, source_target_pairs={{0,64},{64,128},{128,192},{192,0},{1,65},{65,129},{129,193},{193,1... | collective-permute-start | bytes 921608 | tf_op jit(solution)/shard_map/ppermute | solution.py:363
  63.2 11.3 %collective-permute-start.11 = (bf16[1200,128]{1,0:T(8,128)(2,1)}, bf16[1200,128]{1,0:T(8,128)(2,1)}, u32[]{:S(2)}, u32[]{:S(2)}) collective-permute-start(bf16[1200,128]{1,0:T(8,128)(2,1)} %get-tuple-element.45), channel_id=1, source_target_pairs={{0,64},{64,128},{128,192},{192,0},{1,65},{65,129},{129,193},{193,1... | collective-permute-start | bytes 921608 | tf_op jit(solution)/shard_map/ppermute | solution.py:363
  63.2 12.0 %collective-permute-start.12 = (bf16[1200,128]{1,0:T(8,128)(2,1)}, bf16[1200,128]{1,0:T(8,128)(2,1)}, u32[]{:S(2)}, u32[]{:S(2)}) collective-permute-start(bf16[1200,128]{1,0:T(8,128)(2,1)} %get-tuple-element.46), channel_id=1, source_target_pairs={{0,192},{64,0},{128,64},{192,128},{1,193},{65,1},{129,65},{193,129... | collective-permute-start | bytes 921608 | tf_op jit(solution)/shard_map/ppermute | solution.py:363
  70.2 1.3 copy-start.1
  102.4 7.8 %copy-start.2 = (bf16[1200,128]{1,0:T(8,128)(2,1)}, bf16[1200,128]{1,0:T(8,128)(2,1)S(1)}, u32[]{:S(2)}) copy-start(bf16[1200,128]{1,0:T(8,128)(2,1)S(1)} %get-tuple-element.50.refs_0_) | copy-start | bytes 921604
  102.4 7.8 %copy-start.4 = (bf16[1200,128]{1,0:T(8,128)(2,1)}, bf16[1200,128]{1,0:T(8,128)(2,1)S(1)}, u32[]{:S(2)}) copy-start(bf16[1200,128]{1,0:T(8,128)(2,1)S(1)} %get-tuple-element.51.refs_1_) | copy-start | bytes 921604
  103.1 17.9 %collective-permute-start.13 = (bf16[1,4,32,1280]{3,2,1,0:T(8,128)(2,1)S(1)}, bf16[1,4,32,1280]{3,2,1,0:T(8,128)(2,1)S(1)}, u32[]{:S(2)}, u32[]{:S(2)}) collective-permute-start(bf16[1,4,32,1280]{3,2,1,0:T(8,128)(2,1)S(1)} %bitcast.78), channel_id=1, source_target_pairs={{0,1},{1,0},{2,3},{3,2},{4,5},{5,4},{6,7},{7,6},{8,9},{9,8},{10,11... | collective-permute-start | bytes 983048 | tf_op jit(solution)/shard_map/ppermute | solution.py:395
  103.4 14.3 %collective-permute-start.17 = (bf16[1200,128]{1,0:T(8,128)(2,1)S(1)}, bf16[1200,128]{1,0:T(8,128)(2,1)S(1)}, u32[]{:S(2)}, u32[]{:S(2)}) collective-permute-start(bf16[1200,128]{1,0:T(8,128)(2,1)S(1)} %get-tuple-element.51.refs_1_), channel_id=1, source_target_pairs={{0,64},{64,128},{128,192},{192,0},{1,65},{65,129},{129,193},{193,1... | collective-permute-start | bytes 921608 | tf_op jit(solution)/shard_map/ppermute | solution.py:378
  106.4 11.3 %collective-permute-start.14 = (bf16[1200,128]{1,0:T(8,128)(2,1)S(1)}, bf16[1200,128]{1,0:T(8,128)(2,1)S(1)}, u32[]{:S(2)}, u32[]{:S(2)}) collective-permute-start(bf16[1200,128]{1,0:T(8,128)(2,1)S(1)} %get-tuple-element.50.refs_0_), channel_id=1, source_target_pairs={{0,192},{64,0},{128,64},{192,128},{1,193},{65,1},{129,65},{193,129... | collective-permute-start | bytes 921608 | tf_op jit(solution)/shard_map/ppermute | solution.py:378
  106.4 16.6 %collective-permute-start.15 = (bf16[1200,128]{1,0:T(8,128)(2,1)S(1)}, bf16[1200,128]{1,0:T(8,128)(2,1)S(1)}, u32[]{:S(2)}, u32[]{:S(2)}) collective-permute-start(bf16[1200,128]{1,0:T(8,128)(2,1)S(1)} %get-tuple-element.50.refs_0_), channel_id=1, source_target_pairs={{0,64},{64,128},{128,192},{192,0},{1,65},{65,129},{129,193},{193,1... | collective-permute-start | bytes 921608 | tf_op jit(solution)/shard_map/ppermute | solution.py:378
  109.6 14.7 %collective-permute-start.16 = (bf16[1200,128]{1,0:T(8,128)(2,1)S(1)}, bf16[1200,128]{1,0:T(8,128)(2,1)S(1)}, u32[]{:S(2)}, u32[]{:S(2)}) collective-permute-start(bf16[1200,128]{1,0:T(8,128)(2,1)S(1)} %get-tuple-element.51.refs_1_), channel_id=1, source_target_pairs={{0,192},{64,0},{128,64},{192,128},{1,193},{65,1},{129,65},{193,129... | collective-permute-start | bytes 921608 | tf_op jit(solution)/shard_map/ppermute | solution.py:378
  117.7 13.1 %copy-start.6 = (bf16[1200,128]{1,0:T(8,128)(2,1)}, bf16[1200,128]{1,0:T(8,128)(2,1)S(1)}, u32[]{:S(2)}) copy-start(bf16[1200,128]{1,0:T(8,128)(2,1)S(1)} %collective-permute-done.14.refs_2_) | copy-start | bytes 921604
  117.7 12.2 %collective-permute-start.21 = (bf16[1200,128]{1,0:T(8,128)(2,1)S(1)}, bf16[1200,128]{1,0:T(8,128)(2,1)S(1)}, u32[]{:S(2)}, u32[]{:S(2)}) collective-permute-start(bf16[1200,128]{1,0:T(8,128)(2,1)S(1)} %collective-permute-done.14.refs_2_), channel_id=1, source_target_pairs={{0,192},{64,0},{128,64},{192,128},{1,193},{65,1},{129,65},{193,129... | collective-permute-start | bytes 921608 | tf_op jit(solution)/shard_map/ppermute | solution.py:378
  117.7 12.2 %collective-permute-start.22 = (bf16[1200,128]{1,0:T(8,128)(2,1)S(1)}, bf16[1200,128]{1,0:T(8,128)(2,1)S(1)}, u32[]{:S(2)}, u32[]{:S(2)}) collective-permute-start(bf16[1200,128]{1,0:T(8,128)(2,1)S(1)} %collective-permute-done.17.refs_7_), channel_id=1, source_target_pairs={{0,64},{64,128},{128,192},{192,0},{1,65},{65,129},{129,193},{193,1... | collective-permute-start | bytes 921608 | tf_op jit(solution)/shard_map/ppermute | solution.py:378
  121.1 5.3 %collective-permute-start.18 = (bf16[1,32,1280]{2,1,0:T(8,128)(2,1)S(1)}, bf16[1,32,1280]{2,1,0:T(8,128)(2,1)S(1)}, u32[]{:S(2)}, u32[]{:S(2)}) collective-permute-start(bf16[1,32,1280]{2,1,0:T(8,128)(2,1)S(1)} %get-tuple-element.73), channel_id=1, source_target_pairs={{0,6},{2,0},{4,2},{6,4},{1,7},{3,1},{5,3},{7,5},{8,14},{10,8},{12,... | collective-permute-start | bytes 245768 | tf_op jit(solution)/shard_map/ppermute | solution.py:400
  123.0 8.5 %copy-start.8 = (bf16[1200,128]{1,0:T(8,128)(2,1)}, bf16[1200,128]{1,0:T(8,128)(2,1)S(1)}, u32[]{:S(2)}) copy-start(bf16[1200,128]{1,0:T(8,128)(2,1)S(1)} %collective-permute-done.15.refs_6_) | copy-start | bytes 921604
  123.0 6.0 %collective-permute-start.19 = (bf16[1,32,1280]{2,1,0:T(8,128)(2,1)S(1)}, bf16[1,32,1280]{2,1,0:T(8,128)(2,1)S(1)}, u32[]{:S(2)}, u32[]{:S(2)}) collective-permute-start(bf16[1,32,1280]{2,1,0:T(8,128)(2,1)S(1)} %get-tuple-element.72), channel_id=1, source_target_pairs={{0,4},{2,6},{4,0},{6,2},{1,5},{3,7},{5,1},{7,3},{8,12},{10,14},{12... | collective-permute-start | bytes 245768 | tf_op jit(solution)/shard_map/ppermute | solution.py:400
  124.3 2.0 %copy-start.10 = (bf16[1200,128]{1,0:T(8,128)(2,1)}, bf16[1200,128]{1,0:T(8,128)(2,1)S(1)}, u32[]{:S(2)}) copy-start(bf16[1200,128]{1,0:T(8,128)(2,1)S(1)} %collective-permute-done.16.refs_3_) | copy-start | bytes 921604
  124.3 5.7 %collective-permute-start.20 = (bf16[1,32,1280]{2,1,0:T(8,128)(2,1)S(1)}, bf16[1,32,1280]{2,1,0:T(8,128)(2,1)S(1)}, u32[]{:S(2)}, u32[]{:S(2)}) collective-permute-start(bf16[1,32,1280]{2,1,0:T(8,128)(2,1)S(1)} %get-tuple-element.71), channel_id=1, source_target_pairs={{0,2},{2,4},{4,6},{6,0},{1,3},{3,5},{5,7},{7,1},{8,10},{10,12},{12... | collective-permute-start | bytes 245768 | tf_op jit(solution)/shard_map/ppermute | solution.py:400
  130.0 2.2 %copy-start.12 = (bf16[1200,128]{1,0:T(8,128)(2,1)}, bf16[1200,128]{1,0:T(8,128)(2,1)S(1)}, u32[]{:S(2)}) copy-start(bf16[1200,128]{1,0:T(8,128)(2,1)S(1)} %collective-permute-done.21.refs_4_) | copy-start | bytes 921604
  130.0 1.5 copy-start.14
  130.8 2.7 %collective-permute-start.23 = (bf16[3,4,32,1280]{3,2,1,0:T(8,128)(2,1)S(1)}, bf16[3,4,32,1280]{3,2,1,0:T(8,128)(2,1)S(1)}, u32[]{:S(2)}, u32[]{:S(2)}) collective-permute-start(bf16[3,4,32,1280]{3,2,1,0:T(8,128)(2,1)S(1)} %pad_maximum_fusion), channel_id=1, source_target_pairs={{0,1},{1,0},{2,3},{3,2},{4,5},{5,4},{6,7},{7,6},{8,9},{9,8},{10,11... | collective-permute-start | bytes 2949128 | tf_op jit(solution)/shard_map/ppermute | solution.py:395
  133.7 23.1 %copy-start.3 = (bf16[1200,128]{1,0:T(8,128)(2,1)S(1)}, bf16[1200,128]{1,0:T(8,128)(2,1)}, u32[]{:S(2)}) copy-start(bf16[1200,128]{1,0:T(8,128)(2,1)} %copy-done.2) | copy-start | bytes 921604
  133.7 23.1 %copy-start.5 = (bf16[1200,128]{1,0:T(8,128)(2,1)S(1)}, bf16[1200,128]{1,0:T(8,128)(2,1)}, u32[]{:S(2)}) copy-start(bf16[1200,128]{1,0:T(8,128)(2,1)} %copy-done.4) | copy-start | bytes 921604
  133.7 23.1 %copy-start.7 = (bf16[1200,128]{1,0:T(8,128)(2,1)S(1)}, bf16[1200,128]{1,0:T(8,128)(2,1)}, u32[]{:S(2)}) copy-start(bf16[1200,128]{1,0:T(8,128)(2,1)} %copy-done.6) | copy-start | bytes 921604
  133.7 23.1 %copy-start.9 = (bf16[1200,128]{1,0:T(8,128)(2,1)S(1)}, bf16[1200,128]{1,0:T(8,128)(2,1)}, u32[]{:S(2)}) copy-start(bf16[1200,128]{1,0:T(8,128)(2,1)} %copy-done.8) | copy-start | bytes 921604
  133.7 23.1 %copy-start.11 = (bf16[1200,128]{1,0:T(8,128)(2,1)S(1)}, bf16[1200,128]{1,0:T(8,128)(2,1)}, u32[]{:S(2)}) copy-start(bf16[1200,128]{1,0:T(8,128)(2,1)} %copy-done.10) | copy-start | bytes 921604
  133.7 23.1 %copy-start.13 = (bf16[1200,128]{1,0:T(8,128)(2,1)S(1)}, bf16[1200,128]{1,0:T(8,128)(2,1)}, u32[]{:S(2)}) copy-start(bf16[1200,128]{1,0:T(8,128)(2,1)} %copy-done.12) | copy-start | bytes 921604
  133.7 23.1 %copy-start.15 = (bf16[1200,128]{1,0:T(8,128)(2,1)S(1)}, bf16[1200,128]{1,0:T(8,128)(2,1)}, u32[]{:S(2)}) copy-start(bf16[1200,128]{1,0:T(8,128)(2,1)} %copy-done.14) | copy-start | bytes 921604
  133.8 8.9 %collective-permute-start.24 = (bf16[3,32,1280]{2,1,0:T(8,128)(2,1)S(1)}, bf16[3,32,1280]{2,1,0:T(8,128)(2,1)S(1)}, u32[]{:S(2)}, u32[]{:S(2)}) collective-permute-start(bf16[3,32,1280]{2,1,0:T(8,128)(2,1)S(1)} %get-tuple-element.68), channel_id=1, source_target_pairs={{0,6},{2,0},{4,2},{6,4},{1,7},{3,1},{5,3},{7,5},{8,14},{10,8},{12,... | collective-permute-start | bytes 737288 | tf_op jit(solution)/shard_map/ppermute | solution.py:400
  135.6 10.4 %collective-permute-start.25 = (bf16[3,32,1280]{2,1,0:T(8,128)(2,1)S(1)}, bf16[3,32,1280]{2,1,0:T(8,128)(2,1)S(1)}, u32[]{:S(2)}, u32[]{:S(2)}) collective-permute-start(bf16[3,32,1280]{2,1,0:T(8,128)(2,1)S(1)} %get-tuple-element.70), channel_id=1, source_target_pairs={{0,4},{2,6},{4,0},{6,2},{1,5},{3,7},{5,1},{7,3},{8,12},{10,14},{12... | collective-permute-start | bytes 737288 | tf_op jit(solution)/shard_map/ppermute | solution.py:400
  136.7 13.4 %collective-permute-start.26 = (bf16[3,32,1280]{2,1,0:T(8,128)(2,1)S(1)}, bf16[3,32,1280]{2,1,0:T(8,128)(2,1)S(1)}, u32[]{:S(2)}, u32[]{:S(2)}) collective-permute-start(bf16[3,32,1280]{2,1,0:T(8,128)(2,1)S(1)} %get-tuple-element.69), channel_id=1, source_target_pairs={{0,2},{2,4},{4,6},{6,0},{1,3},{3,5},{5,7},{7,1},{8,10},{10,12},{12... | collective-permute-start | bytes 737288 | tf_op jit(solution)/shard_map/ppermute | solution.py:400
  151.3 17.4 %all-to-all-start.3 = ((bf16[32,4,1280]{2,1,0:T(4,128)(2,1)}), bf16[32,4,1280]{2,1,0:T(4,128)(2,1)S(1)}, u32[]{:S(2)}, u32[]{:S(2)}) async-start(bf16[32,4,1280]{2,1,0:T(4,128)(2,1)} %reshape.197), calls=%async_computation.3 | async-start | bytes 655360 | tf_op jit(solution)/shard_map/all_to_all | solution.py:415
  156.9 1.7 %copy-start.17 = (bf16[4,256,1280]{2,1,0:T(8,128)(2,1)S(1)}, bf16[4,256,1280]{2,1,0:T(8,128)(2,1)}, u32[]{:S(2)}) copy-start(bf16[4,256,1280]{2,1,0:T(8,128)(2,1)} %copy-done.16) | copy-start | bytes 7864324
